TPU v7x, 32 devices: a whole 2x2x4 slice. The times are simulated.
32 devices in a mesh: groups: 2 (over y), rows: 16 (over z, x, core).
Axes of the slice: x: 2, y: 2, z: 4, core: 2. Of those that a mesh axis runs over, the one named last changes fastest.
Arguments:
- positions: float32 [64, 2048], P('rows', 'groups'), parts along dimension 1, may hold values from -3.140625 to 3.140625
- momenta: float32 [64, 2048], P('rows', 'groups'), parts along dimension 1, may hold values from -6 to 6
- kick_strength: float32 [64, 1024], P('rows'), may hold values from 0.3 to 3
- coupling: float32 [64, 1024], P('rows'), may hold values from 0.05 to 0.5
- tangent: float32 [4, 64, 1024, 128], P('groups', 'rows'), parts along dimension 0, may hold values from -200 to 200, as said below
- log_growth: float32 [256], P('groups'), parts along dimension 0, may hold values from -4 to 4
Outputs:
- new_positions: float32 [64, 2048], P('rows', 'groups'), parts along dimension 1
- new_momenta: float32 [64, 2048], P('rows', 'groups'), parts along dimension 1
- tangent_out: float32 [4, 64, 1024, 128], P('groups', 'rows'), parts along dimension 0
- growth_out: float32 [256], P('groups'), parts along dimension 0
There are 2 independent parts, one for each index of `groups`. A program takes and returns all parts, laid end to end along the dimension named above; an argument that names none is the same for every part. Nothing has to cross between parts.
Inputs may be any that keep to these rules, and one draw needn't show every extreme that they name: real-valued tangent vectors.
All inputs are finite; a program needn't handle non-finite values.
Results may differ from a plain program's by a relative error of at most 0.0003.
Values sent between devices are 32-bit elements; how exact they have to be, the bound alone decides.
No kernel may reach another device: no remote copies, remote signals or barrier semaphores. Data moves between devices by JAX's collectives and lax.ppermute only.
A program may use at most 64 MiB of HBM per device.

v0:
```python
import math

import jax
import jax.numpy as jnp
from jax import lax
from jax.sharding import PartitionSpec as P


def with_halo(shard, sides, width):
    for axis, dim in sides:
        devices, length = (lax.axis_size(axis), shard.shape[dim])
        up = [(i, (i + 1) % devices) for i in range(devices)]
        down = [(j, i) for i, j in up]
        last = lax.slice_in_dim(shard, length - width, length, axis=dim)
        leading = lax.slice_in_dim(shard, 0, width, axis=dim)
        before = lax.ppermute(last, axis, up)
        after = lax.ppermute(leading, axis, down)
        shard = jnp.concatenate([before, shard, after], axis=dim)
    return shard


def inner_gram(matrix):
    return lax.dot_general(
        matrix, matrix, (((0,), (0,)), ((), ())), precision=lax.Precision.HIGHEST
    )


def upper_factor(gram):
    order = gram.shape[0]
    places = jnp.arange(order)

    def column_step(index, carry):
        work, lower = carry
        pick = (places == index).astype(jnp.float32)
        column = jnp.sum(work * pick[None, :], 1)
        pivot = jnp.sum(column * pick)
        scaled = jnp.where(places >= index, column / jnp.sqrt(pivot), 0.0)
        work = work - scaled[:, None] * scaled[None, :]
        lower = lower + scaled[:, None] * pick[None, :]
        return (work, lower)

    start = (gram, jnp.zeros_like(gram))
    work, lower = lax.fori_loop(0, order, column_step, start)
    return lower.T


def upper_inverse(upper):
    order = upper.shape[0]
    places = jnp.arange(order)

    def row_step(count, inverse):
        index = order - 1 - count
        pick = (places == index).astype(jnp.float32)
        row = jnp.sum(upper * pick[:, None], 0)
        pivot = jnp.sum(row * pick)
        rest = jnp.where(places > index, row, 0.0)
        solved = (pick - jnp.dot(rest, inverse, precision=lax.Precision.HIGHEST)) / pivot
        return inverse + pick[:, None] * solved[None, :]

    return lax.fori_loop(0, order, row_step, jnp.zeros_like(upper))


def local(positions, momenta, kick_strength, coupling, tangent, log_growth):
    local_rows = positions.shape[0]
    columns = positions.shape[1]
    vectors = tangent.shape[3]
    padded_angles = with_halo(positions, (("rows", 0),), 1)
    angle_sides = (
        padded_angles[:-2],
        padded_angles[2:],
        jnp.roll(positions, 1, 1),
        jnp.roll(positions, -1, 1),
    )
    force = kick_strength * jnp.sin(positions)
    spring = jnp.zeros_like(positions)
    for side in angle_sides:
        spring = spring + jnp.sin(side - positions)
    new_momenta = momenta + force + coupling * spring
    new_positions = positions + new_momenta
    tan_pos = tangent[0]
    tan_mom = tangent[1]
    padded_tan = with_halo(tan_pos, (("rows", 0),), 1)
    tan_sides = (padded_tan[:-2], padded_tan[2:], jnp.roll(tan_pos, 1, 1), jnp.roll(tan_pos, -1, 1))
    slope = (kick_strength * jnp.cos(positions))[:, :, None]
    spread = jnp.zeros_like(tan_pos)
    for side, tan_side in zip(angle_sides, tan_sides):
        weight = (coupling * jnp.cos(side - positions))[:, :, None]
        spread = spread + weight * (tan_side - tan_pos)
    mom_next = tan_mom + slope * tan_pos + spread
    pos_next = tan_pos + mom_next
    stacked = jnp.stack([pos_next, mom_next]).reshape(-1, vectors)
    summed_gram = lax.psum(inner_gram(stacked), "rows")
    whole_upper = upper_factor(summed_gram)
    sites_total = local_rows * lax.axis_size("rows") * columns
    ortho = jnp.dot(stacked, upper_inverse(whole_upper), precision=lax.Precision.HIGHEST)
    tangent_out = (ortho * math.sqrt(sites_total)).reshape(2, local_rows, columns, vectors)
    diagonal = jnp.diagonal(whole_upper)
    growth_out = log_growth + jnp.log(diagonal) - 0.5 * math.log(sites_total)
    return (new_positions, new_momenta, tangent_out, growth_out)


def solution(mesh):
    placed = (
        P("rows", "groups"),
        P("rows", "groups"),
        P("rows", None),
        P("rows", None),
        P("groups", "rows", None, None),
        P("groups"),
    )
    return jax.shard_map(
        local,
        mesh=mesh,
        in_specs=placed,
        out_specs=(
            P("rows", "groups"),
            P("rows", "groups"),
            P("groups", "rows", None, None),
            P("groups"),
        ),
        check_vma=False,
    )
```

profile of v0, /device:TPU:0, one launch (start us, length us, event | category | flops | bytes accessed | tf_op | source)
XLA Modules:
  0.0 848.0 jit_solution(7118980005125419949)
XLA Ops:
  8.0 5.5 collective-permute-start.1
  13.5 2.3 slice_bitcast_fusion.2
  15.7 4.4 collective-permute-start.3
  20.3 1.7 slice_bitcast_fusion
  22.1 2.3 fusion.31
  27.2 4.5 collective-permute-done.2
  31.7 7.2 add_bitcast_fusion
  40.9 7.4 convolution_bitcast_fusion.1
  48.3 4.5 pad_maximum_fusion
  52.8 77.7 %all-reduce.2.cloned.1.call-done = f32[128,128]{1,0:T(8,128)} async-done(((f32[128,128]{1,0:T(8,128)}), f32[128,128]{1,0:T(8,128)}) %all-reduce.2.cloned.1.call-update) | async-done | bytes 65552 | tf_op jit(solution)/shard_map/psum | solution.py:92
  130.5 491.4 %while.32 = (s32[]{:T(128)}, f32[128,128]{1,0:T(8,128)}, f32[128,128]{1,0:T(8,128)S(1)}, s32[]{:T(128)}, s32[]{:T(128)}) while((s32[]{:T(128)}, f32[128,128]{1,0:T(8,128)}, f32[128,128]{1,0:T(8,128)S(1)}, s32[]{:T(128)}, s32[]{:T(128)}) %tuple.84), condition=%wide.region_4.5_spmd.clone.clone, body=%wide.region_1.4_spmd.clone.clone.sunk | while | flops 115586 | bytes 331883 | solution.py:43
  132.7 1.6 select_add_fusion.2
  136.6 1.6 select_add_fusion.2
  140.4 1.6 select_add_fusion.2
  144.3 1.6 select_add_fusion.2
  148.1 1.6 select_add_fusion.2
  151.9 1.6 select_add_fusion.2
  155.8 1.6 select_add_fusion.2
  159.6 1.6 select_add_fusion.2
  163.5 1.6 select_add_fusion.2
  167.3 1.6 select_add_fusion.2
  171.1 1.6 select_add_fusion.2
  175.0 1.6 select_add_fusion.2
  178.8 1.6 select_add_fusion.2
  182.7 1.6 select_add_fusion.2
  186.5 1.6 select_add_fusion.2
  190.3 1.6 select_add_fusion.2
  194.2 1.6 select_add_fusion.2
  198.0 1.6 select_add_fusion.2
  201.8 1.6 select_add_fusion.2
  205.7 1.6 select_add_fusion.2
  209.5 1.6 select_add_fusion.2
  213.4 1.6 select_add_fusion.2
  217.2 1.6 select_add_fusion.2
  221.0 1.6 select_add_fusion.2
  224.9 1.6 select_add_fusion.2
  228.7 1.6 select_add_fusion.2
  232.6 1.6 select_add_fusion.2
  236.4 1.6 select_add_fusion.2
  240.2 1.6 select_add_fusion.2
  244.1 1.6 select_add_fusion.2
  247.9 1.6 select_add_fusion.2
  251.8 1.6 select_add_fusion.2
  255.6 1.6 select_add_fusion.2
  259.4 1.6 select_add_fusion.2
  263.3 1.6 select_add_fusion.2
  267.1 1.6 select_add_fusion.2
  270.9 1.6 select_add_fusion.2
  274.8 1.6 select_add_fusion.2
  278.6 1.6 select_add_fusion.2
  282.5 1.6 select_add_fusion.2
  286.3 1.6 select_add_fusion.2
  290.1 1.6 select_add_fusion.2
  305.5 1.6 select_add_fusion.2
  347.7 1.6 select_add_fusion.2
  378.4 1.6 select_add_fusion.2
  420.7 1.6 select_add_fusion.2
  451.4 1.6 select_add_fusion.2
  493.6 1.6 select_add_fusion.2
  524.3 1.6 select_add_fusion.2
  566.5 1.6 select_add_fusion.2
  597.3 1.6 select_add_fusion.2
  622.0 210.9 %while.33 = (s32[]{:T(128)}, f32[128,128]{1,0:T(8,128)S(1)}, f32[128,128]{1,0:T(8,128)S(1)}, s32[]{:T(128)}, s32[]{:T(128)}, /*index=5*/s32[]{:T(128)}) while((s32[]{:T(128)}, f32[128,128]{1,0:T(8,128)S(1)}, f32[128,128]{1,0:T(8,128)S(1)}, s32[]{:T(128)}, s32[]{:T(128)}, /*index=5*/s32[]{:T(128)}) %tuple.92), condition=%wide.region_8.9_spmd.clone.clone, body=%wide.region_5.8_spmd.clone.clone.sunk | while | flops 296195 | bytes 266360 | solution.py:60
  834.2 6.5 convolution_multiply_fusion
  (1262 shorter events, 534.4 us)
Async XLA Ops:
  7.2 13.0 %copy-start.2 = (f32[4,1024]{1,0:T(4,128)S(1)}, f32[4,1024]{1,0:T(4,128)}, u32[]{:S(2)}) copy-start(f32[4,1024]{1,0:T(4,128)} %param.10) | copy-start | bytes 49156
  7.2 123.3 %all-reduce.2.cloned.1.call-start = ((), (), s32[]{:S(2)}) async-start(), calls=%async_computation | async-start | bytes 131072 | tf_op jit(solution)/shard_map/psum | solution.py:92
  8.0 16.4 %collective-permute-start.1 = (f32[1,1024]{1,0:T(1,128)S(1)}, f32[1,1024]{1,0:T(1,128)S(1)}, u32[]{:S(2)}, u32[]{:S(2)}) collective-permute-start(f32[1,1024]{1,0:T(1,128)S(1)} %get-tuple-element.251), channel_id=1, source_target_pairs={{1,0},{2,1},{3,2},{4,3},{5,4},{6,5},{7,6},{8,7},{9,8},{10,9},{11,1... | collective-permute-start | bytes 12296 | tf_op jit(solution)/shard_map/ppermute | solution.py:17
  13.5 11.1 %collective-permute-start = (f32[1,1024]{1,0:T(1,128)S(1)}, f32[1,1024]{1,0:T(1,128)S(1)}, u32[]{:S(2)}, u32[]{:S(2)}) collective-permute-start(f32[1,1024]{1,0:T(1,128)S(1)} %get-tuple-element.250), channel_id=1, source_target_pairs={{0,1},{1,2},{2,3},{3,4},{4,5},{5,6},{6,7},{7,8},{8,9},{9,10},{10,1... | collective-permute-start | bytes 12296 | tf_op jit(solution)/shard_map/ppermute | solution.py:16
  15.7 11.5 %collective-permute-start.3 = (f32[1,1024,128]{2,1,0:T(8,128)}, f32[1,1024,128]{2,1,0:T(8,128)S(1)}, u32[]{:S(2)}, u32[]{:S(2)}) collective-permute-start(f32[1,1024,128]{2,1,0:T(8,128)} %get-tuple-element.241), channel_id=1, source_target_pairs={{1,0},{2,1},{3,2},{4,3},{5,4},{6,5},{7,6},{8,7},{9,8},{10,9},{11,1... | collective-permute-start | bytes 1572872 | tf_op jit(solution)/shard_map/ppermute | solution.py:17
  20.2 11.5 %collective-permute-start.2 = (f32[1,1024,128]{2,1,0:T(8,128)}, f32[1,1024,128]{2,1,0:T(8,128)S(1)}, u32[]{:S(2)}, u32[]{:S(2)}) collective-permute-start(f32[1,1024,128]{2,1,0:T(8,128)} %get-tuple-element.240), channel_id=1, source_target_pairs={{0,1},{1,2},{2,3},{3,4},{4,5},{5,6},{6,7},{7,8},{8,9},{9,10},{10,1... | collective-permute-start | bytes 1572872 | tf_op jit(solution)/shard_map/ppermute | solution.py:16
  22.1 2.4 copy-start.3
  22.1 2.5 copy-start.4
  22.1 2.5 copy-start.5
  38.9 1.3 copy-start
  38.9 2.0 copy-start.1
  834.1 6.5 copy-start.6
Sparse Core Ops, SparseCore 0:
  48.4 82.0 all-reduce.1
where the time goes:
time: 864 us; the launch traced here: 848 us
  other arithmetic  518 us (60%)
  matrix products  116 us (13%)
  loops' own time  95.6 us (11%)
  waiting for transfers between devices  83.6 us (10%)
  between operations  14.2 us (2%)
  local copies, waits for them, and re-layouts  10.6 us (1%)
  starting transfers between devices  9.95 us (1%)
    add x128, other arithmetic, column_step(): lower = lower + scaled[:, None] * pick[None, :]  201 us
    reduce_sum x128, other arithmetic, column_step(): column = jnp.sum(work * pick[None, :], 1)  120 us
    dot_general x128, matrix products, row_step(): jnp.dot(rest, inverse, precision=lax.Precision.HIGHEST)  102 us
    another operation x1, loops' own time, upper_factor(): work, lower = lax.fori_loop(0, order, column_step, start)  91.1 us
    reduce_sum x128, other arithmetic, column_step(): pivot = jnp.sum(column * pick)  78.3 us
    reduce_sum x128, other arithmetic, row_step(): pivot = jnp.sum(row * pick)  78.1 us
    psum x1, waiting for transfers between devices, local(): summed_gram = lax.psum(inner_gram(stacked), 'rows')  77.7 us
  transfers between devices with their start and end apart: 5, of which 3 were waited for; matrix products, arithmetic and copies ran while one was open for 1% of the time, Pallas kernels for 0%

commit v1 on v0

v1 whole, which is shorter than its diff:
```python
import functools
import math

import jax
import jax.numpy as jnp
from jax import lax
from jax.experimental import pallas as pl
from jax.experimental.pallas import tpu as pltpu
from jax.sharding import PartitionSpec as P

LANES = 128
MIB = 1 << 20


def lane_roll(field, shift):
    return pltpu.roll(field, shift % field.shape[1], axis=1)


def split_pair(value):
    high = value.astype(jnp.bfloat16)
    low = (value - high.astype(jnp.float32)).astype(jnp.bfloat16)
    return jnp.concatenate([high, low], axis=1)


def pair_gram(pairs):
    return lax.dot_general(
        pairs, pairs, (((0,), (0,)), ((), ())), preferred_element_type=jnp.float32
    )


def fold_pairs(gram):
    half = gram.shape[0] // 2
    return (gram[:half, :half] + gram[half:, half:]) + (gram[:half, half:] + gram[half:, :half])


def edges_kernel(tangent_ref, positions_ref, near_ref, far_ref, sems):
    rows, columns = positions_ref.shape
    odd = lax.rem(lax.axis_index("rows"), 2)
    near_row = (1 - odd) * (rows - 1)
    copies = []
    for slot, (row, out) in enumerate(((near_row, near_ref), (rows - 1 - near_row, far_ref))):
        copy = pltpu.make_async_copy(
            tangent_ref.at[0, row], out.at[pl.ds(0, columns)], sems.at[slot]
        )
        copy.start()
        copies.append(copy)
        angles = positions_ref[pl.ds(row, 1), :]
        for group in range(columns // LANES):
            out[columns + group : columns + group + 1, :] = angles[
                :, group * LANES : (group + 1) * LANES
            ]
    for copy in copies:
        copy.wait()


def inner_kernel(
    tangent_ref, positions_ref, kick_ref, coupling_ref,
    pairs_ref, partial_ref, gram_ref,
    pos_pad, mom_buf, stack, sems,
):
    rows, columns = positions_ref.shape
    groups = columns // LANES
    order = [*range(rows)]
    pos_copies = [
        pltpu.make_async_copy(
            tangent_ref.at[0, r], pos_pad.at[r, pl.ds(8, columns)], sems.at[0, r]
        )
        for r in order
    ]
    mom_copies = [
        pltpu.make_async_copy(tangent_ref.at[1, r], mom_buf.at[r], sems.at[1, r]) for r in order
    ]
    for r in order:
        pos_copies[r].start()
        mom_copies[r].start()

    x = positions_ref[...]
    coupling = coupling_ref[...]
    left = coupling * jnp.cos(lane_roll(x, 1) - x)
    right = coupling * jnp.cos(lane_roll(x, -1) - x)
    vertical = jnp.cos(x[1:] - x[:-1])
    none = jnp.zeros((1, columns), jnp.float32)
    up = coupling * jnp.concatenate([none, vertical], axis=0)
    down = coupling * jnp.concatenate([vertical, none], axis=0)
    centre = kick_ref[...] * jnp.cos(x) - ((left + right) + (up + down))
    for k, weight in enumerate((centre, left, right, up, down)):
        for r in range(rows):
            for group in range(groups):
                at = k * groups + group
                stack[r, at : at + 1, :] = weight[r : r + 1, group * LANES : (group + 1) * LANES]

    for r in order:
        pos_copies[r].wait()
        mom_copies[r].wait()
        pos_pad[r, 7:8, :] = pos_pad[r, 7 + columns : 8 + columns, :]
        pos_pad[r, 8 + columns : 9 + columns, :] = pos_pad[r, 8:9, :]

    def stepped(r, group, table, sides):
        at = 8 + group * LANES
        factor = lambda k: jnp.broadcast_to(
            table[:, k * groups + group : k * groups + group + 1], (LANES, LANES)
        )
        u = pos_pad[r, at : at + LANES, :]
        total = mom_buf[r, group * LANES : (group + 1) * LANES, :] + factor(0) * u
        total = total + factor(1) * pos_pad[r, at - 1 : at - 1 + LANES, :]
        total = total + factor(2) * pos_pad[r, at + 1 : at + 1 + LANES, :]
        for k, other in sides:
            total = total + factor(k) * pos_pad[other, at : at + LANES, :]
        return u, total

    for slot, (r, sides) in enumerate(((0, ((4, 1),)), (rows - 1, ((3, rows - 2),)))):
        table = stack[r].T
        for group in range(groups):
            _, total = stepped(r, group, table, sides)
            partial_ref[slot, group * LANES : (group + 1) * LANES, :] = total

    gram = jnp.zeros((2 * LANES, 2 * LANES), jnp.float32)
    for r in range(1, rows - 1):
        table = stack[r].T
        for group in range(groups):
            u, mom = stepped(r, group, table, ((3, r - 1), (4, r + 1)))
            span = pl.ds(group * LANES, LANES)
            pairs_ref[0, r - 1, span, :] = split_pair(u + mom)
            pairs_ref[1, r - 1, span, :] = split_pair(mom)
        for part in range(2):
            gram = gram + pair_gram(pairs_ref[part, r - 1])
    gram_ref[...] = fold_pairs(gram)


def edge_gram_kernel(
    near_ref, far_ref, partial_ref, tangent_ref, positions_ref, coupling_ref, inner_gram_ref,
    pairs_ref, gram_ref,
    pos_buf, stack, sems,
):
    rows, columns = positions_ref.shape
    groups = columns // LANES
    copies = [
        pltpu.make_async_copy(tangent_ref.at[0, r], pos_buf.at[slot], sems.at[slot])
        for slot, r in enumerate((0, rows - 1))
    ]
    for copy in copies:
        copy.start()
    odd = lax.rem(lax.axis_index("rows"), 2)
    gram = jnp.zeros((2 * LANES, 2 * LANES), jnp.float32)
    for side, received in enumerate((near_ref, far_ref)):
        slot = (1 - odd) if side == 0 else odd
        row = slot * (rows - 1)
        x = positions_ref[pl.ds(row, 1), :]
        coupling = coupling_ref[pl.ds(row, 1), :]
        for group in range(groups):
            span = slice(group * LANES, (group + 1) * LANES)
            at = side * groups + group
            stack[at : at + 1, :] = coupling[:, span] * jnp.cos(
                received[columns + group : columns + group + 1, :] - x[:, span]
            )
    for copy in copies:
        copy.wait()
    table = stack[...].T
    for side, received in enumerate((near_ref, far_ref)):
        slot = (1 - odd) if side == 0 else odd
        for group in range(groups):
            span = slice(group * LANES, (group + 1) * LANES)
            at = side * groups + group
            factor = jnp.broadcast_to(table[:, at : at + 1], (LANES, LANES))
            u = pos_buf[slot, span, :]
            mom = partial_ref[slot, span, :] + factor * (received[span, :] - u)
            pairs_ref[0, slot, span, :] = split_pair(u + mom)
            pairs_ref[1, slot, span, :] = split_pair(mom)
        for part in range(2):
            gram = gram + pair_gram(pairs_ref[part, slot])
    gram_ref[...] = inner_gram_ref[...] + fold_pairs(gram)


def inverse_factor(gram_ref, inverse_ref):
    order = gram_ref.shape[0]
    step = 8
    lane = lax.broadcasted_iota(jnp.int32, (step, order), 1)
    sub = lax.broadcasted_iota(jnp.int32, (step, order), 0)
    spread = lambda value: jnp.broadcast_to(value, (step, order))
    work = [gram_ref[at : at + step, :] for at in range(0, order, step)]
    squares = jnp.ones((step, order), jnp.float32)
    for block in range(order // step):
        first = block * step
        own = work[block]
        columns = [spread(own[:, first + a : first + a + 1]) for a in range(step)]
        pivot = [
            [spread(columns[a][i : i + 1, :]) if i >= a else None for a in range(step)]
            for i in range(step)
        ]
        inside = (lane >= first) & (lane < first + step)
        extended = jnp.where(inside, jnp.where(lane - first == sub, 1.0, 0.0), own)
        solved = [spread(extended[a : a + 1, :]) for a in range(step)]
        recip = [None] * step
        lower = [[None] * step for _ in range(step)]
        for a in range(step):
            recip[a] = 1.0 / pivot[a][a]
            for i in range(a + 1, step):
                lower[i][a] = pivot[i][a] * recip[a]
            for b in range(a + 1, step):
                for i in range(b, step):
                    pivot[i][b] = pivot[i][b] - lower[i][a] * pivot[b][a]
        for a in range(step):
            for i in range(a + 1, step):
                solved[i] = solved[i] - lower[i][a] * solved[a]
        scaled = [solved[a] * recip[a] for a in range(step)]
        for a in range(step - 1, 0, -1):
            for i in range(a):
                scaled[i] = scaled[i] - lower[a][i] * scaled[a]
        for later in range(block + 1, order // step):
            rest = work[later]
            t = [spread(rest[:, first + a : first + a + 1]) * scaled[a] for a in range(step)]
            while len(t) > 1:
                t = [t[i] + t[i + 1] for i in range(0, len(t), 2)]
            work[later] = jnp.where(inside, 0.0, rest) - t[0]
        rows_out, diagonal = solved[0], pivot[0][0]
        for a in range(step):
            rows_out = jnp.where(sub == a, solved[a], rows_out)
            diagonal = jnp.where(sub == a, pivot[a][a], diagonal)
            squares = jnp.where(lane == first + a, pivot[a][a], squares)
        inverse_ref[first : first + step, :] = jnp.where(
            lane <= first + sub, rows_out * lax.rsqrt(diagonal), 0.0
        )
    return squares


def ortho_kernel(
    sites_total, gram_ref, log_growth_ref, inner_ref, edge_ref,
    out_ref, growth_ref,
    inverse_ref, inner_buf, edge_buf, out_buf, in_sems, out_sems,
):
    rows = out_ref.shape[1]
    loads = [
        pltpu.make_async_copy(inner_ref, inner_buf, in_sems.at[0]),
        pltpu.make_async_copy(edge_ref, edge_buf, in_sems.at[1]),
    ]
    for load in loads:
        load.start()
    squares = inverse_factor(gram_ref, inverse_ref)
    growth_ref[...] = (
        log_growth_ref[...] + 0.5 * jnp.log(squares[:1]) - 0.5 * math.log(sites_total)
    )
    factor = split_pair(inverse_ref[...] * math.sqrt(sites_total))
    high, low = factor[:, :LANES], factor[:, LANES:]
    weights = jnp.concatenate(
        [jnp.concatenate([high, high], axis=1), jnp.concatenate([low, low], axis=1)], axis=0
    )
    for load in loads:
        load.wait()
    stores = []
    for part in range(2):
        for r in range(rows):
            if r in (0, rows - 1):
                pairs = edge_buf[part, 0 if r == 0 else 1]
            else:
                pairs = inner_buf[part, r - 1]
            both = lax.dot_general(
                pairs, weights, (((1,), (1,)), ((), ())), preferred_element_type=jnp.float32
            )
            out_buf[part, r] = both[:, :LANES] + both[:, LANES:]
            store = pltpu.make_async_copy(
                out_buf.at[part, r], out_ref.at[part, r], out_sems.at[part, r]
            )
            store.start()
            stores.append(store)
    for store in stores:
        store.wait()


def sum_over_rows(value):
    devices = lax.axis_size("rows")
    if devices & (devices - 1):
        return lax.psum(value, "rows")
    bit = 1
    while bit < devices:
        value = value + lax.ppermute(value, "rows", [(i, i ^ bit) for i in range(devices)])
        bit *= 2
    return value


def local(positions, momenta, kick_strength, coupling, tangent, log_growth):
    rows, columns = positions.shape
    vectors = tangent.shape[3]
    devices = lax.axis_size("rows")
    groups = columns // LANES
    anywhere = pl.BlockSpec(memory_space=pl.ANY)
    resident = pl.BlockSpec(memory_space=pltpu.VMEM)
    f32 = lambda *shape: jax.ShapeDtypeStruct(shape, jnp.float32)
    bf16 = lambda *shape: jax.ShapeDtypeStruct(shape, jnp.bfloat16)

    near, far = pl.pallas_call(
        edges_kernel,
        out_shape=[f32(columns + groups, vectors)] * 2,
        in_specs=[anywhere, resident],
        out_specs=[resident] * 2,
        scratch_shapes=[pltpu.SemaphoreType.DMA((2,))],
        name="edges",
    )(tangent, positions)
    far = lax.ppermute(
        far, "rows", [(i, (i + 1 if i % 2 else i - 1) % devices) for i in range(devices)]
    )
    near = lax.ppermute(near, "rows", [(i, i ^ 1) for i in range(devices)])

    inner_pairs, partial, inner_gram = pl.pallas_call(
        inner_kernel,
        out_shape=[
            bf16(2, rows - 2, columns, 2 * vectors),
            f32(2, columns, vectors),
            f32(vectors, vectors),
        ],
        in_specs=[anywhere, resident, resident, resident],
        out_specs=[resident] * 3,
        scratch_shapes=[
            pltpu.VMEM((rows, columns + 16, vectors), jnp.float32),
            pltpu.VMEM((rows, columns, vectors), jnp.float32),
            pltpu.VMEM((rows, LANES, LANES), jnp.float32),
            pltpu.SemaphoreType.DMA((2, rows)),
        ],
        compiler_params=pltpu.CompilerParams(vmem_limit_bytes=24 * MIB),
        cost_estimate=pl.CostEstimate(
            flops=2 * 10**9, bytes_accessed=8 * MIB, transcendentals=0
        ),
        name="inner",
    )(tangent, positions, kick_strength, coupling)

    edge_pairs, gram = pl.pallas_call(
        edge_gram_kernel,
        out_shape=[bf16(2, 2, columns, 2 * vectors), f32(vectors, vectors)],
        in_specs=[resident, resident, resident, anywhere, resident, resident, resident],
        out_specs=[resident] * 2,
        scratch_shapes=[
            pltpu.VMEM((2, columns, vectors), jnp.float32),
            pltpu.VMEM((LANES, LANES), jnp.float32),
            pltpu.SemaphoreType.DMA((2,)),
        ],
        compiler_params=pltpu.CompilerParams(vmem_limit_bytes=16 * MIB),
        name="edge_gram",
    )(near, far, partial, tangent, positions, coupling, inner_gram)
    gram = sum_over_rows(gram)

    near_angles = near[columns:].reshape(1, columns)
    far_angles = far[columns:].reshape(1, columns)
    odd = lax.axis_index("rows") % 2 == 1
    above = jnp.where(odd, near_angles, far_angles)
    below = jnp.where(odd, far_angles, near_angles)
    padded = jnp.concatenate([above, positions, below], axis=0)
    spring = jnp.sin(padded[:-2] - positions) + jnp.sin(padded[2:] - positions)
    spring = spring + jnp.sin(jnp.roll(positions, 1, 1) - positions)
    spring = spring + jnp.sin(jnp.roll(positions, -1, 1) - positions)
    new_momenta = momenta + kick_strength * jnp.sin(positions) + coupling * spring
    new_positions = positions + new_momenta

    sites_total = rows * devices * columns
    tangent_out, growth = pl.pallas_call(
        functools.partial(ortho_kernel, sites_total),
        out_shape=[f32(2, rows, columns, vectors), f32(1, vectors)],
        in_specs=[resident, resident, anywhere, anywhere],
        out_specs=[anywhere, resident],
        scratch_shapes=[
            pltpu.VMEM((vectors, vectors), jnp.float32),
            pltpu.VMEM((2, rows - 2, columns, 2 * vectors), jnp.bfloat16),
            pltpu.VMEM((2, 2, columns, 2 * vectors), jnp.bfloat16),
            pltpu.VMEM((2, rows, columns, vectors), jnp.float32),
            pltpu.SemaphoreType.DMA((2,)),
            pltpu.SemaphoreType.DMA((2, rows)),
        ],
        compiler_params=pltpu.CompilerParams(vmem_limit_bytes=24 * MIB),
        name="ortho",
    )(gram, log_growth.reshape(1, vectors), inner_pairs, edge_pairs)
    return (new_positions, new_momenta, tangent_out, growth.reshape(vectors))


def solution(mesh):
    placed = (
        P("rows", "groups"),
        P("rows", "groups"),
        P("rows", None),
        P("rows", None),
        P("groups", "rows", None, None),
        P("groups"),
    )
    return jax.shard_map(
        local,
        mesh=mesh,
        in_specs=placed,
        out_specs=(
            P("rows", "groups"),
            P("rows", "groups"),
            P("groups", "rows", None, None),
            P("groups"),
        ),
        check_vma=False,
    )
```

time: 864 us -> 47.8 us (0.06); the launches traced: 848 us -> 47.5 us
  other arithmetic: 518 us -> 1.22 us
  matrix products: 116 us -> 0 us
  loops' own time: 95.6 us -> 0 us
  waiting for transfers between devices: 83.6 us -> 6.7 us
  Pallas kernels: 0 us -> 17.5 us
  between operations: 14.2 us -> 0.76 us
    reduce_sum x512 -> x0, other arithmetic: 289 us -> none  [the longest x128 120 us: column_step(): column = jnp.sum(work * pick[None, :], 1)]
    add x256 -> x4, other arithmetic: 214 us -> 0.04 us  [sum_over_rows(): value + lax.ppermute(value, 'rows', [(i, i ^ bit) for i in range(devices)])]
    dot_general x130 -> x0, matrix products: 116 us -> none  [the longest x128 102 us: row_step(): jnp.dot(rest, inverse, precision=lax.Precision.HIGHEST)]
    another operation x2 -> x0, loops' own time: 95.6 us -> none  [the longest x1 91.1 us: upper_factor(): work, lower = lax.fori_loop(0, order, column_step, start)]
    psum x1 -> x0, waiting for transfers between devices: 77.7 us -> none  [local(): summed_gram = lax.psum(inner_gram(stacked), 'rows')]
    pallas_call x0 -> x4, Pallas kernels: none -> 17.5 us  [the longest x1 7.91 us: local(): pl.pallas_call(functools.partial(ortho_kernel, sites_total), out_shape=[f...]
    another operation x2 -> x0, other arithmetic: 11.7 us -> none  [local(): stacked = jnp.stack([pos_next, mom_next]).reshape(-1, vectors)]
  transfers between devices with their start and end apart: 5 -> 6, of which waited for: 3 -> 5; matrix products, arithmetic and copies ran while one was open for 1% -> 3% of each run, Pallas kernels for 0% -> 10%
where the time goes in v1:
time: 47.8 us; the launch traced here: 47.5 us
  Pallas kernels  17.5 us (37%)
  starting transfers between devices  16.1 us (34%)
  waiting for transfers between devices  6.7 us (14%)
  local copies, waits for them, and re-layouts  5.26 us (11%)
  other arithmetic  1.22 us (3%)
  between operations  0.76 us (2%)
    ppermute x4, starting transfers between devices, sum_over_rows(): lax.ppermute(value, 'rows', [(i, i ^ bit) for i in range(devices)])  9.9 us
    pallas_call x1, Pallas kernels, local(): pl.pallas_call(functools.partial(ortho_kernel, sites_total), out_shape=[f...  7.91 us
    ppermute x4, waiting for transfers between devices, sum_over_rows(): lax.ppermute(value, 'rows', [(i, i ^ bit) for i in range(devices)])  6.47 us
    ppermute x1, starting transfers between devices, local(): lax.ppermute(far, 'rows', [(i, (i + 1 if i % 2 else i - 1) % devices) for...  5.64 us
    unnamed x18, local copies, waits for them, and re-layouts  5.11 us
    pallas_call x1, Pallas kernels, local(): pl.pallas_call(inner_kernel, out_shape=[bf16(2, rows - 2, columns, 2 * ve...  4.76 us
    pallas_call x1, Pallas kernels, local(): pl.pallas_call(edges_kernel, out_shape=[f32(columns + groups, vectors)] *...  2.96 us
    pallas_call x1, Pallas kernels, local(): pl.pallas_call(edge_gram_kernel, out_shape=[bf16(2, 2, columns, 2 * vecto...  1.87 us
  transfers between devices with their start and end apart: 6, of which 5 were waited for; matrix products, arithmetic and copies ran while one was open for 3% of the time, Pallas kernels for 10%

profile of v1, /device:TPU:0, one launch (start us, length us, event | category | flops | bytes accessed | tf_op | source)
XLA Modules:
  0.0 47.5 jit_solution(12111521035192561265)
XLA Ops:
  0.6 0.0 copy-start.4
  0.6 0.0 copy-start.5
  0.7 0.0 copy-start.6
  0.7 3.0 %edges.1 = (f32[1032,128]{1,0:T(8,128)}, f32[1032,128]{1,0:T(8,128)}) custom-call(f32[2,4,1024,128]{3,2,1,0:T(8,128)} %tangent_ref.5, f32[4,1024]{1,0:T(4,128)} %positions_ref.5), custom_call_target="tpu_custom_call" | custom-call | tf_op jit(solution)/shard_map/edges/pallas_call | solution.py:290
  3.6 0.5 %collective-permute-start = (f32[1032,128]{1,0:T(8,128)}, f32[1032,128]{1,0:T(8,128)S(1)}, u32[]{:S(2)}, u32[]{:S(2)}) collective-permute-start(f32[1032,128]{1,0:T(8,128)} %get-tuple-element.13), channel_id=1, source_target_pairs={{0,1},{1,0},{2,3},{3,2},{4,5},{5,4},{6,7},{7,6},{8,9},{9,8},{10,11... | collective-permute-start | bytes 1585160 | tf_op jit(solution)/shard_map/ppermute | solution.py:301
  4.1 5.6 %collective-permute-start.1 = (f32[1032,128]{1,0:T(8,128)}, f32[1032,128]{1,0:T(8,128)S(1)}, u32[]{:S(2)}, u32[]{:S(2)}) collective-permute-start(f32[1032,128]{1,0:T(8,128)} %get-tuple-element.14), channel_id=1, source_target_pairs={{0,15},{1,2},{2,1},{3,4},{4,3},{5,6},{6,5},{7,8},{8,7},{9,10},{10,... | collective-permute-start | bytes 1585160 | tf_op jit(solution)/shard_map/ppermute | solution.py:298
  9.8 0.0 copy-done.4
  9.8 0.0 copy-done.5
  9.8 0.0 copy-done.6
  9.8 0.0 copy-start
  9.8 2.2 %copy-done = f32[2,4,1024,128]{3,2,1,0:T(8,128)S(1)} copy-done((f32[2,4,1024,128]{3,2,1,0:T(8,128)S(1)}, f32[2,4,1024,128]{3,2,1,0:T(8,128)}, u32[]{:S(2)}) %copy-start) | copy-done | bytes 4194328
  12.0 0.0 copy-start.1
  12.0 4.8 %inner.1 = (bf16[2,2,1024,256]{3,2,1,0:T(8,128)(2,1)S(1)}, f32[2,1024,128]{2,1,0:T(8,128)S(1)}, f32[128,128]{1,0:T(8,128)S(1)}) custom-call(f32[2,4,1024,128]{3,2,1,0:T(8,128)S(1)} %copy-done, f32[4,1024]{1,0:T(4,128)S(1)} %copy-done.4, f32[4,1024]{1,0:T(4,128)S(1)} %copy-done.6, f32[4,1024]{1,0:T(4,128)S(1)} %copy-done.5), custom_call_target="tpu_custom_call" | custom-call | flops 2000000000 | bytes 8388608 | tf_op jit(solution)/shard_map/inner/pallas_call | solution.py:303
  16.8 0.0 copy-start.8
  16.8 0.0 copy-start.7
  16.8 0.0 collective-permute-done.near_ref
  16.8 0.2 collective-permute-done.1.far_ref
  17.0 0.0 copy-done.1
  17.0 1.9 %edge_gram.1 = (bf16[2,2,1024,256]{3,2,1,0:T(8,128)(2,1)S(1)}, f32[128,128]{1,0:T(8,128)S(1)}) custom-call(f32[1032,128]{1,0:T(8,128)S(1)} %collective-permute-done.near_ref, f32[1032,128]{1,0:T(8,128)S(1)} %collective-permute-done.1.far_ref, f32[2,1024,128]{2,1,0:T(8,128)S(1)} %get-tuple-element.15.partial_ref, f32[2,4,1024,128]{3,2,1,0:T(8,128)S(1)} %copy-done.1, ...), custom_call_target="tpu_custom_call" | custom-call | tf_op jit(solution)/shard_map/edge_gram/pallas_call | solution.py:325
  18.9 0.0 copy-start.2
  18.9 1.3 %copy-done.2 = bf16[2,2,1024,256]{3,2,1,0:T(8,128)(2,1)} copy-done((bf16[2,2,1024,256]{3,2,1,0:T(8,128)(2,1)}, bf16[2,2,1024,256]{3,2,1,0:T(8,128)(2,1)S(1)}, u32[]{:S(2)}) %copy-start.2) | copy-done | bytes 2097176
  20.2 2.6 %collective-permute-start.2 = (f32[128,128]{1,0:T(8,128)S(1)}, f32[128,128]{1,0:T(8,128)S(1)}, u32[]{:S(2)}, u32[]{:S(2)}) collective-permute-start(f32[128,128]{1,0:T(8,128)S(1)} %get-tuple-element.17), channel_id=1, source_target_pairs={{0,1},{1,0},{2,3},{3,2},{4,5},{5,4},{6,7},{7,6},{8,9},{9,8},{10,11... | collective-permute-start | bytes 196616 | tf_op jit(solution)/shard_map/ppermute | solution.py:275
  22.8 0.1 fusion.14
  22.9 0.8 %collective-permute-done.2 = f32[128,128]{1,0:T(8,128)S(1)} collective-permute-done((f32[128,128]{1,0:T(8,128)S(1)}, f32[128,128]{1,0:T(8,128)S(1)}, u32[]{:S(2)}, u32[]{:S(2)}) %collective-permute-start.2) | collective-permute-done | bytes 65568 | tf_op jit(solution)/shard_map/ppermute | solution.py:275
  23.7 2.0 %collective-permute-start.3 = (f32[128,128]{1,0:T(8,128)S(1)}, f32[128,128]{1,0:T(8,128)S(1)}, u32[]{:S(2)}, u32[]{:S(2)}) collective-permute-start(f32[128,128]{1,0:T(8,128)S(1)} %add.41), channel_id=1, source_target_pairs={{0,2},{1,3},{2,0},{3,1},{4,6},{5,7},{6,4},{7,5},{8,10},{9,11},{10,... | collective-permute-start | bytes 196616 | tf_op jit(solution)/shard_map/ppermute | solution.py:275
  25.8 0.1 fusion.13
  25.8 2.3 %collective-permute-done.3 = f32[128,128]{1,0:T(8,128)S(1)} collective-permute-done((f32[128,128]{1,0:T(8,128)S(1)}, f32[128,128]{1,0:T(8,128)S(1)}, u32[]{:S(2)}, u32[]{:S(2)}) %collective-permute-start.3) | collective-permute-done | bytes 65568 | tf_op jit(solution)/shard_map/ppermute | solution.py:275
  28.2 2.2 %collective-permute-start.4 = (f32[128,128]{1,0:T(8,128)S(1)}, f32[128,128]{1,0:T(8,128)S(1)}, u32[]{:S(2)}, u32[]{:S(2)}) collective-permute-start(f32[128,128]{1,0:T(8,128)S(1)} %add.42), channel_id=1, source_target_pairs={{0,4},{1,5},{2,6},{3,7},{4,0},{5,1},{6,2},{7,3},{8,12},{9,13},{10,... | collective-permute-start | bytes 196616 | tf_op jit(solution)/shard_map/ppermute | solution.py:275
  30.4 2.2 %collective-permute-done.4 = f32[128,128]{1,0:T(8,128)S(1)} collective-permute-done((f32[128,128]{1,0:T(8,128)S(1)}, f32[128,128]{1,0:T(8,128)S(1)}, u32[]{:S(2)}, u32[]{:S(2)}) %collective-permute-start.4) | collective-permute-done | bytes 65568 | tf_op jit(solution)/shard_map/ppermute | solution.py:275
  32.6 3.1 %collective-permute-start.5 = (f32[128,128]{1,0:T(8,128)S(1)}, f32[128,128]{1,0:T(8,128)S(1)}, u32[]{:S(2)}, u32[]{:S(2)}) collective-permute-start(f32[128,128]{1,0:T(8,128)S(1)} %add.43), channel_id=1, source_target_pairs={{0,8},{1,9},{2,10},{3,11},{4,12},{5,13},{6,14},{7,15},{8,0},{9,1},... | collective-permute-start | bytes 196616 | tf_op jit(solution)/shard_map/ppermute | solution.py:275
  35.7 0.0 copy-done.8
  35.7 1.2 %fusion.11 = (f32[4,1024]{1,0:T(4,128)}, f32[4,1024]{1,0:T(4,128)}) fusion(f32[4,1024]{1,0:T(4,128)S(1)} %copy-done.4, f32[4,1024]{1,0:T(4,128)S(1)} %copy-done.5, f32[4,1]{1,0:T(4,128)S(1)} %get-tuple-element.27, f32[4,1023]{1,0:T(4,128)S(1)} %get-tuple-element.29, f32[4,1023]{1,0:T(4,128)S(1)} %get-tuple-element.28, f32[4,1]{1,0:T(4,128)S(1)} %get-tuple-element.26, ...), kind=kLoop, calls=%fused_computation.17 | loop fusion | flops 65536 | bytes 139264 | tf_op jit(solution)/shard_map/add | solution.py:350
  36.9 1.1 %collective-permute-done.5 = f32[128,128]{1,0:T(8,128)S(1)} collective-permute-done((f32[128,128]{1,0:T(8,128)S(1)}, f32[128,128]{1,0:T(8,128)S(1)}, u32[]{:S(2)}, u32[]{:S(2)}) %collective-permute-start.5) | collective-permute-done | bytes 65568 | tf_op jit(solution)/shard_map/ppermute | solution.py:275
  38.0 0.0 copy-done.7
  38.0 0.0 copy-start.3
  38.0 1.6 %copy-done.3 = bf16[2,2,1024,256]{3,2,1,0:T(8,128)(2,1)S(1)} copy-done((bf16[2,2,1024,256]{3,2,1,0:T(8,128)(2,1)S(1)}, bf16[2,2,1024,256]{3,2,1,0:T(8,128)(2,1)}, u32[]{:S(2)}) %copy-start.3) | copy-done | bytes 2097176
  39.6 7.9 %ortho.1 = (f32[2,4,1024,128]{3,2,1,0:T(8,128)}, f32[1,128]{1,0:T(1,128)}) custom-call(f32[128,128]{1,0:T(8,128)S(1)} %add.44.gram_ref, f32[1,128]{1,0:T(1,128)S(1)} %bitcast.4, bf16[2,2,1024,256]{3,2,1,0:T(8,128)(2,1)S(1)} %get-tuple-element.18.inner_ref, bf16[2,2,1024,256]{3,2,1,0:T(8,128)(2,1)S(1)} %copy-done.3), custom_call_target="tpu_custom_call" | custom-call | tf_op jit(solution)/shard_map/ortho/pallas_call | solution.py:353
  (5 shorter events, 0.0 us)
Async XLA Ops:
  0.6 9.2 %copy-start.4 = (f32[4,1024]{1,0:T(4,128)S(1)}, f32[4,1024]{1,0:T(4,128)}, u32[]{:S(2)}) copy-start(f32[4,1024]{1,0:T(4,128)} %positions_ref.5) | copy-start | bytes 49156
  0.6 9.1 %copy-start.5 = (f32[4,1024]{1,0:T(4,128)S(1)}, f32[4,1024]{1,0:T(4,128)}, u32[]{:S(2)}) copy-start(f32[4,1024]{1,0:T(4,128)} %coupling_ref.3) | copy-start | bytes 49156
  0.7 9.1 %copy-start.6 = (f32[4,1024]{1,0:T(4,128)S(1)}, f32[4,1024]{1,0:T(4,128)}, u32[]{:S(2)}) copy-start(f32[4,1024]{1,0:T(4,128)} %kick_ref.1) | copy-start | bytes 49156
  3.6 13.2 %collective-permute-start = (f32[1032,128]{1,0:T(8,128)}, f32[1032,128]{1,0:T(8,128)S(1)}, u32[]{:S(2)}, u32[]{:S(2)}) collective-permute-start(f32[1032,128]{1,0:T(8,128)} %get-tuple-element.13), channel_id=1, source_target_pairs={{0,1},{1,0},{2,3},{3,2},{4,5},{5,4},{6,7},{7,6},{8,9},{9,8},{10,11... | collective-permute-start | bytes 1585160 | tf_op jit(solution)/shard_map/ppermute | solution.py:301
  4.1 12.9 %collective-permute-start.1 = (f32[1032,128]{1,0:T(8,128)}, f32[1032,128]{1,0:T(8,128)S(1)}, u32[]{:S(2)}, u32[]{:S(2)}) collective-permute-start(f32[1032,128]{1,0:T(8,128)} %get-tuple-element.14), channel_id=1, source_target_pairs={{0,15},{1,2},{2,1},{3,4},{4,3},{5,6},{6,5},{7,8},{8,7},{9,10},{10,... | collective-permute-start | bytes 1585160 | tf_op jit(solution)/shard_map/ppermute | solution.py:298
  9.8 2.2 %copy-start = (f32[2,4,1024,128]{3,2,1,0:T(8,128)S(1)}, f32[2,4,1024,128]{3,2,1,0:T(8,128)}, u32[]{:S(2)}) copy-start(f32[2,4,1024,128]{3,2,1,0:T(8,128)} %tangent_ref.5) | copy-start | bytes 12582916
  12.0 5.0 %copy-start.1 = (f32[2,4,1024,128]{3,2,1,0:T(8,128)S(1)}, f32[2,4,1024,128]{3,2,1,0:T(8,128)}, u32[]{:S(2)}) copy-start(f32[2,4,1024,128]{3,2,1,0:T(8,128)} %tangent_ref.5) | copy-start | bytes 12582916
  16.8 19.0 %copy-start.8 = (f32[4,1024]{1,0:T(4,128)S(1)}, f32[4,1024]{1,0:T(4,128)}, u32[]{:S(2)}) copy-start(f32[4,1024]{1,0:T(4,128)} %param.7) | copy-start | bytes 49156
  16.8 21.2 %copy-start.7 = (f32[128]{0:T(128)S(1)}, f32[128]{0:T(128)}, u32[]{:S(2)}) copy-start(f32[128]{0:T(128)} %param.11) | copy-start | bytes 1540
  18.9 1.3 %copy-start.2 = (bf16[2,2,1024,256]{3,2,1,0:T(8,128)(2,1)}, bf16[2,2,1024,256]{3,2,1,0:T(8,128)(2,1)S(1)}, u32[]{:S(2)}) copy-start(bf16[2,2,1024,256]{3,2,1,0:T(8,128)(2,1)S(1)} %get-tuple-element.19.edge_ref) | copy-start | bytes 6291460
  20.2 3.5 %collective-permute-start.2 = (f32[128,128]{1,0:T(8,128)S(1)}, f32[128,128]{1,0:T(8,128)S(1)}, u32[]{:S(2)}, u32[]{:S(2)}) collective-permute-start(f32[128,128]{1,0:T(8,128)S(1)} %get-tuple-element.17), channel_id=1, source_target_pairs={{0,1},{1,0},{2,3},{3,2},{4,5},{5,4},{6,7},{7,6},{8,9},{9,8},{10,11... | collective-permute-start | bytes 196616 | tf_op jit(solution)/shard_map/ppermute | solution.py:275
  23.7 4.5 %collective-permute-start.3 = (f32[128,128]{1,0:T(8,128)S(1)}, f32[128,128]{1,0:T(8,128)S(1)}, u32[]{:S(2)}, u32[]{:S(2)}) collective-permute-start(f32[128,128]{1,0:T(8,128)S(1)} %add.41), channel_id=1, source_target_pairs={{0,2},{1,3},{2,0},{3,1},{4,6},{5,7},{6,4},{7,5},{8,10},{9,11},{10,... | collective-permute-start | bytes 196616 | tf_op jit(solution)/shard_map/ppermute | solution.py:275
  28.2 4.4 %collective-permute-start.4 = (f32[128,128]{1,0:T(8,128)S(1)}, f32[128,128]{1,0:T(8,128)S(1)}, u32[]{:S(2)}, u32[]{:S(2)}) collective-permute-start(f32[128,128]{1,0:T(8,128)S(1)} %add.42), channel_id=1, source_target_pairs={{0,4},{1,5},{2,6},{3,7},{4,0},{5,1},{6,2},{7,3},{8,12},{9,13},{10,... | collective-permute-start | bytes 196616 | tf_op jit(solution)/shard_map/ppermute | solution.py:275
  32.6 5.3 %collective-permute-start.5 = (f32[128,128]{1,0:T(8,128)S(1)}, f32[128,128]{1,0:T(8,128)S(1)}, u32[]{:S(2)}, u32[]{:S(2)}) collective-permute-start(f32[128,128]{1,0:T(8,128)S(1)} %add.43), channel_id=1, source_target_pairs={{0,8},{1,9},{2,10},{3,11},{4,12},{5,13},{6,14},{7,15},{8,0},{9,1},... | collective-permute-start | bytes 196616 | tf_op jit(solution)/shard_map/ppermute | solution.py:275
  38.0 1.6 %copy-start.3 = (bf16[2,2,1024,256]{3,2,1,0:T(8,128)(2,1)S(1)}, bf16[2,2,1024,256]{3,2,1,0:T(8,128)(2,1)}, u32[]{:S(2)}) copy-start(bf16[2,2,1024,256]{3,2,1,0:T(8,128)(2,1)} %copy-done.2) | copy-start | bytes 6291460

commit v2 on v1

v2 whole, which is shorter than its diff:
```python
import functools
import math

import jax
import jax.numpy as jnp
from jax import lax
from jax.experimental import pallas as pl
from jax.experimental.pallas import tpu as pltpu
from jax.sharding import PartitionSpec as P

LANES = 128
MIB = 1 << 20


def lane_roll(field, shift):
    return pltpu.roll(field, shift % field.shape[1], axis=1)


def split_pair(value):
    high = value.astype(jnp.bfloat16)
    low = (value - high.astype(jnp.float32)).astype(jnp.bfloat16)
    return jnp.concatenate([high, low], axis=1)


def pair_gram(pairs):
    return lax.dot_general(
        pairs, pairs, (((0,), (0,)), ((), ())), preferred_element_type=jnp.float32
    )


def fold_pairs(gram):
    half = gram.shape[0] // 2
    return (gram[:half, :half] + gram[half:, half:]) + (gram[:half, half:] + gram[half:, :half])


def edges_kernel(
    tangent_ref, positions_hbm, near_ref, far_ref, tail_ref, positions_ref, sems
):
    rows, columns = positions_ref.shape
    head = columns - tail_ref.shape[0]
    odd = lax.rem(lax.axis_index("rows"), 2)
    near_row = (1 - odd) * (rows - 1)
    far_row = rows - 1 - near_row
    near, far = tangent_ref.at[0, near_row], tangent_ref.at[0, far_row]
    copies = [
        pltpu.make_async_copy(far.at[pl.ds(0, head)], far_ref.at[pl.ds(0, head)], sems.at[0]),
        pltpu.make_async_copy(far.at[pl.ds(head, columns - head)], tail_ref, sems.at[1]),
        pltpu.make_async_copy(near, near_ref.at[pl.ds(0, columns)], sems.at[2]),
    ]
    angle_copy = pltpu.make_async_copy(positions_hbm, positions_ref, sems.at[3])
    angle_copy.start()
    for copy in copies:
        copy.start()
    angle_copy.wait()
    for row, at, out in ((near_row, columns, near_ref), (far_row, head, far_ref)):
        angles = positions_ref[pl.ds(row, 1), :]
        for group in range(columns // LANES):
            out[at + group : at + group + 1, :] = angles[:, group * LANES : (group + 1) * LANES]
    for copy in copies:
        copy.wait()


def inner_kernel(
    tangent_ref, positions_ref, kick_ref, coupling_ref,
    pairs_ref, partial_ref, gram_ref,
    pos_pad, mom_buf, stack, sems,
):
    rows, columns = positions_ref.shape
    groups = columns // LANES
    order = [*range(rows)]
    pos_copies = [
        pltpu.make_async_copy(
            tangent_ref.at[0, r], pos_pad.at[r, pl.ds(8, columns)], sems.at[0, r]
        )
        for r in order
    ]
    mom_copies = [
        pltpu.make_async_copy(tangent_ref.at[1, r], mom_buf.at[r], sems.at[1, r]) for r in order
    ]
    for r in order:
        pos_copies[r].start()
        mom_copies[r].start()

    x = positions_ref[...]
    coupling = coupling_ref[...]
    left = coupling * jnp.cos(lane_roll(x, 1) - x)
    right = coupling * jnp.cos(lane_roll(x, -1) - x)
    vertical = jnp.cos(x[1:] - x[:-1])
    none = jnp.zeros((1, columns), jnp.float32)
    up = coupling * jnp.concatenate([none, vertical], axis=0)
    down = coupling * jnp.concatenate([vertical, none], axis=0)
    centre = kick_ref[...] * jnp.cos(x) - ((left + right) + (up + down))
    for k, weight in enumerate((centre, left, right, up, down)):
        for r in range(rows):
            for group in range(groups):
                at = k * groups + group
                stack[r, at : at + 1, :] = weight[r : r + 1, group * LANES : (group + 1) * LANES]

    for r in order:
        pos_copies[r].wait()
        mom_copies[r].wait()
        pos_pad[r, 7:8, :] = pos_pad[r, 7 + columns : 8 + columns, :]
        pos_pad[r, 8 + columns : 9 + columns, :] = pos_pad[r, 8:9, :]

    def stepped(r, group, table, sides):
        at = 8 + group * LANES
        factor = lambda k: jnp.broadcast_to(
            table[:, k * groups + group : k * groups + group + 1], (LANES, LANES)
        )
        u = pos_pad[r, at : at + LANES, :]
        total = mom_buf[r, group * LANES : (group + 1) * LANES, :] + factor(0) * u
        total = total + factor(1) * pos_pad[r, at - 1 : at - 1 + LANES, :]
        total = total + factor(2) * pos_pad[r, at + 1 : at + 1 + LANES, :]
        for k, other in sides:
            total = total + factor(k) * pos_pad[other, at : at + LANES, :]
        return u, total

    for slot, (r, sides) in enumerate(((0, ((4, 1),)), (rows - 1, ((3, rows - 2),)))):
        table = stack[r].T
        for group in range(groups):
            u, total = stepped(r, group, table, sides)
            partial_ref[0, slot, group * LANES : (group + 1) * LANES, :] = u
            partial_ref[1, slot, group * LANES : (group + 1) * LANES, :] = total

    gram = jnp.zeros((2 * LANES, 2 * LANES), jnp.float32)
    for r in range(1, rows - 1):
        table = stack[r].T
        for group in range(groups):
            u, mom = stepped(r, group, table, ((3, r - 1), (4, r + 1)))
            span = pl.ds(group * LANES, LANES)
            pairs_ref[0, r - 1, span, :] = split_pair(u + mom)
            pairs_ref[1, r - 1, span, :] = split_pair(mom)
        for part in range(2):
            gram = gram + pair_gram(pairs_ref[part, r - 1])
    gram_ref[...] = fold_pairs(gram)


def side_slot(side):
    odd = lax.rem(lax.axis_index("rows"), 2)
    return odd if side else 1 - odd


def row_gram_kernel(
    side, first, angles_at, angles_ref, halo_ref, partial_ref, positions_ref, coupling_ref,
    before_ref, pairs_ref, gram_ref, stack,
):
    columns = positions_ref.shape[1]
    sites = pairs_ref.shape[1]
    slot = side_slot(side)
    row = slot * (positions_ref.shape[0] - 1)
    x = positions_ref[pl.ds(row, 1), :]
    coupling = coupling_ref[pl.ds(row, 1), :]
    for group in range(sites // LANES):
        span = slice(first + group * LANES, first + (group + 1) * LANES)
        at = angles_at + first // LANES + group
        stack[group : group + 1, :] = coupling[:, span] * jnp.cos(
            angles_ref[at : at + 1, :] - x[:, span]
        )
    table = stack[...].T
    for group in range(sites // LANES):
        span = slice(group * LANES, (group + 1) * LANES)
        from_first = slice(first + group * LANES, first + (group + 1) * LANES)
        factor = jnp.broadcast_to(table[:, group : group + 1], (LANES, LANES))
        u = partial_ref[0, slot, from_first, :]
        mom = partial_ref[1, slot, from_first, :] + factor * (halo_ref[span, :] - u)
        pairs_ref[0, span, :] = split_pair(u + mom)
        pairs_ref[1, span, :] = split_pair(mom)
    gram = pair_gram(pairs_ref[0]) + pair_gram(pairs_ref[1])
    gram_ref[...] = before_ref[...] + fold_pairs(gram)


def add_kernel(left_ref, right_ref, out_ref):
    out_ref[...] = left_ref[...] + right_ref[...]


def angles_kernel(
    near_at, far_at, near_ref, far_ref, positions_ref, momenta_ref, kick_ref, coupling_ref,
    new_positions_ref, new_momenta_ref,
):
    rows, columns = positions_ref.shape
    odd = lax.rem(lax.axis_index("rows"), 2) == 1
    lay = lambda ref, at: jnp.concatenate(
        [ref[at + g : at + g + 1, :] for g in range(columns // LANES)], axis=1
    )
    near, far = lay(near_ref, near_at), lay(far_ref, far_at)
    x = positions_ref[...]
    above = jnp.concatenate([jnp.where(odd, near, far), x[:-1]], axis=0)
    below = jnp.concatenate([x[1:], jnp.where(odd, far, near)], axis=0)
    spring = jnp.sin(above - x) + jnp.sin(below - x)
    spring = spring + jnp.sin(lane_roll(x, 1) - x)
    spring = spring + jnp.sin(lane_roll(x, -1) - x)
    momenta = momenta_ref[...] + kick_ref[...] * jnp.sin(x) + coupling_ref[...] * spring
    new_momenta_ref[...] = momenta
    new_positions_ref[...] = x + momenta


def inverse_factor(gram, inverse_ref):
    order = gram.shape[0]
    step = 8
    lane = lax.broadcasted_iota(jnp.int32, (step, order), 1)
    sub = lax.broadcasted_iota(jnp.int32, (step, order), 0)
    spread = lambda value: jnp.broadcast_to(value, (step, order))
    work = [gram[at : at + step, :] for at in range(0, order, step)]
    squares = jnp.ones((step, order), jnp.float32)
    for block in range(order // step):
        first = block * step
        own = work[block]
        columns = [spread(own[:, first + a : first + a + 1]) for a in range(step)]
        pivot = [
            [spread(columns[a][i : i + 1, :]) if i >= a else None for a in range(step)]
            for i in range(step)
        ]
        inside = (lane >= first) & (lane < first + step)
        extended = jnp.where(inside, jnp.where(lane - first == sub, 1.0, 0.0), own)
        solved = [spread(extended[a : a + 1, :]) for a in range(step)]
        recip = [None] * step
        lower = [[None] * step for _ in range(step)]
        for a in range(step):
            recip[a] = 1.0 / pivot[a][a]
            for i in range(a + 1, step):
                lower[i][a] = pivot[i][a] * recip[a]
            for b in range(a + 1, step):
                for i in range(b, step):
                    pivot[i][b] = pivot[i][b] - lower[i][a] * pivot[b][a]
        for a in range(step):
            for i in range(a + 1, step):
                solved[i] = solved[i] - lower[i][a] * solved[a]
        scaled = [solved[a] * recip[a] for a in range(step)]
        for a in range(step - 1, 0, -1):
            for i in range(a):
                scaled[i] = scaled[i] - lower[a][i] * scaled[a]
        for later in range(block + 1, order // step):
            rest = work[later]
            t = [spread(rest[:, first + a : first + a + 1]) * scaled[a] for a in range(step)]
            while len(t) > 1:
                t = [t[i] + t[i + 1] for i in range(0, len(t), 2)]
            work[later] = jnp.where(inside, 0.0, rest) - t[0]
        rows_out, diagonal = solved[0], pivot[0][0]
        for a in range(step):
            rows_out = jnp.where(sub == a, solved[a], rows_out)
            diagonal = jnp.where(sub == a, pivot[a][a], diagonal)
            squares = jnp.where(lane == first + a, pivot[a][a], squares)
        inverse_ref[first : first + step, :] = jnp.where(
            lane <= first + sub, rows_out * lax.rsqrt(diagonal), 0.0
        )
    return squares


def ortho_kernel(
    sites_total, gram_ref, other_ref, log_growth_ref, inner_ref, near_ref, far_ref, tail_ref,
    out_ref, growth_ref,
    inverse_ref, out_buf, out_sems,
):
    rows, columns = out_ref.shape[1], out_ref.shape[2]
    head = far_ref.shape[1]
    squares = inverse_factor(gram_ref[...] + other_ref[...], inverse_ref)
    growth_ref[...] = (
        log_growth_ref[...] + 0.5 * jnp.log(squares[:1]) - 0.5 * math.log(sites_total)
    )
    factor = split_pair(inverse_ref[...] * math.sqrt(sites_total))
    high, low = factor[:, :LANES], factor[:, LANES:]
    weights = jnp.concatenate(
        [jnp.concatenate([high, high], axis=1), jnp.concatenate([low, low], axis=1)], axis=0
    )

    def product(pairs):
        both = lax.dot_general(
            pairs, weights, (((1,), (1,)), ((), ())), preferred_element_type=jnp.float32
        )
        return both[:, :LANES] + both[:, LANES:]

    stores = []

    def send(part, slot, row):
        store = pltpu.make_async_copy(
            out_buf.at[part, slot], out_ref.at[part, row], out_sems.at[part, slot]
        )
        store.start()
        stores.append(store)

    for part in range(2):
        for r in range(rows - 2):
            out_buf[part, r] = product(inner_ref[part, r])
            send(part, r, r + 1)
        out_buf[part, rows - 2] = product(near_ref[part])
        send(part, rows - 2, side_slot(0) * (rows - 1))
        out_buf[part, rows - 1, :head] = product(far_ref[part])
        out_buf[part, rows - 1, head:] = product(tail_ref[part])
        send(part, rows - 1, side_slot(1) * (rows - 1))
    for store in stores:
        store.wait()


def sum_over_rows(value, summed):
    devices = lax.axis_size("rows")
    if devices & (devices - 1):
        return lax.psum(value, "rows"), jnp.zeros_like(value)
    bit, other = 1, None
    while bit < devices:
        if other is not None:
            value = summed(value, other)
        other = lax.ppermute(value, "rows", [(i, i ^ bit) for i in range(devices)])
        bit *= 2
    return value, other


def local(positions, momenta, kick_strength, coupling, tangent, log_growth):
    rows, columns = positions.shape
    vectors = tangent.shape[3]
    devices = lax.axis_size("rows")
    groups = columns // LANES
    in_hbm = pl.BlockSpec(memory_space=pltpu.HBM)
    resident = pl.BlockSpec(memory_space=pltpu.VMEM)
    f32 = lambda *shape: pltpu.VMEM(shape, jnp.float32)
    bf16 = lambda *shape: pltpu.VMEM(shape, jnp.bfloat16)
    near_core = lambda array: pltpu.with_memory_space_constraint(array, pltpu.VMEM)
    tangent = pltpu.with_memory_space_constraint(tangent, pltpu.HBM)

    tail_sites = columns // 4 if columns % (4 * LANES) == 0 else LANES
    head = columns - tail_sites
    near, far, tail = pl.pallas_call(
        edges_kernel,
        out_shape=[
            f32(columns + groups, vectors), f32(head + groups, vectors), f32(tail_sites, vectors)
        ],
        in_specs=[in_hbm, in_hbm],
        out_specs=[resident] * 3,
        scratch_shapes=[
            pltpu.VMEM((rows, columns), jnp.float32), pltpu.SemaphoreType.DMA((4,))
        ],
        compiler_params=pltpu.CompilerParams(vmem_limit_bytes=4 * MIB),
        name="edges",
    )(tangent, pltpu.with_memory_space_constraint(positions, pltpu.HBM))
    outward = [(i, (i + 1 if i % 2 else i - 1) % devices) for i in range(devices)]
    far = lax.ppermute(far, "rows", outward)
    near = lax.ppermute(near, "rows", [(i, i ^ 1) for i in range(devices)])
    tail = lax.ppermute(tail, "rows", outward)

    inner_pairs, partial, inner_gram = pl.pallas_call(
        inner_kernel,
        out_shape=[
            bf16(2, rows - 2, columns, 2 * vectors),
            f32(2, 2, columns, vectors),
            f32(vectors, vectors),
        ],
        in_specs=[in_hbm, resident, resident, resident],
        out_specs=[resident] * 3,
        scratch_shapes=[
            pltpu.VMEM((rows, columns + 16, vectors), jnp.float32),
            pltpu.VMEM((rows, columns, vectors), jnp.float32),
            pltpu.VMEM((rows, LANES, LANES), jnp.float32),
            pltpu.SemaphoreType.DMA((2, rows)),
        ],
        compiler_params=pltpu.CompilerParams(vmem_limit_bytes=16 * MIB),
        cost_estimate=pl.CostEstimate(
            flops=2 * 10**9, bytes_accessed=8 * MIB, transcendentals=0
        ),
        name="inner",
    )(tangent, positions, kick_strength, coupling)

    def finish(name, side, first, sites, angles_at, angles, halo, before):
        return pl.pallas_call(
            functools.partial(row_gram_kernel, side, first, angles_at),
            out_shape=[bf16(2, sites, 2 * vectors), f32(vectors, vectors)],
            in_specs=[resident] * 6,
            out_specs=[resident] * 2,
            scratch_shapes=[pltpu.VMEM((LANES, LANES), jnp.float32)],
            compiler_params=pltpu.CompilerParams(vmem_limit_bytes=8 * MIB),
            cost_estimate=pl.CostEstimate(
                flops=4 * 10**8, bytes_accessed=2 * MIB, transcendentals=0
            ),
            name=name,
        )(
            near_core(angles), near_core(halo), near_core(partial), near_core(positions),
            near_core(coupling), near_core(before),
        )

    near_pairs, gram = finish("near", 0, 0, columns, columns, near, near, inner_gram)
    far_pairs, gram = finish("far", 1, 0, head, head, far, far, gram)
    tail_pairs, gram = finish("tail", 1, head, tail_sites, head, far, tail, gram)

    def summed(left, right):
        return pl.pallas_call(
            add_kernel,
            out_shape=f32(vectors, vectors),
            in_specs=[resident] * 2,
            out_specs=resident,
            compiler_params=pltpu.CompilerParams(vmem_limit_bytes=1 * MIB),
            name="gram_sum",
        )(near_core(left), near_core(right))

    gram, gram_other = sum_over_rows(gram, summed)

    new_positions, new_momenta = pl.pallas_call(
        functools.partial(angles_kernel, columns, head),
        out_shape=[jax.ShapeDtypeStruct((rows, columns), jnp.float32)] * 2,
        in_specs=[resident] * 6,
        out_specs=[resident] * 2,
        compiler_params=pltpu.CompilerParams(vmem_limit_bytes=4 * MIB),
        cost_estimate=pl.CostEstimate(flops=10**6, bytes_accessed=10**6, transcendentals=0),
        name="angles",
    )(near_core(near), near_core(far), positions, momenta, kick_strength, coupling)

    sites_total = rows * devices * columns
    tangent_out, growth = pl.pallas_call(
        functools.partial(ortho_kernel, sites_total),
        out_shape=[
            pltpu.HBM((2, rows, columns, vectors), jnp.float32),
            jax.ShapeDtypeStruct((1, vectors), jnp.float32),
        ],
        in_specs=[resident] * 7,
        out_specs=[in_hbm, resident],
        scratch_shapes=[
            pltpu.VMEM((vectors, vectors), jnp.float32),
            pltpu.VMEM((2, rows, columns, vectors), jnp.float32),
            pltpu.SemaphoreType.DMA((2, rows)),
        ],
        compiler_params=pltpu.CompilerParams(vmem_limit_bytes=16 * MIB),
        name="ortho",
    )(
        near_core(gram), near_core(gram_other), log_growth.reshape(1, vectors),
        near_core(inner_pairs), near_core(near_pairs), near_core(far_pairs), near_core(tail_pairs),
    )
    return (new_positions, new_momenta, tangent_out, growth.reshape(vectors))


def solution(mesh):
    placed = (
        P("rows", "groups"),
        P("rows", "groups"),
        P("rows", None),
        P("rows", None),
        P("groups", "rows", None, None),
        P("groups"),
    )
    return jax.shard_map(
        local,
        mesh=mesh,
        in_specs=placed,
        out_specs=(
            P("rows", "groups"),
            P("rows", "groups"),
            P("groups", "rows", None, None),
            P("groups"),
        ),
        check_vma=False,
    )
```

time: 47.8 us -> 41.8 us (0.87)
  local copies, waits for them, and re-layouts: 5.26 us -> 0.03 us
  Pallas kernels: 17.5 us -> 19.3 us
  other arithmetic: 1.22 us -> 0 us
  starting transfers between devices: 16.1 us -> 14.9 us
    unnamed x18 -> x10, local copies, waits for them, and re-layouts: 5.11 us -> 0.03 us
    pallas_call x1, Pallas kernels: 4.76 us -> 6.23 us  [local(): pl.pallas_call(inner_kernel, out_shape=[bf16(2, rows - 2, columns, 2 * ve...]
    add x5 -> x0, other arithmetic: 1.22 us -> none  [the longest x1 1.18 us: local(): new_positions = positions + new_momenta]
    ppermute x5 -> x6, starting transfers between devices: 15.5 us -> 14.4 us  [the longest x4 8.72 us: sum_over_rows(): other = lax.ppermute(value, 'rows', [(i, i ^ bit) for i in range(devices)])]
    pallas_call x3 -> x9, Pallas kernels: 12.7 us -> 13.1 us  [the longest x1 8.16 us: local(): pl.pallas_call(functools.partial(ortho_kernel, sites_total), out_shape=[p...]
    ppermute x5 -> x6, waiting for transfers between devices: 6.69 us -> 6.68 us  [the longest x4 6.68 us: sum_over_rows(): other = lax.ppermute(value, 'rows', [(i, i ^ bit) for i in range(devices)])]
  transfers between devices with their start and end apart: 6 -> 7, of which waited for: 5 -> 4; matrix products, arithmetic and copies ran while one was open for 3% -> 0% of each run, Pallas kernels for 10% -> 22%
where the time goes in v2:
time: 41.8 us; the launch traced here: 41.6 us
  Pallas kernels  19.3 us (46%)
  starting transfers between devices  14.9 us (36%)
  waiting for transfers between devices  6.68 us (16%)
  between operations  0.75 us (2%)
    ppermute x4, starting transfers between devices, sum_over_rows(): other = lax.ppermute(value, 'rows', [(i, i ^ bit) for i in range(devices)])  8.72 us
    pallas_call x1, Pallas kernels, local(): pl.pallas_call(functools.partial(ortho_kernel, sites_total), out_shape=[p...  8.16 us
    ppermute x4, waiting for transfers between devices, sum_over_rows(): other = lax.ppermute(value, 'rows', [(i, i ^ bit) for i in range(devices)])  6.68 us
    pallas_call x1, Pallas kernels, local(): pl.pallas_call(inner_kernel, out_shape=[bf16(2, rows - 2, columns, 2 * ve...  6.23 us
    ppermute x1, starting transfers between devices, local(): far = lax.ppermute(far, 'rows', outward)  5.64 us
    pallas_call x3, Pallas kernels, finish(): pl.pallas_call(functools.partial(row_gram_kernel, side, first, angles_at)...  2.44 us
    pallas_call x1, Pallas kernels, local(): pl.pallas_call(edges_kernel, out_shape=[f32(columns + groups, vectors), f...  1.29 us
    pallas_call x1, Pallas kernels, local(): pl.pallas_call(functools.partial(angles_kernel, columns, head), out_shape...  1.13 us
  transfers between devices with their start and end apart: 7, of which 4 were waited for; matrix products, arithmetic and copies ran while one was open for 0% of the time, Pallas kernels for 22%

profile of v2, /device:TPU:0, one launch (start us, length us, event | category | flops | bytes accessed | tf_op | source)
XLA Modules:
  0.0 41.6 jit_solution(5290611093664990685)
XLA Ops:
  0.6 0.0 copy-start
  0.6 0.0 copy-start.1
  0.7 0.0 copy-start.3
  0.7 1.3 %edges.1 = (f32[1032,128]{1,0:T(8,128)S(1)}, f32[776,128]{1,0:T(8,128)S(1)}, f32[256,128]{1,0:T(8,128)S(1)}) custom-call(f32[2,4,1024,128]{3,2,1,0:T(8,128)} %tangent_ref.3, f32[4,1024]{1,0:T(4,128)} %positions_ref.9), custom_call_target="tpu_custom_call" | custom-call | tf_op jit(solution)/shard_map/edges/pallas_call | solution.py:321
  2.0 0.5 %collective-permute-start = (f32[1032,128]{1,0:T(8,128)S(1)}, f32[1032,128]{1,0:T(8,128)S(1)}, u32[]{:S(2)}, u32[]{:S(2)}) collective-permute-start(f32[1032,128]{1,0:T(8,128)S(1)} %get-tuple-element.20), channel_id=1, source_target_pairs={{0,1},{1,0},{2,3},{3,2},{4,5},{5,4},{6,7},{7,6},{8,9},{9,8},{10,11... | collective-permute-start | bytes 1585160 | tf_op jit(solution)/shard_map/ppermute | solution.py:336
  2.5 5.6 %collective-permute-start.1 = (f32[776,128]{1,0:T(8,128)S(1)}, f32[776,128]{1,0:T(8,128)S(1)}, u32[]{:S(2)}, u32[]{:S(2)}) collective-permute-start(f32[776,128]{1,0:T(8,128)S(1)} %get-tuple-element.21), channel_id=1, source_target_pairs={{0,15},{1,2},{2,1},{3,4},{4,3},{5,6},{6,5},{7,8},{8,7},{9,10},{10,... | collective-permute-start | bytes 1191944 | tf_op jit(solution)/shard_map/ppermute | solution.py:335
  8.1 0.0 collective-permute-start.2
  8.2 0.0 copy-done
  8.2 0.0 copy-done.1
  8.2 0.0 copy-done.3
  8.2 6.2 %inner.1 = (bf16[2,2,1024,256]{3,2,1,0:T(8,128)(2,1)S(1)}, f32[2,2,1024,128]{3,2,1,0:T(8,128)S(1)}, f32[128,128]{1,0:T(8,128)S(1)}) custom-call(f32[2,4,1024,128]{3,2,1,0:T(8,128)} %tangent_ref.3, f32[4,1024]{1,0:T(4,128)S(1)} %copy-done, f32[4,1024]{1,0:T(4,128)S(1)} %copy-done.3, f32[4,1024]{1,0:T(4,128)S(1)} %copy-done.1), custom_call_target="tpu_custom_call" | custom-call | flops 2000000000 | bytes 8388608 | tf_op jit(solution)/shard_map/inner/pallas_call | solution.py:339
  14.4 0.0 collective-permute-done.near_ref.angles_ref.halo_ref
  14.4 0.0 copy-start.2
  14.4 1.0 %near.1 = (bf16[2,1024,256]{2,1,0:T(8,128)(2,1)S(1)}, f32[128,128]{1,0:T(8,128)S(1)}) custom-call(f32[1032,128]{1,0:T(8,128)S(1)} %collective-permute-done.near_ref.angles_ref.halo_ref, f32[1032,128]{1,0:T(8,128)S(1)} %collective-permute-done.near_ref.angles_ref.halo_ref, f32[2,2,1024,128]{3,2,1,0:T(8,128)S(1)} %get-tuple-element.25.partial_ref, ...), custom_call_target="tpu_custom_call" | custom-call | flops 400000000 | bytes 2097152 | tf_op jit(solution)/shard_map/near/pallas_call | solution.py:362
  15.5 0.0 copy-start.4
  15.5 0.0 collective-permute-done.1.far_ref.angles_ref.halo_ref
  15.5 0.9 %far.1 = (bf16[2,768,256]{2,1,0:T(8,128)(2,1)S(1)}, f32[128,128]{1,0:T(8,128)S(1)}) custom-call(f32[776,128]{1,0:T(8,128)S(1)} %collective-permute-done.1.far_ref.angles_ref.halo_ref, f32[776,128]{1,0:T(8,128)S(1)} %collective-permute-done.1.far_ref.angles_ref.halo_ref, f32[2,2,1024,128]{3,2,1,0:T(8,128)S(1)} %get-tuple-element.25.partial_ref, ...), custom_call_target="tpu_custom_call" | custom-call | flops 400000000 | bytes 2097152 | tf_op jit(solution)/shard_map/far/pallas_call | solution.py:362
  16.4 0.0 collective-permute-done.2.halo_ref
  16.4 0.5 %tail.1 = (bf16[2,256,256]{2,1,0:T(8,128)(2,1)S(1)}, f32[128,128]{1,0:T(8,128)S(1)}) custom-call(f32[776,128]{1,0:T(8,128)S(1)} %collective-permute-done.1.far_ref.angles_ref.halo_ref, f32[256,128]{1,0:T(8,128)S(1)} %collective-permute-done.2.halo_ref, f32[2,2,1024,128]{3,2,1,0:T(8,128)S(1)} %get-tuple-element.25.partial_ref, f32[4,1024]{1,0:T(4,128)S(1)} %copy-done, ...), custom_call_target="tpu_custom_call" | custom-call | flops 400000000 | bytes 2097152 | tf_op jit(solution)/shard_map/tail/pallas_call | solution.py:362
  16.9 1.4 %collective-permute-start.3 = (f32[128,128]{1,0:T(8,128)S(1)}, f32[128,128]{1,0:T(8,128)S(1)}, u32[]{:S(2)}, u32[]{:S(2)}) collective-permute-start(f32[128,128]{1,0:T(8,128)S(1)} %get-tuple-element.29.left_ref), channel_id=1, source_target_pairs={{0,1},{1,0},{2,3},{3,2},{4,5},{5,4},{6,7},{7,6},{8,9},{9,8},{10,11... | collective-permute-start | bytes 196616 | tf_op jit(solution)/shard_map/ppermute | solution.py:302
  18.3 0.9 %collective-permute-done.3.right_ref = f32[128,128]{1,0:T(8,128)S(1)} collective-permute-done((f32[128,128]{1,0:T(8,128)S(1)}, f32[128,128]{1,0:T(8,128)S(1)}, u32[]{:S(2)}, u32[]{:S(2)}) %collective-permute-start.3) | collective-permute-done | bytes 65568 | tf_op jit(solution)/shard_map/ppermute | solution.py:302
  19.2 2.0 %collective-permute-start.4 = (f32[128,128]{1,0:T(8,128)S(1)}, f32[128,128]{1,0:T(8,128)S(1)}, u32[]{:S(2)}, u32[]{:S(2)}) collective-permute-start(f32[128,128]{1,0:T(8,128)S(1)} %gram_sum.3.left_ref), channel_id=1, source_target_pairs={{0,2},{1,3},{2,0},{3,1},{4,6},{5,7},{6,4},{7,5},{8,10},{9,11},{10,... | collective-permute-start | bytes 196616 | tf_op jit(solution)/shard_map/ppermute | solution.py:302
  21.3 2.4 %collective-permute-done.4.right_ref = f32[128,128]{1,0:T(8,128)S(1)} collective-permute-done((f32[128,128]{1,0:T(8,128)S(1)}, f32[128,128]{1,0:T(8,128)S(1)}, u32[]{:S(2)}, u32[]{:S(2)}) %collective-permute-start.4) | collective-permute-done | bytes 65568 | tf_op jit(solution)/shard_map/ppermute | solution.py:302
  23.7 2.2 %collective-permute-start.5 = (f32[128,128]{1,0:T(8,128)S(1)}, f32[128,128]{1,0:T(8,128)S(1)}, u32[]{:S(2)}, u32[]{:S(2)}) collective-permute-start(f32[128,128]{1,0:T(8,128)S(1)} %gram_sum.4.left_ref), channel_id=1, source_target_pairs={{0,4},{1,5},{2,6},{3,7},{4,0},{5,1},{6,2},{7,3},{8,12},{9,13},{10,... | collective-permute-start | bytes 196616 | tf_op jit(solution)/shard_map/ppermute | solution.py:302
  25.9 2.2 %collective-permute-done.5.right_ref = f32[128,128]{1,0:T(8,128)S(1)} collective-permute-done((f32[128,128]{1,0:T(8,128)S(1)}, f32[128,128]{1,0:T(8,128)S(1)}, u32[]{:S(2)}, u32[]{:S(2)}) %collective-permute-start.5) | collective-permute-done | bytes 65568 | tf_op jit(solution)/shard_map/ppermute | solution.py:302
  28.1 3.1 %collective-permute-start.6 = (f32[128,128]{1,0:T(8,128)S(1)}, f32[128,128]{1,0:T(8,128)S(1)}, u32[]{:S(2)}, u32[]{:S(2)}) collective-permute-start(f32[128,128]{1,0:T(8,128)S(1)} %gram_sum.5.gram_ref), channel_id=1, source_target_pairs={{0,8},{1,9},{2,10},{3,11},{4,12},{5,13},{6,14},{7,15},{8,0},{9,1},... | collective-permute-start | bytes 196616 | tf_op jit(solution)/shard_map/ppermute | solution.py:302
  31.2 0.0 copy-done.2
  31.2 1.1 %angles.1 = (f32[4,1024]{1,0:T(4,128)}, f32[4,1024]{1,0:T(4,128)}) custom-call(f32[1032,128]{1,0:T(8,128)S(1)} %collective-permute-done.near_ref.angles_ref.halo_ref, f32[776,128]{1,0:T(8,128)S(1)} %collective-permute-done.1.far_ref.angles_ref.halo_ref, f32[4,1024]{1,0:T(4,128)S(1)} %copy-done, f32[4,1024]{1,0:T(4,128)S(1)} %copy-done.2, ...), custom_call_target="tpu_custom_call" | custom-call | flops 1000000 | bytes 1000000 | tf_op jit(solution)/shard_map/angles/pallas_call | solution.py:394
  32.4 1.1 %collective-permute-done.6.other_ref = f32[128,128]{1,0:T(8,128)S(1)} collective-permute-done((f32[128,128]{1,0:T(8,128)S(1)}, f32[128,128]{1,0:T(8,128)S(1)}, u32[]{:S(2)}, u32[]{:S(2)}) %collective-permute-start.6) | collective-permute-done | bytes 65568 | tf_op jit(solution)/shard_map/ppermute | solution.py:302
  33.5 0.0 copy-done.4
  33.5 8.2 %ortho.1 = (f32[2,4,1024,128]{3,2,1,0:T(8,128)}, f32[1,128]{1,0:T(1,128)}) custom-call(f32[128,128]{1,0:T(8,128)S(1)} %gram_sum.5.gram_ref, f32[128,128]{1,0:T(8,128)S(1)} %collective-permute-done.6.other_ref, f32[1,128]{1,0:T(1,128)S(1)} %bitcast.2, bf16[2,2,1024,256]{3,2,1,0:T(8,128)(2,1)S(1)} %get-tuple-element.30.inner_ref, ...), custom_call_target="tpu_custom_call" | custom-call | tf_op jit(solution)/shard_map/ortho/pallas_call | solution.py:405
  (3 shorter events, 0.0 us)
Async XLA Ops:
  0.6 7.5 %copy-start = (f32[4,1024]{1,0:T(4,128)S(1)}, f32[4,1024]{1,0:T(4,128)}, u32[]{:S(2)}) copy-start(f32[4,1024]{1,0:T(4,128)} %positions_ref.9) | copy-start | bytes 49156
  0.6 7.5 %copy-start.1 = (f32[4,1024]{1,0:T(4,128)S(1)}, f32[4,1024]{1,0:T(4,128)}, u32[]{:S(2)}) copy-start(f32[4,1024]{1,0:T(4,128)} %coupling_ref.9) | copy-start | bytes 49156
  0.7 7.5 %copy-start.3 = (f32[4,1024]{1,0:T(4,128)S(1)}, f32[4,1024]{1,0:T(4,128)}, u32[]{:S(2)}) copy-start(f32[4,1024]{1,0:T(4,128)} %kick_ref.3) | copy-start | bytes 49156
  2.0 12.4 %collective-permute-start = (f32[1032,128]{1,0:T(8,128)S(1)}, f32[1032,128]{1,0:T(8,128)S(1)}, u32[]{:S(2)}, u32[]{:S(2)}) collective-permute-start(f32[1032,128]{1,0:T(8,128)S(1)} %get-tuple-element.20), channel_id=1, source_target_pairs={{0,1},{1,0},{2,3},{3,2},{4,5},{5,4},{6,7},{7,6},{8,9},{9,8},{10,11... | collective-permute-start | bytes 1585160 | tf_op jit(solution)/shard_map/ppermute | solution.py:336
  2.5 13.0 %collective-permute-start.1 = (f32[776,128]{1,0:T(8,128)S(1)}, f32[776,128]{1,0:T(8,128)S(1)}, u32[]{:S(2)}, u32[]{:S(2)}) collective-permute-start(f32[776,128]{1,0:T(8,128)S(1)} %get-tuple-element.21), channel_id=1, source_target_pairs={{0,15},{1,2},{2,1},{3,4},{4,3},{5,6},{6,5},{7,8},{8,7},{9,10},{10,... | collective-permute-start | bytes 1191944 | tf_op jit(solution)/shard_map/ppermute | solution.py:335
  8.1 8.2 %collective-permute-start.2 = (f32[256,128]{1,0:T(8,128)S(1)}, f32[256,128]{1,0:T(8,128)S(1)}, u32[]{:S(2)}, u32[]{:S(2)}) collective-permute-start(f32[256,128]{1,0:T(8,128)S(1)} %get-tuple-element.24), channel_id=1, source_target_pairs={{0,15},{1,2},{2,1},{3,4},{4,3},{5,6},{6,5},{7,8},{8,7},{9,10},{10,... | collective-permute-start | bytes 393224 | tf_op jit(solution)/shard_map/ppermute | solution.py:337
  14.4 16.8 %copy-start.2 = (f32[4,1024]{1,0:T(4,128)S(1)}, f32[4,1024]{1,0:T(4,128)}, u32[]{:S(2)}) copy-start(f32[4,1024]{1,0:T(4,128)} %momenta_ref.1) | copy-start | bytes 49156
  15.5 18.0 %copy-start.4 = (f32[128]{0:T(128)S(1)}, f32[128]{0:T(128)}, u32[]{:S(2)}) copy-start(f32[128]{0:T(128)} %param.11) | copy-start | bytes 1540
  16.9 2.3 %collective-permute-start.3 = (f32[128,128]{1,0:T(8,128)S(1)}, f32[128,128]{1,0:T(8,128)S(1)}, u32[]{:S(2)}, u32[]{:S(2)}) collective-permute-start(f32[128,128]{1,0:T(8,128)S(1)} %get-tuple-element.29.left_ref), channel_id=1, source_target_pairs={{0,1},{1,0},{2,3},{3,2},{4,5},{5,4},{6,7},{7,6},{8,9},{9,8},{10,11... | collective-permute-start | bytes 196616 | tf_op jit(solution)/shard_map/ppermute | solution.py:302
  19.2 4.5 %collective-permute-start.4 = (f32[128,128]{1,0:T(8,128)S(1)}, f32[128,128]{1,0:T(8,128)S(1)}, u32[]{:S(2)}, u32[]{:S(2)}) collective-permute-start(f32[128,128]{1,0:T(8,128)S(1)} %gram_sum.3.left_ref), channel_id=1, source_target_pairs={{0,2},{1,3},{2,0},{3,1},{4,6},{5,7},{6,4},{7,5},{8,10},{9,11},{10,... | collective-permute-start | bytes 196616 | tf_op jit(solution)/shard_map/ppermute | solution.py:302
  23.7 4.4 %collective-permute-start.5 = (f32[128,128]{1,0:T(8,128)S(1)}, f32[128,128]{1,0:T(8,128)S(1)}, u32[]{:S(2)}, u32[]{:S(2)}) collective-permute-start(f32[128,128]{1,0:T(8,128)S(1)} %gram_sum.4.left_ref), channel_id=1, source_target_pairs={{0,4},{1,5},{2,6},{3,7},{4,0},{5,1},{6,2},{7,3},{8,12},{9,13},{10,... | collective-permute-start | bytes 196616 | tf_op jit(solution)/shard_map/ppermute | solution.py:302
  28.1 5.3 %collective-permute-start.6 = (f32[128,128]{1,0:T(8,128)S(1)}, f32[128,128]{1,0:T(8,128)S(1)}, u32[]{:S(2)}, u32[]{:S(2)}) collective-permute-start(f32[128,128]{1,0:T(8,128)S(1)} %gram_sum.5.gram_ref), channel_id=1, source_target_pairs={{0,8},{1,9},{2,10},{3,11},{4,12},{5,13},{6,14},{7,15},{8,0},{9,1},... | collective-permute-start | bytes 196616 | tf_op jit(solution)/shard_map/ppermute | solution.py:302

commit v3 on v2

--- a/solution.py
+++ b/solution.py
@@ -194,7 +194,14 @@
     new_positions_ref[...] = x + momenta
 
 
-def inverse_factor(gram, inverse_ref):
+def three(value):
+    first = value.astype(jnp.bfloat16).astype(jnp.float32)
+    rest = value - first
+    second = rest.astype(jnp.bfloat16).astype(jnp.float32)
+    return first, second, (rest - second).astype(jnp.bfloat16).astype(jnp.float32)
+
+
+def inverse_factor(gram, scale, weights_ref):
     order = gram.shape[0]
     step = 8
     lane = lax.broadcasted_iota(jnp.int32, (step, order), 1)
@@ -202,10 +209,12 @@
     spread = lambda value: jnp.broadcast_to(value, (step, order))
     work = [gram[at : at + step, :] for at in range(0, order, step)]
     squares = jnp.ones((step, order), jnp.float32)
+    inverse = []
     for block in range(order // step):
         first = block * step
         own = work[block]
-        columns = [spread(own[:, first + a : first + a + 1]) for a in range(step)]
+        if block == 0:
+            columns = [spread(own[:, first + a : first + a + 1]) for a in range(step)]
         pivot = [
             [spread(columns[a][i : i + 1, :]) if i >= a else None for a in range(step)]
             for i in range(step)
@@ -215,6 +224,14 @@
         solved = [spread(extended[a : a + 1, :]) for a in range(step)]
         recip = [None] * step
         lower = [[None] * step for _ in range(step)]
+        ahead = None
+        if block + 1 < order // step:
+            ahead = work[block + 1]
+            ahead_columns = [spread(ahead[:, first + a : first + a + 1]) for a in range(step)]
+            coming = [
+                spread(ahead[:, first + step + b : first + step + b + 1]) for b in range(step)
+            ]
+            ahead = jnp.where(inside, 0.0, ahead)
         for a in range(step):
             recip[a] = 1.0 / pivot[a][a]
             for i in range(a + 1, step):
@@ -222,46 +239,73 @@
             for b in range(a + 1, step):
                 for i in range(b, step):
                     pivot[i][b] = pivot[i][b] - lower[i][a] * pivot[b][a]
-        for a in range(step):
             for i in range(a + 1, step):
                 solved[i] = solved[i] - lower[i][a] * solved[a]
+            if ahead is not None:
+                factor = ahead_columns[a] * recip[a]
+                ahead = ahead - factor * solved[a]
+                for b in range(step):
+                    coming[b] = coming[b] - factor * spread(ahead_columns[a][b : b + 1, :])
+                for b in range(a + 1, step):
+                    ahead_columns[b] = ahead_columns[b] - factor * pivot[b][a]
+        if ahead is not None:
+            work[block + 1], columns = ahead, coming
         scaled = [solved[a] * recip[a] for a in range(step)]
         for a in range(step - 1, 0, -1):
             for i in range(a):
                 scaled[i] = scaled[i] - lower[a][i] * scaled[a]
-        for later in range(block + 1, order // step):
+        reach = min(block + 3, order // step)
+        for later in range(block + 2, reach):
             rest = work[later]
             t = [spread(rest[:, first + a : first + a + 1]) * scaled[a] for a in range(step)]
             while len(t) > 1:
                 t = [t[i] + t[i + 1] for i in range(0, len(t), 2)]
             work[later] = jnp.where(inside, 0.0, rest) - t[0]
+        if reach < order // step:
+            rows_y, rows_s = solved[0], solved[0] * recip[0]
+            for a in range(1, step):
+                rows_y = jnp.where(sub == a, solved[a], rows_y)
+                rows_s = jnp.where(sub == a, solved[a] * recip[a], rows_s)
+            y1, y2, y3 = three(rows_y)
+            s1, s2, s3 = three(rows_s)
+            left = jnp.concatenate([y1, y1, y2, y1, y3, y2], axis=0).astype(jnp.bfloat16)
+            right = jnp.concatenate([s1, s2, s1, s3, s1, s2], axis=0).astype(jnp.bfloat16)
+            update = lax.dot_general(
+                left, right, (((0,), (0,)), ((), ())), preferred_element_type=jnp.float32
+            )
+            for later in range(reach, order // step):
+                work[later] = jnp.where(inside, 0.0, work[later]) - update[
+                    later * step : (later + 1) * step, :
+                ]
         rows_out, diagonal = solved[0], pivot[0][0]
         for a in range(step):
             rows_out = jnp.where(sub == a, solved[a], rows_out)
             diagonal = jnp.where(sub == a, pivot[a][a], diagonal)
             squares = jnp.where(lane == first + a, pivot[a][a], squares)
-        inverse_ref[first : first + step, :] = jnp.where(
-            lane <= first + sub, rows_out * lax.rsqrt(diagonal), 0.0
-        )
+        inverse.append(jnp.where(
+            lane <= first + sub, rows_out * (scale * lax.rsqrt(diagonal)), 0.0
+        ))
+        if block % 2:
+            factor = split_pair(jnp.concatenate(inverse[-2:], axis=0))
+            high, low = factor[:, :order], factor[:, order:]
+            at = first - step
+            weights_ref[at : at + 2 * step, :] = jnp.concatenate([high, high], axis=1)
+            weights_ref[order + at : order + at + 2 * step, :] = jnp.concatenate([low, low], axis=1)
     return squares
 
 
 def ortho_kernel(
     sites_total, gram_ref, other_ref, log_growth_ref, inner_ref, near_ref, far_ref, tail_ref,
     out_ref, growth_ref,
-    inverse_ref, out_buf, out_sems,
+    weights_ref, out_buf, out_sems,
 ):
     rows, columns = out_ref.shape[1], out_ref.shape[2]
     head = far_ref.shape[1]
-    squares = inverse_factor(gram_ref[...] + other_ref[...], inverse_ref)
+    squares = inverse_factor(gram_ref[...] + other_ref[...], math.sqrt(sites_total), weights_ref)
     growth_ref[...] = (
         log_growth_ref[...] + 0.5 * jnp.log(squares[:1]) - 0.5 * math.log(sites_total)
     )
-    factor = split_pair(inverse_ref[...] * math.sqrt(sites_total))
-    high, low = factor[:, :LANES], factor[:, LANES:]
-    weights = jnp.concatenate(
-        [jnp.concatenate([high, high], axis=1), jnp.concatenate([low, low], axis=1)], axis=0
-    )
+    weights = weights_ref[...]
 
     def product(pairs):
         both = lax.dot_general(
@@ -270,6 +314,7 @@
         return both[:, :LANES] + both[:, LANES:]
 
     stores = []
+    piece = columns - head
 
     def send(part, slot, row):
         store = pltpu.make_async_copy(
@@ -280,11 +325,14 @@
 
     for part in range(2):
         for r in range(rows - 2):
-            out_buf[part, r] = product(inner_ref[part, r])
+            for at in range(0, columns, piece):
+                out_buf[part, r, at : at + piece] = product(inner_ref[part, r, at : at + piece])
             send(part, r, r + 1)
-        out_buf[part, rows - 2] = product(near_ref[part])
+        for at in range(0, columns, piece):
+            out_buf[part, rows - 2, at : at + piece] = product(near_ref[part, at : at + piece])
         send(part, rows - 2, side_slot(0) * (rows - 1))
-        out_buf[part, rows - 1, :head] = product(far_ref[part])
+        for at in range(0, head, piece):
+            out_buf[part, rows - 1, at : at + piece] = product(far_ref[part, at : at + piece])
         out_buf[part, rows - 1, head:] = product(tail_ref[part])
         send(part, rows - 1, side_slot(1) * (rows - 1))
     for store in stores:
@@ -411,7 +459,7 @@
         in_specs=[resident] * 7,
         out_specs=[in_hbm, resident],
         scratch_shapes=[
-            pltpu.VMEM((vectors, vectors), jnp.float32),
+            pltpu.VMEM((2 * vectors, 2 * vectors), jnp.bfloat16),
             pltpu.VMEM((2, rows, columns, vectors), jnp.float32),
             pltpu.SemaphoreType.DMA((2, rows)),
         ],

time: 41.8 us -> 39.3 us (0.940)
  Pallas kernels: 19.3 us -> 16.8 us
    pallas_call x1, Pallas kernels: 8.16 us -> 5.64 us  [local(): pl.pallas_call(functools.partial(ortho_kernel, sites_total), out_shape=[p...]
  transfers between devices with their start and end apart: 7 -> 7, of which waited for: 4 -> 4; matrix products, arithmetic and copies ran while one was open for 0% -> 0% of each run, Pallas kernels for 22% -> 24%
where the time goes in v3:
time: 39.3 us; the launch traced here: 39.1 us
  Pallas kernels  16.8 us (43%)
  starting transfers between devices  14.9 us (38%)
  waiting for transfers between devices  6.68 us (17%)
  between operations  0.75 us (2%)
    ppermute x4, starting transfers between devices, sum_over_rows(): other = lax.ppermute(value, 'rows', [(i, i ^ bit) for i in range(devices)])  8.72 us
    ppermute x4, waiting for transfers between devices, sum_over_rows(): other = lax.ppermute(value, 'rows', [(i, i ^ bit) for i in range(devices)])  6.68 us
    pallas_call x1, Pallas kernels, local(): pl.pallas_call(inner_kernel, out_shape=[bf16(2, rows - 2, columns, 2 * ve...  6.23 us
    pallas_call x1, Pallas kernels, local(): pl.pallas_call(functools.partial(ortho_kernel, sites_total), out_shape=[p...  5.64 us
    ppermute x1, starting transfers between devices, local(): far = lax.ppermute(far, 'rows', outward)  5.64 us
    pallas_call x3, Pallas kernels, finish(): pl.pallas_call(functools.partial(row_gram_kernel, side, first, angles_at)...  2.44 us
    pallas_call x1, Pallas kernels, local(): pl.pallas_call(edges_kernel, out_shape=[f32(columns + groups, vectors), f...  1.29 us
    pallas_call x1, Pallas kernels, local(): pl.pallas_call(functools.partial(angles_kernel, columns, head), out_shape...  1.13 us
  transfers between devices with their start and end apart: 7, of which 4 were waited for; matrix products, arithmetic and copies ran while one was open for 0% of the time, Pallas kernels for 24%

profile of v3, /device:TPU:0, one launch (start us, length us, event | category | flops | bytes accessed | tf_op | source)
XLA Modules:
  0.0 39.1 jit_solution(7363900921713495798)
XLA Ops:
  0.6 0.0 copy-start
  0.6 0.0 copy-start.1
  0.7 0.0 copy-start.3
  0.7 1.3 %edges.1 = (f32[1032,128]{1,0:T(8,128)S(1)}, f32[776,128]{1,0:T(8,128)S(1)}, f32[256,128]{1,0:T(8,128)S(1)}) custom-call(f32[2,4,1024,128]{3,2,1,0:T(8,128)} %tangent_ref.3, f32[4,1024]{1,0:T(4,128)} %positions_ref.9), custom_call_target="tpu_custom_call" | custom-call | tf_op jit(solution)/shard_map/edges/pallas_call | solution.py:369
  2.0 0.5 %collective-permute-start = (f32[1032,128]{1,0:T(8,128)S(1)}, f32[1032,128]{1,0:T(8,128)S(1)}, u32[]{:S(2)}, u32[]{:S(2)}) collective-permute-start(f32[1032,128]{1,0:T(8,128)S(1)} %get-tuple-element.20), channel_id=1, source_target_pairs={{0,1},{1,0},{2,3},{3,2},{4,5},{5,4},{6,7},{7,6},{8,9},{9,8},{10,11... | collective-permute-start | bytes 1585160 | tf_op jit(solution)/shard_map/ppermute | solution.py:384
  2.5 5.6 %collective-permute-start.1 = (f32[776,128]{1,0:T(8,128)S(1)}, f32[776,128]{1,0:T(8,128)S(1)}, u32[]{:S(2)}, u32[]{:S(2)}) collective-permute-start(f32[776,128]{1,0:T(8,128)S(1)} %get-tuple-element.21), channel_id=1, source_target_pairs={{0,15},{1,2},{2,1},{3,4},{4,3},{5,6},{6,5},{7,8},{8,7},{9,10},{10,... | collective-permute-start | bytes 1191944 | tf_op jit(solution)/shard_map/ppermute | solution.py:383
  8.1 0.0 collective-permute-start.2
  8.2 0.0 copy-done
  8.2 0.0 copy-done.1
  8.2 0.0 copy-done.3
  8.2 6.2 %inner.1 = (bf16[2,2,1024,256]{3,2,1,0:T(8,128)(2,1)S(1)}, f32[2,2,1024,128]{3,2,1,0:T(8,128)S(1)}, f32[128,128]{1,0:T(8,128)S(1)}) custom-call(f32[2,4,1024,128]{3,2,1,0:T(8,128)} %tangent_ref.3, f32[4,1024]{1,0:T(4,128)S(1)} %copy-done, f32[4,1024]{1,0:T(4,128)S(1)} %copy-done.3, f32[4,1024]{1,0:T(4,128)S(1)} %copy-done.1), custom_call_target="tpu_custom_call" | custom-call | flops 2000000000 | bytes 8388608 | tf_op jit(solution)/shard_map/inner/pallas_call | solution.py:387
  14.4 0.0 collective-permute-done.near_ref.angles_ref.halo_ref
  14.4 0.0 copy-start.2
  14.4 1.0 %near.1 = (bf16[2,1024,256]{2,1,0:T(8,128)(2,1)S(1)}, f32[128,128]{1,0:T(8,128)S(1)}) custom-call(f32[1032,128]{1,0:T(8,128)S(1)} %collective-permute-done.near_ref.angles_ref.halo_ref, f32[1032,128]{1,0:T(8,128)S(1)} %collective-permute-done.near_ref.angles_ref.halo_ref, f32[2,2,1024,128]{3,2,1,0:T(8,128)S(1)} %get-tuple-element.25.partial_ref, ...), custom_call_target="tpu_custom_call" | custom-call | flops 400000000 | bytes 2097152 | tf_op jit(solution)/shard_map/near/pallas_call | solution.py:410
  15.5 0.0 copy-start.4
  15.5 0.0 collective-permute-done.1.far_ref.angles_ref.halo_ref
  15.5 0.9 %far.1 = (bf16[2,768,256]{2,1,0:T(8,128)(2,1)S(1)}, f32[128,128]{1,0:T(8,128)S(1)}) custom-call(f32[776,128]{1,0:T(8,128)S(1)} %collective-permute-done.1.far_ref.angles_ref.halo_ref, f32[776,128]{1,0:T(8,128)S(1)} %collective-permute-done.1.far_ref.angles_ref.halo_ref, f32[2,2,1024,128]{3,2,1,0:T(8,128)S(1)} %get-tuple-element.25.partial_ref, ...), custom_call_target="tpu_custom_call" | custom-call | flops 400000000 | bytes 2097152 | tf_op jit(solution)/shard_map/far/pallas_call | solution.py:410
  16.4 0.0 collective-permute-done.2.halo_ref
  16.4 0.5 %tail.1 = (bf16[2,256,256]{2,1,0:T(8,128)(2,1)S(1)}, f32[128,128]{1,0:T(8,128)S(1)}) custom-call(f32[776,128]{1,0:T(8,128)S(1)} %collective-permute-done.1.far_ref.angles_ref.halo_ref, f32[256,128]{1,0:T(8,128)S(1)} %collective-permute-done.2.halo_ref, f32[2,2,1024,128]{3,2,1,0:T(8,128)S(1)} %get-tuple-element.25.partial_ref, f32[4,1024]{1,0:T(4,128)S(1)} %copy-done, ...), custom_call_target="tpu_custom_call" | custom-call | flops 400000000 | bytes 2097152 | tf_op jit(solution)/shard_map/tail/pallas_call | solution.py:410
  16.9 1.4 %collective-permute-start.3 = (f32[128,128]{1,0:T(8,128)S(1)}, f32[128,128]{1,0:T(8,128)S(1)}, u32[]{:S(2)}, u32[]{:S(2)}) collective-permute-start(f32[128,128]{1,0:T(8,128)S(1)} %get-tuple-element.29.left_ref), channel_id=1, source_target_pairs={{0,1},{1,0},{2,3},{3,2},{4,5},{5,4},{6,7},{7,6},{8,9},{9,8},{10,11... | collective-permute-start | bytes 196616 | tf_op jit(solution)/shard_map/ppermute | solution.py:350
  18.3 0.9 %collective-permute-done.3.right_ref = f32[128,128]{1,0:T(8,128)S(1)} collective-permute-done((f32[128,128]{1,0:T(8,128)S(1)}, f32[128,128]{1,0:T(8,128)S(1)}, u32[]{:S(2)}, u32[]{:S(2)}) %collective-permute-start.3) | collective-permute-done | bytes 65568 | tf_op jit(solution)/shard_map/ppermute | solution.py:350
  19.2 2.0 %collective-permute-start.4 = (f32[128,128]{1,0:T(8,128)S(1)}, f32[128,128]{1,0:T(8,128)S(1)}, u32[]{:S(2)}, u32[]{:S(2)}) collective-permute-start(f32[128,128]{1,0:T(8,128)S(1)} %gram_sum.3.left_ref), channel_id=1, source_target_pairs={{0,2},{1,3},{2,0},{3,1},{4,6},{5,7},{6,4},{7,5},{8,10},{9,11},{10,... | collective-permute-start | bytes 196616 | tf_op jit(solution)/shard_map/ppermute | solution.py:350
  21.3 2.4 %collective-permute-done.4.right_ref = f32[128,128]{1,0:T(8,128)S(1)} collective-permute-done((f32[128,128]{1,0:T(8,128)S(1)}, f32[128,128]{1,0:T(8,128)S(1)}, u32[]{:S(2)}, u32[]{:S(2)}) %collective-permute-start.4) | collective-permute-done | bytes 65568 | tf_op jit(solution)/shard_map/ppermute | solution.py:350
  23.7 2.2 %collective-permute-start.5 = (f32[128,128]{1,0:T(8,128)S(1)}, f32[128,128]{1,0:T(8,128)S(1)}, u32[]{:S(2)}, u32[]{:S(2)}) collective-permute-start(f32[128,128]{1,0:T(8,128)S(1)} %gram_sum.4.left_ref), channel_id=1, source_target_pairs={{0,4},{1,5},{2,6},{3,7},{4,0},{5,1},{6,2},{7,3},{8,12},{9,13},{10,... | collective-permute-start | bytes 196616 | tf_op jit(solution)/shard_map/ppermute | solution.py:350
  25.9 2.2 %collective-permute-done.5.right_ref = f32[128,128]{1,0:T(8,128)S(1)} collective-permute-done((f32[128,128]{1,0:T(8,128)S(1)}, f32[128,128]{1,0:T(8,128)S(1)}, u32[]{:S(2)}, u32[]{:S(2)}) %collective-permute-start.5) | collective-permute-done | bytes 65568 | tf_op jit(solution)/shard_map/ppermute | solution.py:350
  28.1 3.1 %collective-permute-start.6 = (f32[128,128]{1,0:T(8,128)S(1)}, f32[128,128]{1,0:T(8,128)S(1)}, u32[]{:S(2)}, u32[]{:S(2)}) collective-permute-start(f32[128,128]{1,0:T(8,128)S(1)} %gram_sum.5.gram_ref), channel_id=1, source_target_pairs={{0,8},{1,9},{2,10},{3,11},{4,12},{5,13},{6,14},{7,15},{8,0},{9,1},... | collective-permute-start | bytes 196616 | tf_op jit(solution)/shard_map/ppermute | solution.py:350
  31.2 0.0 copy-done.2
  31.2 1.1 %angles.1 = (f32[4,1024]{1,0:T(4,128)}, f32[4,1024]{1,0:T(4,128)}) custom-call(f32[1032,128]{1,0:T(8,128)S(1)} %collective-permute-done.near_ref.angles_ref.halo_ref, f32[776,128]{1,0:T(8,128)S(1)} %collective-permute-done.1.far_ref.angles_ref.halo_ref, f32[4,1024]{1,0:T(4,128)S(1)} %copy-done, f32[4,1024]{1,0:T(4,128)S(1)} %copy-done.2, ...), custom_call_target="tpu_custom_call" | custom-call | flops 1000000 | bytes 1000000 | tf_op jit(solution)/shard_map/angles/pallas_call | solution.py:442
  32.4 1.1 %collective-permute-done.6.other_ref = f32[128,128]{1,0:T(8,128)S(1)} collective-permute-done((f32[128,128]{1,0:T(8,128)S(1)}, f32[128,128]{1,0:T(8,128)S(1)}, u32[]{:S(2)}, u32[]{:S(2)}) %collective-permute-start.6) | collective-permute-done | bytes 65568 | tf_op jit(solution)/shard_map/ppermute | solution.py:350
  33.5 0.0 copy-done.4
  33.5 5.6 %ortho.1 = (f32[2,4,1024,128]{3,2,1,0:T(8,128)}, f32[1,128]{1,0:T(1,128)}) custom-call(f32[128,128]{1,0:T(8,128)S(1)} %gram_sum.5.gram_ref, f32[128,128]{1,0:T(8,128)S(1)} %collective-permute-done.6.other_ref, f32[1,128]{1,0:T(1,128)S(1)} %bitcast.2, bf16[2,2,1024,256]{3,2,1,0:T(8,128)(2,1)S(1)} %get-tuple-element.30.inner_ref, ...), custom_call_target="tpu_custom_call" | custom-call | tf_op jit(solution)/shard_map/ortho/pallas_call | solution.py:453
  (3 shorter events, 0.0 us)
Async XLA Ops:
  0.6 7.5 %copy-start = (f32[4,1024]{1,0:T(4,128)S(1)}, f32[4,1024]{1,0:T(4,128)}, u32[]{:S(2)}) copy-start(f32[4,1024]{1,0:T(4,128)} %positions_ref.9) | copy-start | bytes 49156
  0.6 7.5 %copy-start.1 = (f32[4,1024]{1,0:T(4,128)S(1)}, f32[4,1024]{1,0:T(4,128)}, u32[]{:S(2)}) copy-start(f32[4,1024]{1,0:T(4,128)} %coupling_ref.9) | copy-start | bytes 49156
  0.7 7.5 %copy-start.3 = (f32[4,1024]{1,0:T(4,128)S(1)}, f32[4,1024]{1,0:T(4,128)}, u32[]{:S(2)}) copy-start(f32[4,1024]{1,0:T(4,128)} %kick_ref.3) | copy-start | bytes 49156
  2.0 12.4 %collective-permute-start = (f32[1032,128]{1,0:T(8,128)S(1)}, f32[1032,128]{1,0:T(8,128)S(1)}, u32[]{:S(2)}, u32[]{:S(2)}) collective-permute-start(f32[1032,128]{1,0:T(8,128)S(1)} %get-tuple-element.20), channel_id=1, source_target_pairs={{0,1},{1,0},{2,3},{3,2},{4,5},{5,4},{6,7},{7,6},{8,9},{9,8},{10,11... | collective-permute-start | bytes 1585160 | tf_op jit(solution)/shard_map/ppermute | solution.py:384
  2.5 13.0 %collective-permute-start.1 = (f32[776,128]{1,0:T(8,128)S(1)}, f32[776,128]{1,0:T(8,128)S(1)}, u32[]{:S(2)}, u32[]{:S(2)}) collective-permute-start(f32[776,128]{1,0:T(8,128)S(1)} %get-tuple-element.21), channel_id=1, source_target_pairs={{0,15},{1,2},{2,1},{3,4},{4,3},{5,6},{6,5},{7,8},{8,7},{9,10},{10,... | collective-permute-start | bytes 1191944 | tf_op jit(solution)/shard_map/ppermute | solution.py:383
  8.1 8.2 %collective-permute-start.2 = (f32[256,128]{1,0:T(8,128)S(1)}, f32[256,128]{1,0:T(8,128)S(1)}, u32[]{:S(2)}, u32[]{:S(2)}) collective-permute-start(f32[256,128]{1,0:T(8,128)S(1)} %get-tuple-element.24), channel_id=1, source_target_pairs={{0,15},{1,2},{2,1},{3,4},{4,3},{5,6},{6,5},{7,8},{8,7},{9,10},{10,... | collective-permute-start | bytes 393224 | tf_op jit(solution)/shard_map/ppermute | solution.py:385
  14.4 16.8 %copy-start.2 = (f32[4,1024]{1,0:T(4,128)S(1)}, f32[4,1024]{1,0:T(4,128)}, u32[]{:S(2)}) copy-start(f32[4,1024]{1,0:T(4,128)} %momenta_ref.1) | copy-start | bytes 49156
  15.5 18.0 %copy-start.4 = (f32[128]{0:T(128)S(1)}, f32[128]{0:T(128)}, u32[]{:S(2)}) copy-start(f32[128]{0:T(128)} %param.11) | copy-start | bytes 1540
  16.9 2.3 %collective-permute-start.3 = (f32[128,128]{1,0:T(8,128)S(1)}, f32[128,128]{1,0:T(8,128)S(1)}, u32[]{:S(2)}, u32[]{:S(2)}) collective-permute-start(f32[128,128]{1,0:T(8,128)S(1)} %get-tuple-element.29.left_ref), channel_id=1, source_target_pairs={{0,1},{1,0},{2,3},{3,2},{4,5},{5,4},{6,7},{7,6},{8,9},{9,8},{10,11... | collective-permute-start | bytes 196616 | tf_op jit(solution)/shard_map/ppermute | solution.py:350
  19.2 4.5 %collective-permute-start.4 = (f32[128,128]{1,0:T(8,128)S(1)}, f32[128,128]{1,0:T(8,128)S(1)}, u32[]{:S(2)}, u32[]{:S(2)}) collective-permute-start(f32[128,128]{1,0:T(8,128)S(1)} %gram_sum.3.left_ref), channel_id=1, source_target_pairs={{0,2},{1,3},{2,0},{3,1},{4,6},{5,7},{6,4},{7,5},{8,10},{9,11},{10,... | collective-permute-start | bytes 196616 | tf_op jit(solution)/shard_map/ppermute | solution.py:350
  23.7 4.4 %collective-permute-start.5 = (f32[128,128]{1,0:T(8,128)S(1)}, f32[128,128]{1,0:T(8,128)S(1)}, u32[]{:S(2)}, u32[]{:S(2)}) collective-permute-start(f32[128,128]{1,0:T(8,128)S(1)} %gram_sum.4.left_ref), channel_id=1, source_target_pairs={{0,4},{1,5},{2,6},{3,7},{4,0},{5,1},{6,2},{7,3},{8,12},{9,13},{10,... | collective-permute-start | bytes 196616 | tf_op jit(solution)/shard_map/ppermute | solution.py:350
  28.1 5.3 %collective-permute-start.6 = (f32[128,128]{1,0:T(8,128)S(1)}, f32[128,128]{1,0:T(8,128)S(1)}, u32[]{:S(2)}, u32[]{:S(2)}) collective-permute-start(f32[128,128]{1,0:T(8,128)S(1)} %gram_sum.5.gram_ref), channel_id=1, source_target_pairs={{0,8},{1,9},{2,10},{3,11},{4,12},{5,13},{6,14},{7,15},{8,0},{9,1},... | collective-permute-start | bytes 196616 | tf_op jit(solution)/shard_map/ppermute | solution.py:350

commit v4 on v3

--- a/solution.py
+++ b/solution.py
@@ -169,8 +169,17 @@
     gram_ref[...] = before_ref[...] + fold_pairs(gram)
 
 
-def add_kernel(left_ref, right_ref, out_ref):
-    out_ref[...] = left_ref[...] + right_ref[...]
+def pairwise(terms):
+    while len(terms) > 1:
+        terms = [
+            terms[i] + terms[i + 1] if i + 1 < len(terms) else terms[i]
+            for i in range(0, len(terms), 2)
+        ]
+    return terms[0]
+
+
+def add_kernel(*refs):
+    refs[-1][...] = pairwise([ref[...] for ref in refs[:-1]])
 
 
 def angles_kernel(
@@ -342,14 +351,24 @@
 def sum_over_rows(value, summed):
     devices = lax.axis_size("rows")
     if devices & (devices - 1):
-        return lax.psum(value, "rows"), jnp.zeros_like(value)
-    bit, other = 1, None
-    while bit < devices:
-        if other is not None:
-            value = summed(value, other)
-        other = lax.ppermute(value, "rows", [(i, i ^ bit) for i in range(devices)])
-        bit *= 2
-    return value, other
+        return [lax.psum(value, "rows"), jnp.zeros_like(value)]
+    bits = [1 << k for k in range(devices.bit_length() - 1)]
+    stages = [bits[:1]]
+    if len(bits) > 2:
+        stages.append([bits[1], bits[2], bits[1] + bits[2]])
+        bits = bits[3:]
+    else:
+        bits = bits[1:]
+    stages.extend([bit] for bit in bits)
+    terms = [value]
+    for stage in stages:
+        if len(terms) > 1:
+            terms = [summed(terms)]
+        terms.extend([
+            lax.ppermute(terms[0], "rows", [(i, i ^ offset) for i in range(devices)])
+            for offset in stage
+        ])
+    return terms
 
 
 def local(positions, momenta, kick_strength, coupling, tangent, log_growth):
@@ -427,17 +446,20 @@
     far_pairs, gram = finish("far", 1, 0, head, head, far, far, gram)
     tail_pairs, gram = finish("tail", 1, head, tail_sites, head, far, tail, gram)
 
-    def summed(left, right):
+    def summed(terms):
         return pl.pallas_call(
             add_kernel,
             out_shape=f32(vectors, vectors),
-            in_specs=[resident] * 2,
+            in_specs=[resident] * len(terms),
             out_specs=resident,
             compiler_params=pltpu.CompilerParams(vmem_limit_bytes=1 * MIB),
             name="gram_sum",
-        )(near_core(left), near_core(right))
-
-    gram, gram_other = sum_over_rows(gram, summed)
+        )(*[near_core(term) for term in terms])
+
+    terms = sum_over_rows(gram, summed)
+    if len(terms) > 2:
+        terms = [summed(terms), jnp.zeros_like(gram)]
+    gram, gram_other = terms
 
     new_positions, new_momenta = pl.pallas_call(
         functools.partial(angles_kernel, columns, head),

time: 39.3 us -> 38.1 us (0.969)
  starting transfers between devices: 14.9 us -> 14 us
    ppermute x4 -> x5, starting transfers between devices: 8.72 us -> 7.76 us  [sum_over_rows(): lax.ppermute(terms[0], 'rows', [(i, i ^ offset) for i in range(devices)])]
    ppermute x4 -> x5, waiting for transfers between devices: 6.68 us -> 6.42 us  [sum_over_rows(): lax.ppermute(terms[0], 'rows', [(i, i ^ offset) for i in range(devices)])]
  transfers between devices with their start and end apart: 7 -> 8, of which waited for: 4 -> 5; matrix products, arithmetic and copies ran while one was open for 0% -> 0% of each run, Pallas kernels for 24% -> 24%
where the time goes in v4:
time: 38.1 us; the launch traced here: 37.9 us
  Pallas kernels  16.8 us (44%)
  starting transfers between devices  14 us (37%)
  waiting for transfers between devices  6.42 us (17%)
  between operations  0.74 us (2%)
    ppermute x5, starting transfers between devices, sum_over_rows(): lax.ppermute(terms[0], 'rows', [(i, i ^ offset) for i in range(devices)])  7.76 us
    ppermute x5, waiting for transfers between devices, sum_over_rows(): lax.ppermute(terms[0], 'rows', [(i, i ^ offset) for i in range(devices)])  6.42 us
    pallas_call x1, Pallas kernels, local(): pl.pallas_call(inner_kernel, out_shape=[bf16(2, rows - 2, columns, 2 * ve...  6.23 us
    pallas_call x1, Pallas kernels, local(): pl.pallas_call(functools.partial(ortho_kernel, sites_total), out_shape=[p...  5.64 us
    ppermute x1, starting transfers between devices, local(): far = lax.ppermute(far, 'rows', outward)  5.64 us
    pallas_call x3, Pallas kernels, finish(): pl.pallas_call(functools.partial(row_gram_kernel, side, first, angles_at)...  2.44 us
    pallas_call x1, Pallas kernels, local(): pl.pallas_call(edges_kernel, out_shape=[f32(columns + groups, vectors), f...  1.29 us
    pallas_call x1, Pallas kernels, local(): pl.pallas_call(functools.partial(angles_kernel, columns, head), out_shape...  1.13 us
  transfers between devices with their start and end apart: 8, of which 5 were waited for; matrix products, arithmetic and copies ran while one was open for 0% of the time, Pallas kernels for 24%

profile of v4, /device:TPU:0, one launch (start us, length us, event | category | flops | bytes accessed | tf_op | source)
XLA Modules:
  0.0 37.9 jit_solution(1165627904719314235)
XLA Ops:
  0.6 0.0 copy-start
  0.6 0.0 copy-start.1
  0.7 0.0 copy-start.3
  0.7 1.3 %edges.1 = (f32[1032,128]{1,0:T(8,128)S(1)}, f32[776,128]{1,0:T(8,128)S(1)}, f32[256,128]{1,0:T(8,128)S(1)}) custom-call(f32[2,4,1024,128]{3,2,1,0:T(8,128)} %tangent_ref.3, f32[4,1024]{1,0:T(4,128)} %positions_ref.9), custom_call_target="tpu_custom_call" | custom-call | tf_op jit(solution)/shard_map/edges/pallas_call | solution.py:388
  2.0 0.5 %collective-permute-start = (f32[1032,128]{1,0:T(8,128)S(1)}, f32[1032,128]{1,0:T(8,128)S(1)}, u32[]{:S(2)}, u32[]{:S(2)}) collective-permute-start(f32[1032,128]{1,0:T(8,128)S(1)} %get-tuple-element.20), channel_id=1, source_target_pairs={{0,1},{1,0},{2,3},{3,2},{4,5},{5,4},{6,7},{7,6},{8,9},{9,8},{10,11... | collective-permute-start | bytes 1585160 | tf_op jit(solution)/shard_map/ppermute | solution.py:403
  2.5 5.6 %collective-permute-start.1 = (f32[776,128]{1,0:T(8,128)S(1)}, f32[776,128]{1,0:T(8,128)S(1)}, u32[]{:S(2)}, u32[]{:S(2)}) collective-permute-start(f32[776,128]{1,0:T(8,128)S(1)} %get-tuple-element.21), channel_id=1, source_target_pairs={{0,15},{1,2},{2,1},{3,4},{4,3},{5,6},{6,5},{7,8},{8,7},{9,10},{10,... | collective-permute-start | bytes 1191944 | tf_op jit(solution)/shard_map/ppermute | solution.py:402
  8.1 0.0 collective-permute-start.2
  8.2 0.0 copy-done
  8.2 0.0 copy-done.1
  8.2 0.0 copy-done.3
  8.2 6.2 %inner.1 = (bf16[2,2,1024,256]{3,2,1,0:T(8,128)(2,1)S(1)}, f32[2,2,1024,128]{3,2,1,0:T(8,128)S(1)}, f32[128,128]{1,0:T(8,128)S(1)}) custom-call(f32[2,4,1024,128]{3,2,1,0:T(8,128)} %tangent_ref.3, f32[4,1024]{1,0:T(4,128)S(1)} %copy-done, f32[4,1024]{1,0:T(4,128)S(1)} %copy-done.3, f32[4,1024]{1,0:T(4,128)S(1)} %copy-done.1), custom_call_target="tpu_custom_call" | custom-call | flops 2000000000 | bytes 8388608 | tf_op jit(solution)/shard_map/inner/pallas_call | solution.py:406
  14.4 0.0 collective-permute-done.near_ref.angles_ref.halo_ref
  14.4 0.0 copy-start.2
  14.4 1.0 %near.1 = (bf16[2,1024,256]{2,1,0:T(8,128)(2,1)S(1)}, f32[128,128]{1,0:T(8,128)S(1)}) custom-call(f32[1032,128]{1,0:T(8,128)S(1)} %collective-permute-done.near_ref.angles_ref.halo_ref, f32[1032,128]{1,0:T(8,128)S(1)} %collective-permute-done.near_ref.angles_ref.halo_ref, f32[2,2,1024,128]{3,2,1,0:T(8,128)S(1)} %get-tuple-element.25.partial_ref, ...), custom_call_target="tpu_custom_call" | custom-call | flops 400000000 | bytes 2097152 | tf_op jit(solution)/shard_map/near/pallas_call | solution.py:429
  15.5 0.0 copy-start.4
  15.5 0.0 collective-permute-done.1.far_ref.angles_ref.halo_ref
  15.5 0.9 %far.1 = (bf16[2,768,256]{2,1,0:T(8,128)(2,1)S(1)}, f32[128,128]{1,0:T(8,128)S(1)}) custom-call(f32[776,128]{1,0:T(8,128)S(1)} %collective-permute-done.1.far_ref.angles_ref.halo_ref, f32[776,128]{1,0:T(8,128)S(1)} %collective-permute-done.1.far_ref.angles_ref.halo_ref, f32[2,2,1024,128]{3,2,1,0:T(8,128)S(1)} %get-tuple-element.25.partial_ref, ...), custom_call_target="tpu_custom_call" | custom-call | flops 400000000 | bytes 2097152 | tf_op jit(solution)/shard_map/far/pallas_call | solution.py:429
  16.4 0.0 collective-permute-done.2.halo_ref
  16.4 0.5 %tail.1 = (bf16[2,256,256]{2,1,0:T(8,128)(2,1)S(1)}, f32[128,128]{1,0:T(8,128)S(1)}) custom-call(f32[776,128]{1,0:T(8,128)S(1)} %collective-permute-done.1.far_ref.angles_ref.halo_ref, f32[256,128]{1,0:T(8,128)S(1)} %collective-permute-done.2.halo_ref, f32[2,2,1024,128]{3,2,1,0:T(8,128)S(1)} %get-tuple-element.25.partial_ref, f32[4,1024]{1,0:T(4,128)S(1)} %copy-done, ...), custom_call_target="tpu_custom_call" | custom-call | flops 400000000 | bytes 2097152 | tf_op jit(solution)/shard_map/tail/pallas_call | solution.py:429
  16.9 1.4 %collective-permute-start.3 = (f32[128,128]{1,0:T(8,128)S(1)}, f32[128,128]{1,0:T(8,128)S(1)}, u32[]{:S(2)}, u32[]{:S(2)}) collective-permute-start(f32[128,128]{1,0:T(8,128)S(1)} %get-tuple-element.29.refs_0_), channel_id=1, source_target_pairs={{0,1},{1,0},{2,3},{3,2},{4,5},{5,4},{6,7},{7,6},{8,9},{9,8},{10,11... | collective-permute-start | bytes 196616 | tf_op jit(solution)/shard_map/ppermute | solution.py:368
  18.3 0.9 %collective-permute-done.3.refs_1_ = f32[128,128]{1,0:T(8,128)S(1)} collective-permute-done((f32[128,128]{1,0:T(8,128)S(1)}, f32[128,128]{1,0:T(8,128)S(1)}, u32[]{:S(2)}, u32[]{:S(2)}) %collective-permute-start.3) | collective-permute-done | bytes 65568 | tf_op jit(solution)/shard_map/ppermute | solution.py:368
  19.2 3.1 %collective-permute-start.6 = (f32[128,128]{1,0:T(8,128)S(1)}, f32[128,128]{1,0:T(8,128)S(1)}, u32[]{:S(2)}, u32[]{:S(2)}) collective-permute-start(f32[128,128]{1,0:T(8,128)S(1)} %gram_sum.2.refs_0_), channel_id=1, source_target_pairs={{0,6},{1,7},{2,4},{3,5},{4,2},{5,3},{6,0},{7,1},{8,14},{9,15},{10,... | collective-permute-start | bytes 196616 | tf_op jit(solution)/shard_map/ppermute | solution.py:368
  22.3 0.4 %collective-permute-start.5 = (f32[128,128]{1,0:T(8,128)S(1)}, f32[128,128]{1,0:T(8,128)S(1)}, u32[]{:S(2)}, u32[]{:S(2)}) collective-permute-start(f32[128,128]{1,0:T(8,128)S(1)} %gram_sum.2.refs_0_), channel_id=1, source_target_pairs={{0,4},{1,5},{2,6},{3,7},{4,0},{5,1},{6,2},{7,3},{8,12},{9,13},{10,... | collective-permute-start | bytes 196616 | tf_op jit(solution)/shard_map/ppermute | solution.py:368
  22.7 0.2 collective-permute-start.4
  22.9 1.8 %collective-permute-done.6.refs_3_ = f32[128,128]{1,0:T(8,128)S(1)} collective-permute-done((f32[128,128]{1,0:T(8,128)S(1)}, f32[128,128]{1,0:T(8,128)S(1)}, u32[]{:S(2)}, u32[]{:S(2)}) %collective-permute-start.6) | collective-permute-done | bytes 65568 | tf_op jit(solution)/shard_map/ppermute | solution.py:368
  24.7 1.9 %collective-permute-done.5.refs_2_ = f32[128,128]{1,0:T(8,128)S(1)} collective-permute-done((f32[128,128]{1,0:T(8,128)S(1)}, f32[128,128]{1,0:T(8,128)S(1)}, u32[]{:S(2)}, u32[]{:S(2)}) %collective-permute-start.5) | collective-permute-done | bytes 65568 | tf_op jit(solution)/shard_map/ppermute | solution.py:368
  26.6 0.4 %collective-permute-done.4.refs_1_ = f32[128,128]{1,0:T(8,128)S(1)} collective-permute-done((f32[128,128]{1,0:T(8,128)S(1)}, f32[128,128]{1,0:T(8,128)S(1)}, u32[]{:S(2)}, u32[]{:S(2)}) %collective-permute-start.4) | collective-permute-done | bytes 65568 | tf_op jit(solution)/shard_map/ppermute | solution.py:368
  27.0 2.7 %collective-permute-start.7 = (f32[128,128]{1,0:T(8,128)S(1)}, f32[128,128]{1,0:T(8,128)S(1)}, u32[]{:S(2)}, u32[]{:S(2)}) collective-permute-start(f32[128,128]{1,0:T(8,128)S(1)} %gram_sum.3.gram_ref), channel_id=1, source_target_pairs={{0,8},{1,9},{2,10},{3,11},{4,12},{5,13},{6,14},{7,15},{8,0},{9,1},... | collective-permute-start | bytes 196616 | tf_op jit(solution)/shard_map/ppermute | solution.py:368
  29.7 0.0 copy-done.2
  29.7 1.1 %angles.1 = (f32[4,1024]{1,0:T(4,128)}, f32[4,1024]{1,0:T(4,128)}) custom-call(f32[1032,128]{1,0:T(8,128)S(1)} %collective-permute-done.near_ref.angles_ref.halo_ref, f32[776,128]{1,0:T(8,128)S(1)} %collective-permute-done.1.far_ref.angles_ref.halo_ref, f32[4,1024]{1,0:T(4,128)S(1)} %copy-done, f32[4,1024]{1,0:T(4,128)S(1)} %copy-done.2, ...), custom_call_target="tpu_custom_call" | custom-call | flops 1000000 | bytes 1000000 | tf_op jit(solution)/shard_map/angles/pallas_call | solution.py:464
  30.8 1.4 %collective-permute-done.7.other_ref = f32[128,128]{1,0:T(8,128)S(1)} collective-permute-done((f32[128,128]{1,0:T(8,128)S(1)}, f32[128,128]{1,0:T(8,128)S(1)}, u32[]{:S(2)}, u32[]{:S(2)}) %collective-permute-start.7) | collective-permute-done | bytes 65568 | tf_op jit(solution)/shard_map/ppermute | solution.py:368
  32.3 0.0 copy-done.4
  32.3 5.6 %ortho.1 = (f32[2,4,1024,128]{3,2,1,0:T(8,128)}, f32[1,128]{1,0:T(1,128)}) custom-call(f32[128,128]{1,0:T(8,128)S(1)} %gram_sum.3.gram_ref, f32[128,128]{1,0:T(8,128)S(1)} %collective-permute-done.7.other_ref, f32[1,128]{1,0:T(1,128)S(1)} %bitcast.2, bf16[2,2,1024,256]{3,2,1,0:T(8,128)(2,1)S(1)} %get-tuple-element.30.inner_ref, ...), custom_call_target="tpu_custom_call" | custom-call | tf_op jit(solution)/shard_map/ortho/pallas_call | solution.py:475
  (2 shorter events, 0.0 us)
Async XLA Ops:
  0.6 7.5 %copy-start = (f32[4,1024]{1,0:T(4,128)S(1)}, f32[4,1024]{1,0:T(4,128)}, u32[]{:S(2)}) copy-start(f32[4,1024]{1,0:T(4,128)} %positions_ref.9) | copy-start | bytes 49156
  0.6 7.5 %copy-start.1 = (f32[4,1024]{1,0:T(4,128)S(1)}, f32[4,1024]{1,0:T(4,128)}, u32[]{:S(2)}) copy-start(f32[4,1024]{1,0:T(4,128)} %coupling_ref.9) | copy-start | bytes 49156
  0.7 7.5 %copy-start.3 = (f32[4,1024]{1,0:T(4,128)S(1)}, f32[4,1024]{1,0:T(4,128)}, u32[]{:S(2)}) copy-start(f32[4,1024]{1,0:T(4,128)} %kick_ref.3) | copy-start | bytes 49156
  2.0 12.4 %collective-permute-start = (f32[1032,128]{1,0:T(8,128)S(1)}, f32[1032,128]{1,0:T(8,128)S(1)}, u32[]{:S(2)}, u32[]{:S(2)}) collective-permute-start(f32[1032,128]{1,0:T(8,128)S(1)} %get-tuple-element.20), channel_id=1, source_target_pairs={{0,1},{1,0},{2,3},{3,2},{4,5},{5,4},{6,7},{7,6},{8,9},{9,8},{10,11... | collective-permute-start | bytes 1585160 | tf_op jit(solution)/shard_map/ppermute | solution.py:403
  2.5 13.0 %collective-permute-start.1 = (f32[776,128]{1,0:T(8,128)S(1)}, f32[776,128]{1,0:T(8,128)S(1)}, u32[]{:S(2)}, u32[]{:S(2)}) collective-permute-start(f32[776,128]{1,0:T(8,128)S(1)} %get-tuple-element.21), channel_id=1, source_target_pairs={{0,15},{1,2},{2,1},{3,4},{4,3},{5,6},{6,5},{7,8},{8,7},{9,10},{10,... | collective-permute-start | bytes 1191944 | tf_op jit(solution)/shard_map/ppermute | solution.py:402
  8.1 8.2 %collective-permute-start.2 = (f32[256,128]{1,0:T(8,128)S(1)}, f32[256,128]{1,0:T(8,128)S(1)}, u32[]{:S(2)}, u32[]{:S(2)}) collective-permute-start(f32[256,128]{1,0:T(8,128)S(1)} %get-tuple-element.24), channel_id=1, source_target_pairs={{0,15},{1,2},{2,1},{3,4},{4,3},{5,6},{6,5},{7,8},{8,7},{9,10},{10,... | collective-permute-start | bytes 393224 | tf_op jit(solution)/shard_map/ppermute | solution.py:404
  14.4 15.3 %copy-start.2 = (f32[4,1024]{1,0:T(4,128)S(1)}, f32[4,1024]{1,0:T(4,128)}, u32[]{:S(2)}) copy-start(f32[4,1024]{1,0:T(4,128)} %momenta_ref.1) | copy-start | bytes 49156
  15.5 16.8 %copy-start.4 = (f32[128]{0:T(128)S(1)}, f32[128]{0:T(128)}, u32[]{:S(2)}) copy-start(f32[128]{0:T(128)} %param.11) | copy-start | bytes 1540
  16.9 2.3 %collective-permute-start.3 = (f32[128,128]{1,0:T(8,128)S(1)}, f32[128,128]{1,0:T(8,128)S(1)}, u32[]{:S(2)}, u32[]{:S(2)}) collective-permute-start(f32[128,128]{1,0:T(8,128)S(1)} %get-tuple-element.29.refs_0_), channel_id=1, source_target_pairs={{0,1},{1,0},{2,3},{3,2},{4,5},{5,4},{6,7},{7,6},{8,9},{9,8},{10,11... | collective-permute-start | bytes 196616 | tf_op jit(solution)/shard_map/ppermute | solution.py:368
  19.2 5.5 %collective-permute-start.6 = (f32[128,128]{1,0:T(8,128)S(1)}, f32[128,128]{1,0:T(8,128)S(1)}, u32[]{:S(2)}, u32[]{:S(2)}) collective-permute-start(f32[128,128]{1,0:T(8,128)S(1)} %gram_sum.2.refs_0_), channel_id=1, source_target_pairs={{0,6},{1,7},{2,4},{3,5},{4,2},{5,3},{6,0},{7,1},{8,14},{9,15},{10,... | collective-permute-start | bytes 196616 | tf_op jit(solution)/shard_map/ppermute | solution.py:368
  22.3 4.3 %collective-permute-start.5 = (f32[128,128]{1,0:T(8,128)S(1)}, f32[128,128]{1,0:T(8,128)S(1)}, u32[]{:S(2)}, u32[]{:S(2)}) collective-permute-start(f32[128,128]{1,0:T(8,128)S(1)} %gram_sum.2.refs_0_), channel_id=1, source_target_pairs={{0,4},{1,5},{2,6},{3,7},{4,0},{5,1},{6,2},{7,3},{8,12},{9,13},{10,... | collective-permute-start | bytes 196616 | tf_op jit(solution)/shard_map/ppermute | solution.py:368
  22.7 4.3 %collective-permute-start.4 = (f32[128,128]{1,0:T(8,128)S(1)}, f32[128,128]{1,0:T(8,128)S(1)}, u32[]{:S(2)}, u32[]{:S(2)}) collective-permute-start(f32[128,128]{1,0:T(8,128)S(1)} %gram_sum.2.refs_0_), channel_id=1, source_target_pairs={{0,2},{1,3},{2,0},{3,1},{4,6},{5,7},{6,4},{7,5},{8,10},{9,11},{10,... | collective-permute-start | bytes 196616 | tf_op jit(solution)/shard_map/ppermute | solution.py:368
  27.0 5.2 %collective-permute-start.7 = (f32[128,128]{1,0:T(8,128)S(1)}, f32[128,128]{1,0:T(8,128)S(1)}, u32[]{:S(2)}, u32[]{:S(2)}) collective-permute-start(f32[128,128]{1,0:T(8,128)S(1)} %gram_sum.3.gram_ref), channel_id=1, source_target_pairs={{0,8},{1,9},{2,10},{3,11},{4,12},{5,13},{6,14},{7,15},{8,0},{9,1},... | collective-permute-start | bytes 196616 | tf_op jit(solution)/shard_map/ppermute | solution.py:368

commit v5 on v4

--- a/solution.py
+++ b/solution.py
@@ -140,9 +140,48 @@
     return odd if side else 1 - odd
 
 
+def pack_symmetric(gram):
+    half = gram.shape[0] // 2
+    shape = (half, 2 * half)
+    row = lax.broadcasted_iota(jnp.int32, shape, 0)
+    lane = lax.broadcasted_iota(jnp.int32, shape, 1)
+    corner = lane_roll(gram[half:], half)
+    top = jnp.where((lane < half) & (lane > row), corner, gram[:half])
+    diagonal = jnp.sum(jnp.where(lane == row, corner, 0.0), axis=0, keepdims=True)
+    return jnp.concatenate([top, jnp.broadcast_to(diagonal, (8, 2 * half))], axis=0)
+
+
+def unpack_symmetric(packed):
+    order = packed.shape[1]
+    half = order // 2
+    top = packed[:half]
+    row = lax.broadcasted_iota(jnp.int32, (half, order), 0)
+    lane = lax.broadcasted_iota(jnp.int32, (half, order), 1)
+    on = lane == row
+    upper = jnp.where((lane >= half) | (lane < row), top, jnp.where(on, 0.5 * top, 0.0))
+    corner = jnp.where(
+        (lane < half) & (lane > row), top, jnp.where(on, 0.5 * packed[half : half + 1], 0.0)
+    )
+    triangle = jnp.concatenate([upper, lane_roll(corner, half)], axis=0)
+    return triangle + triangle.T
+
+
+def finish_sites(table, first_group, first, slot, halo_ref, partial_ref, pairs_ref):
+    for group in range(pairs_ref.shape[1] // LANES):
+        span = slice(group * LANES, (group + 1) * LANES)
+        from_first = slice(first + group * LANES, first + (group + 1) * LANES)
+        at = first_group + group
+        factor = jnp.broadcast_to(table[:, at : at + 1], (LANES, LANES))
+        u = partial_ref[0, slot, from_first, :]
+        mom = partial_ref[1, slot, from_first, :] + factor * (halo_ref[span, :] - u)
+        pairs_ref[0, span, :] = split_pair(u + mom)
+        pairs_ref[1, span, :] = split_pair(mom)
+    return fold_pairs(pair_gram(pairs_ref[0]) + pair_gram(pairs_ref[1]))
+
+
 def row_gram_kernel(
-    side, first, angles_at, angles_ref, halo_ref, partial_ref, positions_ref, coupling_ref,
-    before_ref, pairs_ref, gram_ref, stack,
+    side, halo_ref, partial_ref, positions_ref, coupling_ref, before_ref,
+    pairs_ref, gram_ref, table_ref, stack,
 ):
     columns = positions_ref.shape[1]
     sites = pairs_ref.shape[1]
@@ -150,23 +189,22 @@
     row = slot * (positions_ref.shape[0] - 1)
     x = positions_ref[pl.ds(row, 1), :]
     coupling = coupling_ref[pl.ds(row, 1), :]
-    for group in range(sites // LANES):
-        span = slice(first + group * LANES, first + (group + 1) * LANES)
-        at = angles_at + first // LANES + group
+    for group in range(columns // LANES):
+        span = slice(group * LANES, (group + 1) * LANES)
         stack[group : group + 1, :] = coupling[:, span] * jnp.cos(
-            angles_ref[at : at + 1, :] - x[:, span]
+            halo_ref[sites + group : sites + group + 1, :] - x[:, span]
         )
     table = stack[...].T
-    for group in range(sites // LANES):
-        span = slice(group * LANES, (group + 1) * LANES)
-        from_first = slice(first + group * LANES, first + (group + 1) * LANES)
-        factor = jnp.broadcast_to(table[:, group : group + 1], (LANES, LANES))
-        u = partial_ref[0, slot, from_first, :]
-        mom = partial_ref[1, slot, from_first, :] + factor * (halo_ref[span, :] - u)
-        pairs_ref[0, span, :] = split_pair(u + mom)
-        pairs_ref[1, span, :] = split_pair(mom)
-    gram = pair_gram(pairs_ref[0]) + pair_gram(pairs_ref[1])
-    gram_ref[...] = before_ref[...] + fold_pairs(gram)
+    table_ref[...] = table
+    gram = finish_sites(table, 0, 0, slot, halo_ref, partial_ref, pairs_ref)
+    gram_ref[...] = before_ref[...] + gram
+
+
+def tail_gram_kernel(first, halo_ref, partial_ref, table_ref, before_ref, pairs_ref, packed_ref):
+    gram = finish_sites(
+        table_ref[...], first // LANES, first, side_slot(1), halo_ref, partial_ref, pairs_ref
+    )
+    packed_ref[...] = pack_symmetric(before_ref[...] + gram)
 
 
 def pairwise(terms):
@@ -310,7 +348,9 @@
 ):
     rows, columns = out_ref.shape[1], out_ref.shape[2]
     head = far_ref.shape[1]
-    squares = inverse_factor(gram_ref[...] + other_ref[...], math.sqrt(sites_total), weights_ref)
+    squares = inverse_factor(
+        unpack_symmetric(gram_ref[...] + other_ref[...]), math.sqrt(sites_total), weights_ref
+    )
     growth_ref[...] = (
         log_growth_ref[...] + 0.5 * jnp.log(squares[:1]) - 0.5 * math.log(sites_total)
     )
@@ -425,12 +465,14 @@
         name="inner",
     )(tangent, positions, kick_strength, coupling)
 
-    def finish(name, side, first, sites, angles_at, angles, halo, before):
+    def finish(name, side, sites, halo, before):
         return pl.pallas_call(
-            functools.partial(row_gram_kernel, side, first, angles_at),
-            out_shape=[bf16(2, sites, 2 * vectors), f32(vectors, vectors)],
-            in_specs=[resident] * 6,
-            out_specs=[resident] * 2,
+            functools.partial(row_gram_kernel, side),
+            out_shape=[
+                bf16(2, sites, 2 * vectors), f32(vectors, vectors), f32(LANES, LANES)
+            ],
+            in_specs=[resident] * 5,
+            out_specs=[resident] * 3,
             scratch_shapes=[pltpu.VMEM((LANES, LANES), jnp.float32)],
             compiler_params=pltpu.CompilerParams(vmem_limit_bytes=8 * MIB),
             cost_estimate=pl.CostEstimate(
@@ -438,18 +480,26 @@
             ),
             name=name,
         )(
-            near_core(angles), near_core(halo), near_core(partial), near_core(positions),
-            near_core(coupling), near_core(before),
+            near_core(halo), near_core(partial), near_core(positions), near_core(coupling),
+            near_core(before),
         )
 
-    near_pairs, gram = finish("near", 0, 0, columns, columns, near, near, inner_gram)
-    far_pairs, gram = finish("far", 1, 0, head, head, far, far, gram)
-    tail_pairs, gram = finish("tail", 1, head, tail_sites, head, far, tail, gram)
+    packed_rows = vectors // 2 + 8
+    near_pairs, gram, _ = finish("near", 0, columns, near, inner_gram)
+    far_pairs, gram, table = finish("far", 1, head, far, gram)
+    tail_pairs, gram = pl.pallas_call(
+        functools.partial(tail_gram_kernel, head),
+        out_shape=[bf16(2, tail_sites, 2 * vectors), f32(packed_rows, vectors)],
+        in_specs=[resident] * 4,
+        out_specs=[resident] * 2,
+        compiler_params=pltpu.CompilerParams(vmem_limit_bytes=8 * MIB),
+        name="tail",
+    )(near_core(tail), near_core(partial), near_core(table), near_core(gram))
 
     def summed(terms):
         return pl.pallas_call(
             add_kernel,
-            out_shape=f32(vectors, vectors),
+            out_shape=f32(packed_rows, vectors),
             in_specs=[resident] * len(terms),
             out_specs=resident,
             compiler_params=pltpu.CompilerParams(vmem_limit_bytes=1 * MIB),

time: 38.1 us -> 37.4 us (0.982)
  waiting for transfers between devices: 6.42 us -> 5.78 us
  starting transfers between devices: 14 us -> 13.5 us
  Pallas kernels: 16.8 us -> 17.2 us
    ppermute x5, waiting for transfers between devices: 6.42 us -> 5.77 us  [sum_over_rows(): lax.ppermute(terms[0], 'rows', [(i, i ^ offset) for i in range(devices)])]
    ppermute x5, starting transfers between devices: 7.76 us -> 7.33 us  [sum_over_rows(): lax.ppermute(terms[0], 'rows', [(i, i ^ offset) for i in range(devices)])]
  transfers between devices with their start and end apart: 8 -> 8, of which waited for: 5 -> 5; matrix products, arithmetic and copies ran while one was open for 0% -> 0% of each run, Pallas kernels for 24% -> 26%
where the time goes in v5:
time: 37.4 us; the launch traced here: 37.2 us
  Pallas kernels  17.2 us (46%)
  starting transfers between devices  13.5 us (36%)
  waiting for transfers between devices  5.78 us (15%)
  between operations  0.73 us (2%)
    ppermute x5, starting transfers between devices, sum_over_rows(): lax.ppermute(terms[0], 'rows', [(i, i ^ offset) for i in range(devices)])  7.33 us
    pallas_call x1, Pallas kernels, local(): pl.pallas_call(inner_kernel, out_shape=[bf16(2, rows - 2, columns, 2 * ve...  6.21 us
    ppermute x5, waiting for transfers between devices, sum_over_rows(): lax.ppermute(terms[0], 'rows', [(i, i ^ offset) for i in range(devices)])  5.77 us
    pallas_call x1, Pallas kernels, local(): pl.pallas_call(functools.partial(ortho_kernel, sites_total), out_shape=[p...  5.77 us
    ppermute x1, starting transfers between devices, local(): far = lax.ppermute(far, 'rows', outward)  5.64 us
    pallas_call x2, Pallas kernels, finish(): pl.pallas_call(functools.partial(row_gram_kernel, side), out_shape=[bf16(...  2.31 us
    pallas_call x1, Pallas kernels, local(): pl.pallas_call(edges_kernel, out_shape=[f32(columns + groups, vectors), f...  1.29 us
    pallas_call x1, Pallas kernels, local(): pl.pallas_call(functools.partial(angles_kernel, columns, head), out_shape...  1.13 us
  transfers between devices with their start and end apart: 8, of which 5 were waited for; matrix products, arithmetic and copies ran while one was open for 0% of the time, Pallas kernels for 26%

profile of v5, /device:TPU:0, one launch (start us, length us, event | category | flops | bytes accessed | tf_op | source)
XLA Modules:
  0.0 37.2 jit_solution(729333101099453249)
XLA Ops:
  0.6 0.0 copy-start
  0.6 0.0 copy-start.1
  0.7 0.0 copy-start.3
  0.7 1.3 %edges.1 = (f32[1032,128]{1,0:T(8,128)S(1)}, f32[776,128]{1,0:T(8,128)S(1)}, f32[256,128]{1,0:T(8,128)S(1)}) custom-call(f32[2,4,1024,128]{3,2,1,0:T(8,128)} %tangent_ref.3, f32[4,1024]{1,0:T(4,128)} %positions_ref.7), custom_call_target="tpu_custom_call" | custom-call | tf_op jit(solution)/shard_map/edges/pallas_call | solution.py:428
  2.0 0.5 %collective-permute-start = (f32[1032,128]{1,0:T(8,128)S(1)}, f32[1032,128]{1,0:T(8,128)S(1)}, u32[]{:S(2)}, u32[]{:S(2)}) collective-permute-start(f32[1032,128]{1,0:T(8,128)S(1)} %get-tuple-element.21), channel_id=1, source_target_pairs={{0,1},{1,0},{2,3},{3,2},{4,5},{5,4},{6,7},{7,6},{8,9},{9,8},{10,11... | collective-permute-start | bytes 1585160 | tf_op jit(solution)/shard_map/ppermute | solution.py:443
  2.5 5.6 %collective-permute-start.1 = (f32[776,128]{1,0:T(8,128)S(1)}, f32[776,128]{1,0:T(8,128)S(1)}, u32[]{:S(2)}, u32[]{:S(2)}) collective-permute-start(f32[776,128]{1,0:T(8,128)S(1)} %get-tuple-element.22), channel_id=1, source_target_pairs={{0,15},{1,2},{2,1},{3,4},{4,3},{5,6},{6,5},{7,8},{8,7},{9,10},{10,... | collective-permute-start | bytes 1191944 | tf_op jit(solution)/shard_map/ppermute | solution.py:442
  8.1 0.0 collective-permute-start.2
  8.2 0.0 copy-done
  8.2 0.0 copy-done.1
  8.2 0.0 copy-done.3
  8.2 6.2 %inner.1 = (bf16[2,2,1024,256]{3,2,1,0:T(8,128)(2,1)S(1)}, f32[2,2,1024,128]{3,2,1,0:T(8,128)S(1)}, f32[128,128]{1,0:T(8,128)S(1)}) custom-call(f32[2,4,1024,128]{3,2,1,0:T(8,128)} %tangent_ref.3, f32[4,1024]{1,0:T(4,128)S(1)} %copy-done, f32[4,1024]{1,0:T(4,128)S(1)} %copy-done.3, f32[4,1024]{1,0:T(4,128)S(1)} %copy-done.1), custom_call_target="tpu_custom_call" | custom-call | flops 2000000000 | bytes 8388608 | tf_op jit(solution)/shard_map/inner/pallas_call | solution.py:446
  14.4 0.0 copy-start.2
  14.4 0.0 collective-permute-done.near_ref.halo_ref
  14.4 0.0 copy-start.4
  14.4 1.4 %near.1 = (bf16[2,1024,256]{2,1,0:T(8,128)(2,1)S(1)}, f32[128,128]{1,0:T(8,128)S(1)}, f32[128,128]{1,0:T(8,128)}) custom-call(f32[1032,128]{1,0:T(8,128)S(1)} %collective-permute-done.near_ref.halo_ref, f32[2,2,1024,128]{3,2,1,0:T(8,128)S(1)} %get-tuple-element.26.partial_ref, f32[4,1024]{1,0:T(4,128)S(1)} %copy-done, f32[4,1024]{1,0:T(4,128)S(1)} %copy-done.1, ...), custom_call_target="tpu_custom_call" | custom-call | flops 400000000 | bytes 2097152 | tf_op jit(solution)/shard_map/near/pallas_call | solution.py:469
  15.8 0.0 collective-permute-done.1.far_ref.halo_ref
  15.8 0.9 %far.1 = (bf16[2,768,256]{2,1,0:T(8,128)(2,1)S(1)}, f32[128,128]{1,0:T(8,128)S(1)}, f32[128,128]{1,0:T(8,128)S(1)}) custom-call(f32[776,128]{1,0:T(8,128)S(1)} %collective-permute-done.1.far_ref.halo_ref, f32[2,2,1024,128]{3,2,1,0:T(8,128)S(1)} %get-tuple-element.26.partial_ref, f32[4,1024]{1,0:T(4,128)S(1)} %copy-done, f32[4,1024]{1,0:T(4,128)S(1)} %copy-done.1, ...), custom_call_target="tpu_custom_call" | custom-call | flops 400000000 | bytes 2097152 | tf_op jit(solution)/shard_map/far/pallas_call | solution.py:469
  16.7 0.0 collective-permute-done.2.halo_ref
  16.7 0.5 %tail.1 = (bf16[2,256,256]{2,1,0:T(8,128)(2,1)S(1)}, f32[72,128]{1,0:T(8,128)S(1)}) custom-call(f32[256,128]{1,0:T(8,128)S(1)} %collective-permute-done.2.halo_ref, f32[2,2,1024,128]{3,2,1,0:T(8,128)S(1)} %get-tuple-element.26.partial_ref, f32[128,128]{1,0:T(8,128)S(1)} %get-tuple-element.29.table_ref, f32[128,128]{1,0:T(8,128)S(1)} %get-tuple-element.30.before_ref), custom_call_target="tpu_custom_call" | custom-call | tf_op jit(solution)/shard_map/tail/pallas_call | solution.py:490
  17.2 1.0 %collective-permute-start.3 = (f32[72,128]{1,0:T(8,128)S(1)}, f32[72,128]{1,0:T(8,128)S(1)}, u32[]{:S(2)}, u32[]{:S(2)}) collective-permute-start(f32[72,128]{1,0:T(8,128)S(1)} %get-tuple-element.31.refs_0_), channel_id=1, source_target_pairs={{0,1},{1,0},{2,3},{3,2},{4,5},{5,4},{6,7},{7,6},{8,9},{9,8},{10,11... | collective-permute-start | bytes 110600 | tf_op jit(solution)/shard_map/ppermute | solution.py:408
  18.3 0.9 %collective-permute-done.3.refs_1_ = f32[72,128]{1,0:T(8,128)S(1)} collective-permute-done((f32[72,128]{1,0:T(8,128)S(1)}, f32[72,128]{1,0:T(8,128)S(1)}, u32[]{:S(2)}, u32[]{:S(2)}) %collective-permute-start.3) | collective-permute-done | bytes 36896 | tf_op jit(solution)/shard_map/ppermute | solution.py:408
  19.1 3.0 %collective-permute-start.6 = (f32[72,128]{1,0:T(8,128)S(1)}, f32[72,128]{1,0:T(8,128)S(1)}, u32[]{:S(2)}, u32[]{:S(2)}) collective-permute-start(f32[72,128]{1,0:T(8,128)S(1)} %gram_sum.2.refs_0_), channel_id=1, source_target_pairs={{0,6},{1,7},{2,4},{3,5},{4,2},{5,3},{6,0},{7,1},{8,14},{9,15},{10,... | collective-permute-start | bytes 110600 | tf_op jit(solution)/shard_map/ppermute | solution.py:408
  22.1 0.4 %collective-permute-start.5 = (f32[72,128]{1,0:T(8,128)S(1)}, f32[72,128]{1,0:T(8,128)S(1)}, u32[]{:S(2)}, u32[]{:S(2)}) collective-permute-start(f32[72,128]{1,0:T(8,128)S(1)} %gram_sum.2.refs_0_), channel_id=1, source_target_pairs={{0,4},{1,5},{2,6},{3,7},{4,0},{5,1},{6,2},{7,3},{8,12},{9,13},{10,... | collective-permute-start | bytes 110600 | tf_op jit(solution)/shard_map/ppermute | solution.py:408
  22.6 0.2 collective-permute-start.4
  22.8 1.3 %collective-permute-done.6.refs_3_ = f32[72,128]{1,0:T(8,128)S(1)} collective-permute-done((f32[72,128]{1,0:T(8,128)S(1)}, f32[72,128]{1,0:T(8,128)S(1)}, u32[]{:S(2)}, u32[]{:S(2)}) %collective-permute-start.6) | collective-permute-done | bytes 36896 | tf_op jit(solution)/shard_map/ppermute | solution.py:408
  24.1 2.0 %collective-permute-done.5.refs_2_ = f32[72,128]{1,0:T(8,128)S(1)} collective-permute-done((f32[72,128]{1,0:T(8,128)S(1)}, f32[72,128]{1,0:T(8,128)S(1)}, u32[]{:S(2)}, u32[]{:S(2)}) %collective-permute-start.5) | collective-permute-done | bytes 36896 | tf_op jit(solution)/shard_map/ppermute | solution.py:408
  26.1 0.4 %collective-permute-done.4.refs_1_ = f32[72,128]{1,0:T(8,128)S(1)} collective-permute-done((f32[72,128]{1,0:T(8,128)S(1)}, f32[72,128]{1,0:T(8,128)S(1)}, u32[]{:S(2)}, u32[]{:S(2)}) %collective-permute-start.4) | collective-permute-done | bytes 36896 | tf_op jit(solution)/shard_map/ppermute | solution.py:408
  26.5 2.7 %collective-permute-start.7 = (f32[72,128]{1,0:T(8,128)S(1)}, f32[72,128]{1,0:T(8,128)S(1)}, u32[]{:S(2)}, u32[]{:S(2)}) collective-permute-start(f32[72,128]{1,0:T(8,128)S(1)} %gram_sum.3.gram_ref), channel_id=1, source_target_pairs={{0,8},{1,9},{2,10},{3,11},{4,12},{5,13},{6,14},{7,15},{8,0},{9,1},... | collective-permute-start | bytes 110600 | tf_op jit(solution)/shard_map/ppermute | solution.py:408
  29.2 0.0 copy-done.2
  29.2 1.1 %angles.1 = (f32[4,1024]{1,0:T(4,128)}, f32[4,1024]{1,0:T(4,128)}) custom-call(f32[1032,128]{1,0:T(8,128)S(1)} %collective-permute-done.near_ref.halo_ref, f32[776,128]{1,0:T(8,128)S(1)} %collective-permute-done.1.far_ref.halo_ref, f32[4,1024]{1,0:T(4,128)S(1)} %copy-done, f32[4,1024]{1,0:T(4,128)S(1)} %copy-done.2, f32[4,1024]{1,0:T(4,128)S(1)} %copy-done.3, ...), custom_call_target="tpu_custom_call" | custom-call | flops 1000000 | bytes 1000000 | tf_op jit(solution)/shard_map/angles/pallas_call | solution.py:514
  30.3 1.1 %collective-permute-done.7.other_ref = f32[72,128]{1,0:T(8,128)S(1)} collective-permute-done((f32[72,128]{1,0:T(8,128)S(1)}, f32[72,128]{1,0:T(8,128)S(1)}, u32[]{:S(2)}, u32[]{:S(2)}) %collective-permute-start.7) | collective-permute-done | bytes 36896 | tf_op jit(solution)/shard_map/ppermute | solution.py:408
  31.5 0.0 copy-done.4
  31.5 5.8 %ortho.1 = (f32[2,4,1024,128]{3,2,1,0:T(8,128)}, f32[1,128]{1,0:T(1,128)}) custom-call(f32[72,128]{1,0:T(8,128)S(1)} %gram_sum.3.gram_ref, f32[72,128]{1,0:T(8,128)S(1)} %collective-permute-done.7.other_ref, f32[1,128]{1,0:T(1,128)S(1)} %bitcast.2, bf16[2,2,1024,256]{3,2,1,0:T(8,128)(2,1)S(1)} %get-tuple-element.32.inner_ref, ...), custom_call_target="tpu_custom_call" | custom-call | tf_op jit(solution)/shard_map/ortho/pallas_call | solution.py:525
  (2 shorter events, 0.0 us)
Async XLA Ops:
  0.6 7.5 %copy-start = (f32[4,1024]{1,0:T(4,128)S(1)}, f32[4,1024]{1,0:T(4,128)}, u32[]{:S(2)}) copy-start(f32[4,1024]{1,0:T(4,128)} %positions_ref.7) | copy-start | bytes 49156
  0.6 7.5 %copy-start.1 = (f32[4,1024]{1,0:T(4,128)S(1)}, f32[4,1024]{1,0:T(4,128)}, u32[]{:S(2)}) copy-start(f32[4,1024]{1,0:T(4,128)} %coupling_ref.7) | copy-start | bytes 49156
  0.7 7.5 %copy-start.3 = (f32[4,1024]{1,0:T(4,128)S(1)}, f32[4,1024]{1,0:T(4,128)}, u32[]{:S(2)}) copy-start(f32[4,1024]{1,0:T(4,128)} %kick_ref.3) | copy-start | bytes 49156
  2.0 12.4 %collective-permute-start = (f32[1032,128]{1,0:T(8,128)S(1)}, f32[1032,128]{1,0:T(8,128)S(1)}, u32[]{:S(2)}, u32[]{:S(2)}) collective-permute-start(f32[1032,128]{1,0:T(8,128)S(1)} %get-tuple-element.21), channel_id=1, source_target_pairs={{0,1},{1,0},{2,3},{3,2},{4,5},{5,4},{6,7},{7,6},{8,9},{9,8},{10,11... | collective-permute-start | bytes 1585160 | tf_op jit(solution)/shard_map/ppermute | solution.py:443
  2.5 13.4 %collective-permute-start.1 = (f32[776,128]{1,0:T(8,128)S(1)}, f32[776,128]{1,0:T(8,128)S(1)}, u32[]{:S(2)}, u32[]{:S(2)}) collective-permute-start(f32[776,128]{1,0:T(8,128)S(1)} %get-tuple-element.22), channel_id=1, source_target_pairs={{0,15},{1,2},{2,1},{3,4},{4,3},{5,6},{6,5},{7,8},{8,7},{9,10},{10,... | collective-permute-start | bytes 1191944 | tf_op jit(solution)/shard_map/ppermute | solution.py:442
  8.1 8.6 %collective-permute-start.2 = (f32[256,128]{1,0:T(8,128)S(1)}, f32[256,128]{1,0:T(8,128)S(1)}, u32[]{:S(2)}, u32[]{:S(2)}) collective-permute-start(f32[256,128]{1,0:T(8,128)S(1)} %get-tuple-element.25), channel_id=1, source_target_pairs={{0,15},{1,2},{2,1},{3,4},{4,3},{5,6},{6,5},{7,8},{8,7},{9,10},{10,... | collective-permute-start | bytes 393224 | tf_op jit(solution)/shard_map/ppermute | solution.py:444
  14.4 14.8 %copy-start.2 = (f32[4,1024]{1,0:T(4,128)S(1)}, f32[4,1024]{1,0:T(4,128)}, u32[]{:S(2)}) copy-start(f32[4,1024]{1,0:T(4,128)} %momenta_ref.1) | copy-start | bytes 49156
  14.4 17.1 %copy-start.4 = (f32[128]{0:T(128)S(1)}, f32[128]{0:T(128)}, u32[]{:S(2)}) copy-start(f32[128]{0:T(128)} %param.11) | copy-start | bytes 1540
  17.2 1.9 %collective-permute-start.3 = (f32[72,128]{1,0:T(8,128)S(1)}, f32[72,128]{1,0:T(8,128)S(1)}, u32[]{:S(2)}, u32[]{:S(2)}) collective-permute-start(f32[72,128]{1,0:T(8,128)S(1)} %get-tuple-element.31.refs_0_), channel_id=1, source_target_pairs={{0,1},{1,0},{2,3},{3,2},{4,5},{5,4},{6,7},{7,6},{8,9},{9,8},{10,11... | collective-permute-start | bytes 110600 | tf_op jit(solution)/shard_map/ppermute | solution.py:408
  19.1 4.9 %collective-permute-start.6 = (f32[72,128]{1,0:T(8,128)S(1)}, f32[72,128]{1,0:T(8,128)S(1)}, u32[]{:S(2)}, u32[]{:S(2)}) collective-permute-start(f32[72,128]{1,0:T(8,128)S(1)} %gram_sum.2.refs_0_), channel_id=1, source_target_pairs={{0,6},{1,7},{2,4},{3,5},{4,2},{5,3},{6,0},{7,1},{8,14},{9,15},{10,... | collective-permute-start | bytes 110600 | tf_op jit(solution)/shard_map/ppermute | solution.py:408
  22.1 4.0 %collective-permute-start.5 = (f32[72,128]{1,0:T(8,128)S(1)}, f32[72,128]{1,0:T(8,128)S(1)}, u32[]{:S(2)}, u32[]{:S(2)}) collective-permute-start(f32[72,128]{1,0:T(8,128)S(1)} %gram_sum.2.refs_0_), channel_id=1, source_target_pairs={{0,4},{1,5},{2,6},{3,7},{4,0},{5,1},{6,2},{7,3},{8,12},{9,13},{10,... | collective-permute-start | bytes 110600 | tf_op jit(solution)/shard_map/ppermute | solution.py:408
  22.6 4.0 %collective-permute-start.4 = (f32[72,128]{1,0:T(8,128)S(1)}, f32[72,128]{1,0:T(8,128)S(1)}, u32[]{:S(2)}, u32[]{:S(2)}) collective-permute-start(f32[72,128]{1,0:T(8,128)S(1)} %gram_sum.2.refs_0_), channel_id=1, source_target_pairs={{0,2},{1,3},{2,0},{3,1},{4,6},{5,7},{6,4},{7,5},{8,10},{9,11},{10,... | collective-permute-start | bytes 110600 | tf_op jit(solution)/shard_map/ppermute | solution.py:408
  26.5 4.9 %collective-permute-start.7 = (f32[72,128]{1,0:T(8,128)S(1)}, f32[72,128]{1,0:T(8,128)S(1)}, u32[]{:S(2)}, u32[]{:S(2)}) collective-permute-start(f32[72,128]{1,0:T(8,128)S(1)} %gram_sum.3.gram_ref), channel_id=1, source_target_pairs={{0,8},{1,9},{2,10},{3,11},{4,12},{5,13},{6,14},{7,15},{8,0},{9,1},... | collective-permute-start | bytes 110600 | tf_op jit(solution)/shard_map/ppermute | solution.py:408

commit v6 on v5

--- a/solution.py
+++ b/solution.py
@@ -33,30 +33,26 @@
     return (gram[:half, :half] + gram[half:, half:]) + (gram[:half, half:] + gram[half:, :half])
 
 
-def edges_kernel(
-    tangent_ref, positions_hbm, near_ref, far_ref, tail_ref, positions_ref, sems
-):
+def edge_kernel(side, earlier, tangent_ref, positions_hbm, *refs):
+    first_ref, second_ref, positions_ref, sems = refs[earlier:]
     rows, columns = positions_ref.shape
-    head = columns - tail_ref.shape[0]
-    odd = lax.rem(lax.axis_index("rows"), 2)
-    near_row = (1 - odd) * (rows - 1)
-    far_row = rows - 1 - near_row
-    near, far = tangent_ref.at[0, near_row], tangent_ref.at[0, far_row]
+    head = columns - second_ref.shape[0]
+    row = side_slot(side) * (rows - 1)
+    source = tangent_ref.at[0, row]
     copies = [
-        pltpu.make_async_copy(far.at[pl.ds(0, head)], far_ref.at[pl.ds(0, head)], sems.at[0]),
-        pltpu.make_async_copy(far.at[pl.ds(head, columns - head)], tail_ref, sems.at[1]),
-        pltpu.make_async_copy(near, near_ref.at[pl.ds(0, columns)], sems.at[2]),
+        pltpu.make_async_copy(positions_hbm, positions_ref, sems.at[0]),
+        pltpu.make_async_copy(source.at[pl.ds(0, head)], first_ref.at[pl.ds(0, head)], sems.at[1]),
+        pltpu.make_async_copy(source.at[pl.ds(head, columns - head)], second_ref, sems.at[2]),
     ]
-    angle_copy = pltpu.make_async_copy(positions_hbm, positions_ref, sems.at[3])
-    angle_copy.start()
     for copy in copies:
         copy.start()
-    angle_copy.wait()
-    for row, at, out in ((near_row, columns, near_ref), (far_row, head, far_ref)):
-        angles = positions_ref[pl.ds(row, 1), :]
-        for group in range(columns // LANES):
-            out[at + group : at + group + 1, :] = angles[:, group * LANES : (group + 1) * LANES]
-    for copy in copies:
+    copies[0].wait()
+    angles = positions_ref[pl.ds(row, 1), :]
+    for group in range(columns // LANES):
+        first_ref[head + group : head + group + 1, :] = angles[
+            :, group * LANES : (group + 1) * LANES
+        ]
+    for copy in copies[1:]:
         copy.wait()
 
 
@@ -166,25 +162,34 @@
     return triangle + triangle.T
 
 
-def finish_sites(table, first_group, first, slot, halo_ref, partial_ref, pairs_ref):
+def finish_sites(table, first_group, first, slot, halo, partial_ref, pairs_ref):
     for group in range(pairs_ref.shape[1] // LANES):
         span = slice(group * LANES, (group + 1) * LANES)
         from_first = slice(first + group * LANES, first + (group + 1) * LANES)
         at = first_group + group
         factor = jnp.broadcast_to(table[:, at : at + 1], (LANES, LANES))
         u = partial_ref[0, slot, from_first, :]
-        mom = partial_ref[1, slot, from_first, :] + factor * (halo_ref[span, :] - u)
+        mom = partial_ref[1, slot, from_first, :] + factor * (halo(group * LANES) - u)
         pairs_ref[0, span, :] = split_pair(u + mom)
         pairs_ref[1, span, :] = split_pair(mom)
     return fold_pairs(pair_gram(pairs_ref[0]) + pair_gram(pairs_ref[1]))
 
 
 def row_gram_kernel(
-    side, halo_ref, partial_ref, positions_ref, coupling_ref, before_ref,
-    pairs_ref, gram_ref, table_ref, stack,
+    side, parts, *refs,
 ):
+    halo_ref, halo_rest = refs[0], refs[1:parts]
+    (
+        partial_ref, positions_ref, coupling_ref, before_ref, pairs_ref, gram_ref, *table_ref, stack
+    ) = refs[parts:]
     columns = positions_ref.shape[1]
-    sites = pairs_ref.shape[1]
+    sites = halo_ref.shape[0] - columns // LANES
+
+    def halo(at):
+        if at < sites:
+            return halo_ref[at : at + LANES, :]
+        return halo_rest[0][at - sites : at - sites + LANES, :]
+
     slot = side_slot(side)
     row = slot * (positions_ref.shape[0] - 1)
     x = positions_ref[pl.ds(row, 1), :]
@@ -195,14 +200,16 @@
             halo_ref[sites + group : sites + group + 1, :] - x[:, span]
         )
     table = stack[...].T
-    table_ref[...] = table
-    gram = finish_sites(table, 0, 0, slot, halo_ref, partial_ref, pairs_ref)
+    if table_ref:
+        table_ref[0][...] = table
+    gram = finish_sites(table, 0, 0, slot, halo, partial_ref, pairs_ref)
     gram_ref[...] = before_ref[...] + gram
 
 
 def tail_gram_kernel(first, halo_ref, partial_ref, table_ref, before_ref, pairs_ref, packed_ref):
     gram = finish_sites(
-        table_ref[...], first // LANES, first, side_slot(1), halo_ref, partial_ref, pairs_ref
+        table_ref[...], first // LANES, first, side_slot(1),
+        lambda at: halo_ref[at : at + LANES, :], partial_ref, pairs_ref,
     )
     packed_ref[...] = pack_symmetric(before_ref[...] + gram)
 
@@ -425,22 +432,30 @@
 
     tail_sites = columns // 4 if columns % (4 * LANES) == 0 else LANES
     head = columns - tail_sites
-    near, far, tail = pl.pallas_call(
-        edges_kernel,
-        out_shape=[
-            f32(columns + groups, vectors), f32(head + groups, vectors), f32(tail_sites, vectors)
-        ],
-        in_specs=[in_hbm, in_hbm],
-        out_specs=[resident] * 3,
-        scratch_shapes=[
-            pltpu.VMEM((rows, columns), jnp.float32), pltpu.SemaphoreType.DMA((4,))
-        ],
-        compiler_params=pltpu.CompilerParams(vmem_limit_bytes=4 * MIB),
-        name="edges",
-    )(tangent, pltpu.with_memory_space_constraint(positions, pltpu.HBM))
+    half = columns // 2
+
+    def edge(name, side, first_sites, *earlier):
+        return pl.pallas_call(
+            functools.partial(edge_kernel, side, len(earlier)),
+            out_shape=[
+                f32(first_sites + groups, vectors), f32(columns - first_sites, vectors)
+            ],
+            in_specs=[in_hbm, in_hbm] + [resident] * len(earlier),
+            out_specs=[resident] * 2,
+            scratch_shapes=[
+                pltpu.VMEM((rows, columns), jnp.float32), pltpu.SemaphoreType.DMA((3,))
+            ],
+            compiler_params=pltpu.CompilerParams(vmem_limit_bytes=4 * MIB),
+            name=name,
+        )(tangent, pltpu.with_memory_space_constraint(positions, pltpu.HBM), *earlier)
+
+    far, tail = edge("far_edge", 1, head)
+    packed = tail
     outward = [(i, (i + 1 if i % 2 else i - 1) % devices) for i in range(devices)]
     far = lax.ppermute(far, "rows", outward)
+    near, rest = edge("near_edge", 0, half, near_core(packed))
     near = lax.ppermute(near, "rows", [(i, i ^ 1) for i in range(devices)])
+    rest = lax.ppermute(rest, "rows", [(i, i ^ 1) for i in range(devices)])
     tail = lax.ppermute(tail, "rows", outward)
 
     inner_pairs, partial, inner_gram = pl.pallas_call(
@@ -465,14 +480,15 @@
         name="inner",
     )(tangent, positions, kick_strength, coupling)
 
-    def finish(name, side, sites, halo, before):
+    def finish(name, side, sites, halos, before, tables):
         return pl.pallas_call(
-            functools.partial(row_gram_kernel, side),
+            functools.partial(row_gram_kernel, side, len(halos)),
             out_shape=[
-                bf16(2, sites, 2 * vectors), f32(vectors, vectors), f32(LANES, LANES)
+                bf16(2, sites, 2 * vectors), f32(vectors, vectors),
+                *[f32(LANES, LANES)] * tables,
             ],
-            in_specs=[resident] * 5,
-            out_specs=[resident] * 3,
+            in_specs=[resident] * (4 + len(halos)),
+            out_specs=[resident] * (2 + tables),
             scratch_shapes=[pltpu.VMEM((LANES, LANES), jnp.float32)],
             compiler_params=pltpu.CompilerParams(vmem_limit_bytes=8 * MIB),
             cost_estimate=pl.CostEstimate(
@@ -480,13 +496,13 @@
             ),
             name=name,
         )(
-            near_core(halo), near_core(partial), near_core(positions), near_core(coupling),
-            near_core(before),
+            *[near_core(halo) for halo in halos], near_core(partial), near_core(positions),
+            near_core(coupling), near_core(before),
         )
 
     packed_rows = vectors // 2 + 8
-    near_pairs, gram, _ = finish("near", 0, columns, near, inner_gram)
-    far_pairs, gram, table = finish("far", 1, head, far, gram)
+    near_pairs, gram = finish("near", 0, columns, [near, rest], inner_gram, 0)
+    far_pairs, gram, table = finish("far", 1, head, [far], gram, 1)
     tail_pairs, gram = pl.pallas_call(
         functools.partial(tail_gram_kernel, head),
         out_shape=[bf16(2, tail_sites, 2 * vectors), f32(packed_rows, vectors)],
@@ -512,7 +528,7 @@
     gram, gram_other = terms
 
     new_positions, new_momenta = pl.pallas_call(
-        functools.partial(angles_kernel, columns, head),
+        functools.partial(angles_kernel, half, head),
         out_shape=[jax.ShapeDtypeStruct((rows, columns), jnp.float32)] * 2,
         in_specs=[resident] * 6,
         out_specs=[resident] * 2,

time: 37.4 us -> 37.2 us (level)
  starting transfers between devices: 13.5 us -> 12.6 us
  Pallas kernels: 17.2 us -> 17.7 us
    ppermute x5, starting transfers between devices: 7.33 us -> 6.27 us  [sum_over_rows(): lax.ppermute(terms[0], 'rows', [(i, i ^ offset) for i in range(devices)])]
    ppermute x0 -> x1, starting transfers between devices: none -> 0.5 us  [local(): rest = lax.ppermute(rest, 'rows', [(i, i ^ 1) for i in range(devices)])]
    pallas_call x4 -> x5, Pallas kernels: 4.73 us -> 5.23 us  [the longest x2 2.15 us: edge(): pl.pallas_call(functools.partial(edge_kernel, side, len(earlier)), out_sh...]
    ppermute x1, starting transfers between devices: 0.52 us -> 0.07 us  [local(): near = lax.ppermute(near, 'rows', [(i, i ^ 1) for i in range(devices)])]
  transfers between devices with their start and end apart: 8 -> 9, of which waited for: 5 -> 5; matrix products, arithmetic and copies ran while one was open for 0% -> 0% of each run, Pallas kernels for 26% -> 28%
where the time goes in v6:
time: 37.2 us; the launch traced here: 36.9 us
  Pallas kernels  17.7 us (48%)
  starting transfers between devices  12.6 us (34%)
  waiting for transfers between devices  5.92 us (16%)
  between operations  0.76 us (2%)
    ppermute x5, starting transfers between devices, sum_over_rows(): lax.ppermute(terms[0], 'rows', [(i, i ^ offset) for i in range(devices)])  6.27 us
    pallas_call x1, Pallas kernels, local(): pl.pallas_call(inner_kernel, out_shape=[bf16(2, rows - 2, columns, 2 * ve...  6.19 us
    ppermute x5, waiting for transfers between devices, sum_over_rows(): lax.ppermute(terms[0], 'rows', [(i, i ^ offset) for i in range(devices)])  5.91 us
    pallas_call x1, Pallas kernels, local(): pl.pallas_call(functools.partial(ortho_kernel, sites_total), out_shape=[p...  5.76 us
    ppermute x1, starting transfers between devices, local(): far = lax.ppermute(far, 'rows', outward)  5.48 us
    pallas_call x2, Pallas kernels, edge(): pl.pallas_call(functools.partial(edge_kernel, side, len(earlier)), out_sh...  2.15 us
    pallas_call x2, Pallas kernels, finish(): pl.pallas_call(functools.partial(row_gram_kernel, side, len(halos)), out_...  1.94 us
    pallas_call x1, Pallas kernels, local(): pl.pallas_call(functools.partial(angles_kernel, half, head), out_shape=[j...  1.13 us
  transfers between devices with their start and end apart: 9, of which 5 were waited for; matrix products, arithmetic and copies ran while one was open for 0% of the time, Pallas kernels for 28%

profile of v6, /device:TPU:0, one launch (start us, length us, event | category | flops | bytes accessed | tf_op | source)
XLA Modules:
  0.0 36.9 jit_solution(1788354391616688826)
XLA Ops:
  0.6 0.0 copy-start
  0.6 0.0 copy-start.1
  0.7 0.0 copy-start.3
  0.7 1.1 %far_edge.1 = (f32[776,128]{1,0:T(8,128)S(1)}, f32[256,128]{1,0:T(8,128)S(1)}) custom-call(f32[2,4,1024,128]{3,2,1,0:T(8,128)} %tangent_ref.5, f32[4,1024]{1,0:T(4,128)} %refs_2_.1), custom_call_target="tpu_custom_call" | custom-call | tf_op jit(solution)/shard_map/far_edge/pallas_call | solution.py:438
  1.8 5.5 %collective-permute-start.1 = (f32[776,128]{1,0:T(8,128)S(1)}, f32[776,128]{1,0:T(8,128)S(1)}, u32[]{:S(2)}, u32[]{:S(2)}) collective-permute-start(f32[776,128]{1,0:T(8,128)S(1)} %get-tuple-element.24), channel_id=1, source_target_pairs={{0,15},{1,2},{2,1},{3,4},{4,3},{5,6},{6,5},{7,8},{8,7},{9,10},{10,... | collective-permute-start | bytes 1191944 | tf_op jit(solution)/shard_map/ppermute | solution.py:455
  7.2 1.1 %near_edge.1 = (f32[520,128]{1,0:T(8,128)S(1)}, f32[512,128]{1,0:T(8,128)S(1)}) custom-call(f32[2,4,1024,128]{3,2,1,0:T(8,128)} %tangent_ref.5, f32[4,1024]{1,0:T(4,128)} %refs_2_.1, f32[256,128]{1,0:T(8,128)S(1)} %get-tuple-element.22.refs_0_), custom_call_target="tpu_custom_call" | custom-call | tf_op jit(solution)/shard_map/near_edge/pallas_call | solution.py:438
  8.3 0.1 collective-permute-start
  8.4 0.5 %collective-permute-start.3 = (f32[512,128]{1,0:T(8,128)S(1)}, f32[512,128]{1,0:T(8,128)S(1)}, u32[]{:S(2)}, u32[]{:S(2)}) collective-permute-start(f32[512,128]{1,0:T(8,128)S(1)} %get-tuple-element.28), channel_id=1, source_target_pairs={{0,1},{1,0},{2,3},{3,2},{4,5},{5,4},{6,7},{7,6},{8,9},{9,8},{10,11... | collective-permute-start | bytes 786440 | tf_op jit(solution)/shard_map/ppermute | solution.py:458
  8.9 0.3 collective-permute-start.2
  9.2 0.0 copy-done
  9.2 0.0 copy-done.1
  9.2 0.0 copy-done.3
  9.2 6.2 %inner.1 = (bf16[2,2,1024,256]{3,2,1,0:T(8,128)(2,1)S(1)}, f32[2,2,1024,128]{3,2,1,0:T(8,128)S(1)}, f32[128,128]{1,0:T(8,128)S(1)}) custom-call(f32[2,4,1024,128]{3,2,1,0:T(8,128)} %tangent_ref.5, f32[4,1024]{1,0:T(4,128)S(1)} %copy-done, f32[4,1024]{1,0:T(4,128)S(1)} %copy-done.3, f32[4,1024]{1,0:T(4,128)S(1)} %copy-done.1), custom_call_target="tpu_custom_call" | custom-call | flops 2000000000 | bytes 8388608 | tf_op jit(solution)/shard_map/inner/pallas_call | solution.py:461
  15.4 0.0 copy-start.2
  15.4 0.0 collective-permute-done.3.refs_1_
  15.4 0.0 collective-permute-done.near_ref.refs_0_
  15.4 0.0 copy-start.4
  15.4 1.0 %near.1 = (bf16[2,1024,256]{2,1,0:T(8,128)(2,1)S(1)}, f32[128,128]{1,0:T(8,128)S(1)}) custom-call(f32[520,128]{1,0:T(8,128)S(1)} %collective-permute-done.near_ref.refs_0_, f32[512,128]{1,0:T(8,128)S(1)} %collective-permute-done.3.refs_1_, f32[2,2,1024,128]{3,2,1,0:T(8,128)S(1)} %get-tuple-element.27.refs_2_.refs_1_.partial_ref, f32[4,1024]{1,0:T(4,128)S(1)} %copy-done, ...), custom_call_target="tpu_custom_call" | custom-call | flops 400000000 | bytes 2097152 | tf_op jit(solution)/shard_map/near/pallas_call | solution.py:484
  16.5 0.0 collective-permute-done.1.far_ref.refs_0_
  16.5 0.9 %far.1 = (bf16[2,768,256]{2,1,0:T(8,128)(2,1)S(1)}, f32[128,128]{1,0:T(8,128)S(1)}, f32[128,128]{1,0:T(8,128)S(1)}) custom-call(f32[776,128]{1,0:T(8,128)S(1)} %collective-permute-done.1.far_ref.refs_0_, f32[2,2,1024,128]{3,2,1,0:T(8,128)S(1)} %get-tuple-element.27.refs_2_.refs_1_.partial_ref, f32[4,1024]{1,0:T(4,128)S(1)} %copy-done, ...), custom_call_target="tpu_custom_call" | custom-call | flops 400000000 | bytes 2097152 | tf_op jit(solution)/shard_map/far/pallas_call | solution.py:484
  17.4 0.0 collective-permute-done.2.halo_ref
  17.4 0.5 %tail.1 = (bf16[2,256,256]{2,1,0:T(8,128)(2,1)S(1)}, f32[72,128]{1,0:T(8,128)S(1)}) custom-call(f32[256,128]{1,0:T(8,128)S(1)} %collective-permute-done.2.halo_ref, f32[2,2,1024,128]{3,2,1,0:T(8,128)S(1)} %get-tuple-element.27.refs_2_.refs_1_.partial_ref, f32[128,128]{1,0:T(8,128)S(1)} %get-tuple-element.31.table_ref, ...), custom_call_target="tpu_custom_call" | custom-call | tf_op jit(solution)/shard_map/tail/pallas_call | solution.py:506
  17.8 0.1 collective-permute-start.4
  18.0 1.2 %collective-permute-done.4.refs_1_ = f32[72,128]{1,0:T(8,128)S(1)} collective-permute-done((f32[72,128]{1,0:T(8,128)S(1)}, f32[72,128]{1,0:T(8,128)S(1)}, u32[]{:S(2)}, u32[]{:S(2)}) %collective-permute-start.4) | collective-permute-done | bytes 36896 | tf_op jit(solution)/shard_map/ppermute | solution.py:415
  19.1 2.7 %collective-permute-start.7 = (f32[72,128]{1,0:T(8,128)S(1)}, f32[72,128]{1,0:T(8,128)S(1)}, u32[]{:S(2)}, u32[]{:S(2)}) collective-permute-start(f32[72,128]{1,0:T(8,128)S(1)} %gram_sum.2.refs_0_), channel_id=1, source_target_pairs={{0,6},{1,7},{2,4},{3,5},{4,2},{5,3},{6,0},{7,1},{8,14},{9,15},{10,... | collective-permute-start | bytes 110600 | tf_op jit(solution)/shard_map/ppermute | solution.py:415
  21.8 0.4 %collective-permute-start.6 = (f32[72,128]{1,0:T(8,128)S(1)}, f32[72,128]{1,0:T(8,128)S(1)}, u32[]{:S(2)}, u32[]{:S(2)}) collective-permute-start(f32[72,128]{1,0:T(8,128)S(1)} %gram_sum.2.refs_0_), channel_id=1, source_target_pairs={{0,4},{1,5},{2,6},{3,7},{4,0},{5,1},{6,2},{7,3},{8,12},{9,13},{10,... | collective-permute-start | bytes 110600 | tf_op jit(solution)/shard_map/ppermute | solution.py:415
  22.3 0.3 collective-permute-start.5
  22.6 1.5 %collective-permute-done.7.refs_3_ = f32[72,128]{1,0:T(8,128)S(1)} collective-permute-done((f32[72,128]{1,0:T(8,128)S(1)}, f32[72,128]{1,0:T(8,128)S(1)}, u32[]{:S(2)}, u32[]{:S(2)}) %collective-permute-start.7) | collective-permute-done | bytes 36896 | tf_op jit(solution)/shard_map/ppermute | solution.py:415
  24.1 1.7 %collective-permute-done.6.refs_2_ = f32[72,128]{1,0:T(8,128)S(1)} collective-permute-done((f32[72,128]{1,0:T(8,128)S(1)}, f32[72,128]{1,0:T(8,128)S(1)}, u32[]{:S(2)}, u32[]{:S(2)}) %collective-permute-start.6) | collective-permute-done | bytes 36896 | tf_op jit(solution)/shard_map/ppermute | solution.py:415
  25.8 0.4 %collective-permute-done.5.refs_1_ = f32[72,128]{1,0:T(8,128)S(1)} collective-permute-done((f32[72,128]{1,0:T(8,128)S(1)}, f32[72,128]{1,0:T(8,128)S(1)}, u32[]{:S(2)}, u32[]{:S(2)}) %collective-permute-start.5) | collective-permute-done | bytes 36896 | tf_op jit(solution)/shard_map/ppermute | solution.py:415
  26.3 2.7 %collective-permute-start.8 = (f32[72,128]{1,0:T(8,128)S(1)}, f32[72,128]{1,0:T(8,128)S(1)}, u32[]{:S(2)}, u32[]{:S(2)}) collective-permute-start(f32[72,128]{1,0:T(8,128)S(1)} %gram_sum.3.gram_ref), channel_id=1, source_target_pairs={{0,8},{1,9},{2,10},{3,11},{4,12},{5,13},{6,14},{7,15},{8,0},{9,1},... | collective-permute-start | bytes 110600 | tf_op jit(solution)/shard_map/ppermute | solution.py:415
  28.9 0.0 copy-done.2
  28.9 1.1 %angles.1 = (f32[4,1024]{1,0:T(4,128)}, f32[4,1024]{1,0:T(4,128)}) custom-call(f32[520,128]{1,0:T(8,128)S(1)} %collective-permute-done.near_ref.refs_0_, f32[776,128]{1,0:T(8,128)S(1)} %collective-permute-done.1.far_ref.refs_0_, f32[4,1024]{1,0:T(4,128)S(1)} %copy-done, f32[4,1024]{1,0:T(4,128)S(1)} %copy-done.2, f32[4,1024]{1,0:T(4,128)S(1)} %copy-done.3, ...), custom_call_target="tpu_custom_call" | custom-call | flops 1000000 | bytes 1000000 | tf_op jit(solution)/shard_map/angles/pallas_call | solution.py:530
  30.0 1.1 %collective-permute-done.8.other_ref = f32[72,128]{1,0:T(8,128)S(1)} collective-permute-done((f32[72,128]{1,0:T(8,128)S(1)}, f32[72,128]{1,0:T(8,128)S(1)}, u32[]{:S(2)}, u32[]{:S(2)}) %collective-permute-start.8) | collective-permute-done | bytes 36896 | tf_op jit(solution)/shard_map/ppermute | solution.py:415
  31.2 0.0 copy-done.4
  31.2 5.8 %ortho.1 = (f32[2,4,1024,128]{3,2,1,0:T(8,128)}, f32[1,128]{1,0:T(1,128)}) custom-call(f32[72,128]{1,0:T(8,128)S(1)} %gram_sum.3.gram_ref, f32[72,128]{1,0:T(8,128)S(1)} %collective-permute-done.8.other_ref, f32[1,128]{1,0:T(1,128)S(1)} %bitcast.2, bf16[2,2,1024,256]{3,2,1,0:T(8,128)(2,1)S(1)} %get-tuple-element.34.inner_ref, ...), custom_call_target="tpu_custom_call" | custom-call | tf_op jit(solution)/shard_map/ortho/pallas_call | solution.py:541
  (2 shorter events, 0.0 us)
Async XLA Ops:
  0.6 8.5 %copy-start = (f32[4,1024]{1,0:T(4,128)S(1)}, f32[4,1024]{1,0:T(4,128)}, u32[]{:S(2)}) copy-start(f32[4,1024]{1,0:T(4,128)} %refs_2_.1) | copy-start | bytes 49156
  0.6 8.5 %copy-start.1 = (f32[4,1024]{1,0:T(4,128)S(1)}, f32[4,1024]{1,0:T(4,128)}, u32[]{:S(2)}) copy-start(f32[4,1024]{1,0:T(4,128)} %refs_3_.3) | copy-start | bytes 49156
  0.7 8.5 %copy-start.3 = (f32[4,1024]{1,0:T(4,128)S(1)}, f32[4,1024]{1,0:T(4,128)}, u32[]{:S(2)}) copy-start(f32[4,1024]{1,0:T(4,128)} %kick_ref.3) | copy-start | bytes 49156
  1.8 14.7 %collective-permute-start.1 = (f32[776,128]{1,0:T(8,128)S(1)}, f32[776,128]{1,0:T(8,128)S(1)}, u32[]{:S(2)}, u32[]{:S(2)}) collective-permute-start(f32[776,128]{1,0:T(8,128)S(1)} %get-tuple-element.24), channel_id=1, source_target_pairs={{0,15},{1,2},{2,1},{3,4},{4,3},{5,6},{6,5},{7,8},{8,7},{9,10},{10,... | collective-permute-start | bytes 1191944 | tf_op jit(solution)/shard_map/ppermute | solution.py:455
  8.3 7.1 %collective-permute-start = (f32[520,128]{1,0:T(8,128)S(1)}, f32[520,128]{1,0:T(8,128)S(1)}, u32[]{:S(2)}, u32[]{:S(2)}) collective-permute-start(f32[520,128]{1,0:T(8,128)S(1)} %get-tuple-element.23), channel_id=1, source_target_pairs={{0,1},{1,0},{2,3},{3,2},{4,5},{5,4},{6,7},{7,6},{8,9},{9,8},{10,11... | collective-permute-start | bytes 798728 | tf_op jit(solution)/shard_map/ppermute | solution.py:457
  8.4 7.0 %collective-permute-start.3 = (f32[512,128]{1,0:T(8,128)S(1)}, f32[512,128]{1,0:T(8,128)S(1)}, u32[]{:S(2)}, u32[]{:S(2)}) collective-permute-start(f32[512,128]{1,0:T(8,128)S(1)} %get-tuple-element.28), channel_id=1, source_target_pairs={{0,1},{1,0},{2,3},{3,2},{4,5},{5,4},{6,7},{7,6},{8,9},{9,8},{10,11... | collective-permute-start | bytes 786440 | tf_op jit(solution)/shard_map/ppermute | solution.py:458
  8.9 8.5 %collective-permute-start.2 = (f32[256,128]{1,0:T(8,128)S(1)}, f32[256,128]{1,0:T(8,128)S(1)}, u32[]{:S(2)}, u32[]{:S(2)}) collective-permute-start(f32[256,128]{1,0:T(8,128)S(1)} %get-tuple-element.22.refs_0_), channel_id=1, source_target_pairs={{0,15},{1,2},{2,1},{3,4},{4,3},{5,6},{6,5},{7,8},{8,7},{9,10},{10,... | collective-permute-start | bytes 393224 | tf_op jit(solution)/shard_map/ppermute | solution.py:459
  15.4 13.6 %copy-start.2 = (f32[4,1024]{1,0:T(4,128)S(1)}, f32[4,1024]{1,0:T(4,128)}, u32[]{:S(2)}) copy-start(f32[4,1024]{1,0:T(4,128)} %momenta_ref.1) | copy-start | bytes 49156
  15.4 15.8 %copy-start.4 = (f32[128]{0:T(128)S(1)}, f32[128]{0:T(128)}, u32[]{:S(2)}) copy-start(f32[128]{0:T(128)} %param.11) | copy-start | bytes 1540
  17.8 1.3 %collective-permute-start.4 = (f32[72,128]{1,0:T(8,128)S(1)}, f32[72,128]{1,0:T(8,128)S(1)}, u32[]{:S(2)}, u32[]{:S(2)}) collective-permute-start(f32[72,128]{1,0:T(8,128)S(1)} %get-tuple-element.33.refs_0_), channel_id=1, source_target_pairs={{0,1},{1,0},{2,3},{3,2},{4,5},{5,4},{6,7},{7,6},{8,9},{9,8},{10,11... | collective-permute-start | bytes 110600 | tf_op jit(solution)/shard_map/ppermute | solution.py:415
  19.1 5.0 %collective-permute-start.7 = (f32[72,128]{1,0:T(8,128)S(1)}, f32[72,128]{1,0:T(8,128)S(1)}, u32[]{:S(2)}, u32[]{:S(2)}) collective-permute-start(f32[72,128]{1,0:T(8,128)S(1)} %gram_sum.2.refs_0_), channel_id=1, source_target_pairs={{0,6},{1,7},{2,4},{3,5},{4,2},{5,3},{6,0},{7,1},{8,14},{9,15},{10,... | collective-permute-start | bytes 110600 | tf_op jit(solution)/shard_map/ppermute | solution.py:415
  21.8 4.0 %collective-permute-start.6 = (f32[72,128]{1,0:T(8,128)S(1)}, f32[72,128]{1,0:T(8,128)S(1)}, u32[]{:S(2)}, u32[]{:S(2)}) collective-permute-start(f32[72,128]{1,0:T(8,128)S(1)} %gram_sum.2.refs_0_), channel_id=1, source_target_pairs={{0,4},{1,5},{2,6},{3,7},{4,0},{5,1},{6,2},{7,3},{8,12},{9,13},{10,... | collective-permute-start | bytes 110600 | tf_op jit(solution)/shard_map/ppermute | solution.py:415
  22.3 4.0 %collective-permute-start.5 = (f32[72,128]{1,0:T(8,128)S(1)}, f32[72,128]{1,0:T(8,128)S(1)}, u32[]{:S(2)}, u32[]{:S(2)}) collective-permute-start(f32[72,128]{1,0:T(8,128)S(1)} %gram_sum.2.refs_0_), channel_id=1, source_target_pairs={{0,2},{1,3},{2,0},{3,1},{4,6},{5,7},{6,4},{7,5},{8,10},{9,11},{10,... | collective-permute-start | bytes 110600 | tf_op jit(solution)/shard_map/ppermute | solution.py:415
  26.3 4.9 %collective-permute-start.8 = (f32[72,128]{1,0:T(8,128)S(1)}, f32[72,128]{1,0:T(8,128)S(1)}, u32[]{:S(2)}, u32[]{:S(2)}) collective-permute-start(f32[72,128]{1,0:T(8,128)S(1)} %gram_sum.3.gram_ref), channel_id=1, source_target_pairs={{0,8},{1,9},{2,10},{3,11},{4,12},{5,13},{6,14},{7,15},{8,0},{9,1},... | collective-permute-start | bytes 110600 | tf_op jit(solution)/shard_map/ppermute | solution.py:415

commit v7 on v6

--- a/solution.py
+++ b/solution.py
@@ -370,7 +370,7 @@
         return both[:, :LANES] + both[:, LANES:]
 
     stores = []
-    piece = columns - head
+    piece = columns // 2
 
     def send(part, slot, row):
         store = pltpu.make_async_copy(
@@ -387,8 +387,8 @@
         for at in range(0, columns, piece):
             out_buf[part, rows - 2, at : at + piece] = product(near_ref[part, at : at + piece])
         send(part, rows - 2, side_slot(0) * (rows - 1))
-        for at in range(0, head, piece):
-            out_buf[part, rows - 1, at : at + piece] = product(far_ref[part, at : at + piece])
+        for at in range(0, head, head // 2):
+            out_buf[part, rows - 1, at : at + head // 2] = product(far_ref[part, at : at + head // 2])
         out_buf[part, rows - 1, head:] = product(tail_ref[part])
         send(part, rows - 1, side_slot(1) * (rows - 1))
     for store in stores:

time: 37.2 us -> 37.2 us (level)
  no operation moved by 1% of the time
where the time goes in v7:
time: 37.2 us; the launch traced here: 37 us
  Pallas kernels  17.7 us (48%)
  starting transfers between devices  12.6 us (34%)
  waiting for transfers between devices  5.92 us (16%)
  between operations  0.76 us (2%)
    ppermute x5, starting transfers between devices, sum_over_rows(): lax.ppermute(terms[0], 'rows', [(i, i ^ offset) for i in range(devices)])  6.27 us
    pallas_call x1, Pallas kernels, local(): pl.pallas_call(inner_kernel, out_shape=[bf16(2, rows - 2, columns, 2 * ve...  6.19 us
    ppermute x5, waiting for transfers between devices, sum_over_rows(): lax.ppermute(terms[0], 'rows', [(i, i ^ offset) for i in range(devices)])  5.91 us
    pallas_call x1, Pallas kernels, local(): pl.pallas_call(functools.partial(ortho_kernel, sites_total), out_shape=[p...  5.79 us
    ppermute x1, starting transfers between devices, local(): far = lax.ppermute(far, 'rows', outward)  5.48 us
    pallas_call x2, Pallas kernels, edge(): pl.pallas_call(functools.partial(edge_kernel, side, len(earlier)), out_sh...  2.15 us
    pallas_call x2, Pallas kernels, finish(): pl.pallas_call(functools.partial(row_gram_kernel, side, len(halos)), out_...  1.94 us
    pallas_call x1, Pallas kernels, local(): pl.pallas_call(functools.partial(angles_kernel, half, head), out_shape=[j...  1.13 us
  transfers between devices with their start and end apart: 9, of which 5 were waited for; matrix products, arithmetic and copies ran while one was open for 0% of the time, Pallas kernels for 28%

profile of v7, /device:TPU:0, one launch (start us, length us, event | category | flops | bytes accessed | tf_op | source)
XLA Modules:
  0.0 37.0 jit_solution(314247762616355663)
XLA Ops:
  0.6 0.0 copy-start
  0.6 0.0 copy-start.1
  0.7 0.0 copy-start.3
  0.7 1.1 %far_edge.1 = (f32[776,128]{1,0:T(8,128)S(1)}, f32[256,128]{1,0:T(8,128)S(1)}) custom-call(f32[2,4,1024,128]{3,2,1,0:T(8,128)} %tangent_ref.5, f32[4,1024]{1,0:T(4,128)} %refs_2_.1), custom_call_target="tpu_custom_call" | custom-call | tf_op jit(solution)/shard_map/far_edge/pallas_call | solution.py:438
  1.8 5.5 %collective-permute-start.1 = (f32[776,128]{1,0:T(8,128)S(1)}, f32[776,128]{1,0:T(8,128)S(1)}, u32[]{:S(2)}, u32[]{:S(2)}) collective-permute-start(f32[776,128]{1,0:T(8,128)S(1)} %get-tuple-element.24), channel_id=1, source_target_pairs={{0,15},{1,2},{2,1},{3,4},{4,3},{5,6},{6,5},{7,8},{8,7},{9,10},{10,... | collective-permute-start | bytes 1191944 | tf_op jit(solution)/shard_map/ppermute | solution.py:455
  7.2 1.1 %near_edge.1 = (f32[520,128]{1,0:T(8,128)S(1)}, f32[512,128]{1,0:T(8,128)S(1)}) custom-call(f32[2,4,1024,128]{3,2,1,0:T(8,128)} %tangent_ref.5, f32[4,1024]{1,0:T(4,128)} %refs_2_.1, f32[256,128]{1,0:T(8,128)S(1)} %get-tuple-element.22.refs_0_), custom_call_target="tpu_custom_call" | custom-call | tf_op jit(solution)/shard_map/near_edge/pallas_call | solution.py:438
  8.3 0.1 collective-permute-start
  8.4 0.5 %collective-permute-start.3 = (f32[512,128]{1,0:T(8,128)S(1)}, f32[512,128]{1,0:T(8,128)S(1)}, u32[]{:S(2)}, u32[]{:S(2)}) collective-permute-start(f32[512,128]{1,0:T(8,128)S(1)} %get-tuple-element.28), channel_id=1, source_target_pairs={{0,1},{1,0},{2,3},{3,2},{4,5},{5,4},{6,7},{7,6},{8,9},{9,8},{10,11... | collective-permute-start | bytes 786440 | tf_op jit(solution)/shard_map/ppermute | solution.py:458
  8.9 0.3 collective-permute-start.2
  9.2 0.0 copy-done
  9.2 0.0 copy-done.1
  9.2 0.0 copy-done.3
  9.2 6.2 %inner.1 = (bf16[2,2,1024,256]{3,2,1,0:T(8,128)(2,1)S(1)}, f32[2,2,1024,128]{3,2,1,0:T(8,128)S(1)}, f32[128,128]{1,0:T(8,128)S(1)}) custom-call(f32[2,4,1024,128]{3,2,1,0:T(8,128)} %tangent_ref.5, f32[4,1024]{1,0:T(4,128)S(1)} %copy-done, f32[4,1024]{1,0:T(4,128)S(1)} %copy-done.3, f32[4,1024]{1,0:T(4,128)S(1)} %copy-done.1), custom_call_target="tpu_custom_call" | custom-call | flops 2000000000 | bytes 8388608 | tf_op jit(solution)/shard_map/inner/pallas_call | solution.py:461
  15.4 0.0 copy-start.2
  15.4 0.0 collective-permute-done.3.refs_1_
  15.4 0.0 collective-permute-done.near_ref.refs_0_
  15.4 0.0 copy-start.4
  15.4 1.0 %near.1 = (bf16[2,1024,256]{2,1,0:T(8,128)(2,1)S(1)}, f32[128,128]{1,0:T(8,128)S(1)}) custom-call(f32[520,128]{1,0:T(8,128)S(1)} %collective-permute-done.near_ref.refs_0_, f32[512,128]{1,0:T(8,128)S(1)} %collective-permute-done.3.refs_1_, f32[2,2,1024,128]{3,2,1,0:T(8,128)S(1)} %get-tuple-element.27.refs_2_.refs_1_.partial_ref, f32[4,1024]{1,0:T(4,128)S(1)} %copy-done, ...), custom_call_target="tpu_custom_call" | custom-call | flops 400000000 | bytes 2097152 | tf_op jit(solution)/shard_map/near/pallas_call | solution.py:484
  16.5 0.0 collective-permute-done.1.far_ref.refs_0_
  16.5 0.9 %far.1 = (bf16[2,768,256]{2,1,0:T(8,128)(2,1)S(1)}, f32[128,128]{1,0:T(8,128)S(1)}, f32[128,128]{1,0:T(8,128)S(1)}) custom-call(f32[776,128]{1,0:T(8,128)S(1)} %collective-permute-done.1.far_ref.refs_0_, f32[2,2,1024,128]{3,2,1,0:T(8,128)S(1)} %get-tuple-element.27.refs_2_.refs_1_.partial_ref, f32[4,1024]{1,0:T(4,128)S(1)} %copy-done, ...), custom_call_target="tpu_custom_call" | custom-call | flops 400000000 | bytes 2097152 | tf_op jit(solution)/shard_map/far/pallas_call | solution.py:484
  17.4 0.0 collective-permute-done.2.halo_ref
  17.4 0.5 %tail.1 = (bf16[2,256,256]{2,1,0:T(8,128)(2,1)S(1)}, f32[72,128]{1,0:T(8,128)S(1)}) custom-call(f32[256,128]{1,0:T(8,128)S(1)} %collective-permute-done.2.halo_ref, f32[2,2,1024,128]{3,2,1,0:T(8,128)S(1)} %get-tuple-element.27.refs_2_.refs_1_.partial_ref, f32[128,128]{1,0:T(8,128)S(1)} %get-tuple-element.31.table_ref, ...), custom_call_target="tpu_custom_call" | custom-call | tf_op jit(solution)/shard_map/tail/pallas_call | solution.py:506
  17.8 0.1 collective-permute-start.4
  18.0 1.2 %collective-permute-done.4.refs_1_ = f32[72,128]{1,0:T(8,128)S(1)} collective-permute-done((f32[72,128]{1,0:T(8,128)S(1)}, f32[72,128]{1,0:T(8,128)S(1)}, u32[]{:S(2)}, u32[]{:S(2)}) %collective-permute-start.4) | collective-permute-done | bytes 36896 | tf_op jit(solution)/shard_map/ppermute | solution.py:415
  19.1 2.7 %collective-permute-start.7 = (f32[72,128]{1,0:T(8,128)S(1)}, f32[72,128]{1,0:T(8,128)S(1)}, u32[]{:S(2)}, u32[]{:S(2)}) collective-permute-start(f32[72,128]{1,0:T(8,128)S(1)} %gram_sum.2.refs_0_), channel_id=1, source_target_pairs={{0,6},{1,7},{2,4},{3,5},{4,2},{5,3},{6,0},{7,1},{8,14},{9,15},{10,... | collective-permute-start | bytes 110600 | tf_op jit(solution)/shard_map/ppermute | solution.py:415
  21.8 0.4 %collective-permute-start.6 = (f32[72,128]{1,0:T(8,128)S(1)}, f32[72,128]{1,0:T(8,128)S(1)}, u32[]{:S(2)}, u32[]{:S(2)}) collective-permute-start(f32[72,128]{1,0:T(8,128)S(1)} %gram_sum.2.refs_0_), channel_id=1, source_target_pairs={{0,4},{1,5},{2,6},{3,7},{4,0},{5,1},{6,2},{7,3},{8,12},{9,13},{10,... | collective-permute-start | bytes 110600 | tf_op jit(solution)/shard_map/ppermute | solution.py:415
  22.3 0.3 collective-permute-start.5
  22.6 1.5 %collective-permute-done.7.refs_3_ = f32[72,128]{1,0:T(8,128)S(1)} collective-permute-done((f32[72,128]{1,0:T(8,128)S(1)}, f32[72,128]{1,0:T(8,128)S(1)}, u32[]{:S(2)}, u32[]{:S(2)}) %collective-permute-start.7) | collective-permute-done | bytes 36896 | tf_op jit(solution)/shard_map/ppermute | solution.py:415
  24.1 1.7 %collective-permute-done.6.refs_2_ = f32[72,128]{1,0:T(8,128)S(1)} collective-permute-done((f32[72,128]{1,0:T(8,128)S(1)}, f32[72,128]{1,0:T(8,128)S(1)}, u32[]{:S(2)}, u32[]{:S(2)}) %collective-permute-start.6) | collective-permute-done | bytes 36896 | tf_op jit(solution)/shard_map/ppermute | solution.py:415
  25.8 0.4 %collective-permute-done.5.refs_1_ = f32[72,128]{1,0:T(8,128)S(1)} collective-permute-done((f32[72,128]{1,0:T(8,128)S(1)}, f32[72,128]{1,0:T(8,128)S(1)}, u32[]{:S(2)}, u32[]{:S(2)}) %collective-permute-start.5) | collective-permute-done | bytes 36896 | tf_op jit(solution)/shard_map/ppermute | solution.py:415
  26.3 2.7 %collective-permute-start.8 = (f32[72,128]{1,0:T(8,128)S(1)}, f32[72,128]{1,0:T(8,128)S(1)}, u32[]{:S(2)}, u32[]{:S(2)}) collective-permute-start(f32[72,128]{1,0:T(8,128)S(1)} %gram_sum.3.gram_ref), channel_id=1, source_target_pairs={{0,8},{1,9},{2,10},{3,11},{4,12},{5,13},{6,14},{7,15},{8,0},{9,1},... | collective-permute-start | bytes 110600 | tf_op jit(solution)/shard_map/ppermute | solution.py:415
  28.9 0.0 copy-done.2
  28.9 1.1 %angles.1 = (f32[4,1024]{1,0:T(4,128)}, f32[4,1024]{1,0:T(4,128)}) custom-call(f32[520,128]{1,0:T(8,128)S(1)} %collective-permute-done.near_ref.refs_0_, f32[776,128]{1,0:T(8,128)S(1)} %collective-permute-done.1.far_ref.refs_0_, f32[4,1024]{1,0:T(4,128)S(1)} %copy-done, f32[4,1024]{1,0:T(4,128)S(1)} %copy-done.2, f32[4,1024]{1,0:T(4,128)S(1)} %copy-done.3, ...), custom_call_target="tpu_custom_call" | custom-call | flops 1000000 | bytes 1000000 | tf_op jit(solution)/shard_map/angles/pallas_call | solution.py:530
  30.0 1.1 %collective-permute-done.8.other_ref = f32[72,128]{1,0:T(8,128)S(1)} collective-permute-done((f32[72,128]{1,0:T(8,128)S(1)}, f32[72,128]{1,0:T(8,128)S(1)}, u32[]{:S(2)}, u32[]{:S(2)}) %collective-permute-start.8) | collective-permute-done | bytes 36896 | tf_op jit(solution)/shard_map/ppermute | solution.py:415
  31.2 0.0 copy-done.4
  31.2 5.8 %ortho.1 = (f32[2,4,1024,128]{3,2,1,0:T(8,128)}, f32[1,128]{1,0:T(1,128)}) custom-call(f32[72,128]{1,0:T(8,128)S(1)} %gram_sum.3.gram_ref, f32[72,128]{1,0:T(8,128)S(1)} %collective-permute-done.8.other_ref, f32[1,128]{1,0:T(1,128)S(1)} %bitcast.2, bf16[2,2,1024,256]{3,2,1,0:T(8,128)(2,1)S(1)} %get-tuple-element.34.inner_ref, ...), custom_call_target="tpu_custom_call" | custom-call | tf_op jit(solution)/shard_map/ortho/pallas_call | solution.py:541
  (2 shorter events, 0.0 us)
Async XLA Ops:
  0.6 8.5 %copy-start = (f32[4,1024]{1,0:T(4,128)S(1)}, f32[4,1024]{1,0:T(4,128)}, u32[]{:S(2)}) copy-start(f32[4,1024]{1,0:T(4,128)} %refs_2_.1) | copy-start | bytes 49156
  0.6 8.5 %copy-start.1 = (f32[4,1024]{1,0:T(4,128)S(1)}, f32[4,1024]{1,0:T(4,128)}, u32[]{:S(2)}) copy-start(f32[4,1024]{1,0:T(4,128)} %refs_3_.3) | copy-start | bytes 49156
  0.7 8.5 %copy-start.3 = (f32[4,1024]{1,0:T(4,128)S(1)}, f32[4,1024]{1,0:T(4,128)}, u32[]{:S(2)}) copy-start(f32[4,1024]{1,0:T(4,128)} %kick_ref.3) | copy-start | bytes 49156
  1.8 14.7 %collective-permute-start.1 = (f32[776,128]{1,0:T(8,128)S(1)}, f32[776,128]{1,0:T(8,128)S(1)}, u32[]{:S(2)}, u32[]{:S(2)}) collective-permute-start(f32[776,128]{1,0:T(8,128)S(1)} %get-tuple-element.24), channel_id=1, source_target_pairs={{0,15},{1,2},{2,1},{3,4},{4,3},{5,6},{6,5},{7,8},{8,7},{9,10},{10,... | collective-permute-start | bytes 1191944 | tf_op jit(solution)/shard_map/ppermute | solution.py:455
  8.3 7.1 %collective-permute-start = (f32[520,128]{1,0:T(8,128)S(1)}, f32[520,128]{1,0:T(8,128)S(1)}, u32[]{:S(2)}, u32[]{:S(2)}) collective-permute-start(f32[520,128]{1,0:T(8,128)S(1)} %get-tuple-element.23), channel_id=1, source_target_pairs={{0,1},{1,0},{2,3},{3,2},{4,5},{5,4},{6,7},{7,6},{8,9},{9,8},{10,11... | collective-permute-start | bytes 798728 | tf_op jit(solution)/shard_map/ppermute | solution.py:457
  8.4 7.0 %collective-permute-start.3 = (f32[512,128]{1,0:T(8,128)S(1)}, f32[512,128]{1,0:T(8,128)S(1)}, u32[]{:S(2)}, u32[]{:S(2)}) collective-permute-start(f32[512,128]{1,0:T(8,128)S(1)} %get-tuple-element.28), channel_id=1, source_target_pairs={{0,1},{1,0},{2,3},{3,2},{4,5},{5,4},{6,7},{7,6},{8,9},{9,8},{10,11... | collective-permute-start | bytes 786440 | tf_op jit(solution)/shard_map/ppermute | solution.py:458
  8.9 8.5 %collective-permute-start.2 = (f32[256,128]{1,0:T(8,128)S(1)}, f32[256,128]{1,0:T(8,128)S(1)}, u32[]{:S(2)}, u32[]{:S(2)}) collective-permute-start(f32[256,128]{1,0:T(8,128)S(1)} %get-tuple-element.22.refs_0_), channel_id=1, source_target_pairs={{0,15},{1,2},{2,1},{3,4},{4,3},{5,6},{6,5},{7,8},{8,7},{9,10},{10,... | collective-permute-start | bytes 393224 | tf_op jit(solution)/shard_map/ppermute | solution.py:459
  15.4 13.6 %copy-start.2 = (f32[4,1024]{1,0:T(4,128)S(1)}, f32[4,1024]{1,0:T(4,128)}, u32[]{:S(2)}) copy-start(f32[4,1024]{1,0:T(4,128)} %momenta_ref.1) | copy-start | bytes 49156
  15.4 15.8 %copy-start.4 = (f32[128]{0:T(128)S(1)}, f32[128]{0:T(128)}, u32[]{:S(2)}) copy-start(f32[128]{0:T(128)} %param.11) | copy-start | bytes 1540
  17.8 1.3 %collective-permute-start.4 = (f32[72,128]{1,0:T(8,128)S(1)}, f32[72,128]{1,0:T(8,128)S(1)}, u32[]{:S(2)}, u32[]{:S(2)}) collective-permute-start(f32[72,128]{1,0:T(8,128)S(1)} %get-tuple-element.33.refs_0_), channel_id=1, source_target_pairs={{0,1},{1,0},{2,3},{3,2},{4,5},{5,4},{6,7},{7,6},{8,9},{9,8},{10,11... | collective-permute-start | bytes 110600 | tf_op jit(solution)/shard_map/ppermute | solution.py:415
  19.1 5.0 %collective-permute-start.7 = (f32[72,128]{1,0:T(8,128)S(1)}, f32[72,128]{1,0:T(8,128)S(1)}, u32[]{:S(2)}, u32[]{:S(2)}) collective-permute-start(f32[72,128]{1,0:T(8,128)S(1)} %gram_sum.2.refs_0_), channel_id=1, source_target_pairs={{0,6},{1,7},{2,4},{3,5},{4,2},{5,3},{6,0},{7,1},{8,14},{9,15},{10,... | collective-permute-start | bytes 110600 | tf_op jit(solution)/shard_map/ppermute | solution.py:415
  21.8 4.0 %collective-permute-start.6 = (f32[72,128]{1,0:T(8,128)S(1)}, f32[72,128]{1,0:T(8,128)S(1)}, u32[]{:S(2)}, u32[]{:S(2)}) collective-permute-start(f32[72,128]{1,0:T(8,128)S(1)} %gram_sum.2.refs_0_), channel_id=1, source_target_pairs={{0,4},{1,5},{2,6},{3,7},{4,0},{5,1},{6,2},{7,3},{8,12},{9,13},{10,... | collective-permute-start | bytes 110600 | tf_op jit(solution)/shard_map/ppermute | solution.py:415
  22.3 4.0 %collective-permute-start.5 = (f32[72,128]{1,0:T(8,128)S(1)}, f32[72,128]{1,0:T(8,128)S(1)}, u32[]{:S(2)}, u32[]{:S(2)}) collective-permute-start(f32[72,128]{1,0:T(8,128)S(1)} %gram_sum.2.refs_0_), channel_id=1, source_target_pairs={{0,2},{1,3},{2,0},{3,1},{4,6},{5,7},{6,4},{7,5},{8,10},{9,11},{10,... | collective-permute-start | bytes 110600 | tf_op jit(solution)/shard_map/ppermute | solution.py:415
  26.3 4.9 %collective-permute-start.8 = (f32[72,128]{1,0:T(8,128)S(1)}, f32[72,128]{1,0:T(8,128)S(1)}, u32[]{:S(2)}, u32[]{:S(2)}) collective-permute-start(f32[72,128]{1,0:T(8,128)S(1)} %gram_sum.3.gram_ref), channel_id=1, source_target_pairs={{0,8},{1,9},{2,10},{3,11},{4,12},{5,13},{6,14},{7,15},{8,0},{9,1},... | collective-permute-start | bytes 110600 | tf_op jit(solution)/shard_map/ppermute | solution.py:415
